TPU v7x, 32 devices: a whole 2x2x4 slice. The times are simulated.
32 devices in a mesh: row: 4 (over z), col: 4 (over y, x), layer: 2 (over core).
Axes of the slice: x: 2, y: 2, z: 4, core: 2. Of those that a mesh axis runs over, the one named last changes fastest.
Arguments:
- left_blocks: bfloat16 [1024, 2, 512], P('row', 'layer', 'col'), may hold values from 3.886223e-05 to 0.00390625
- batch_blocks: bfloat16 [2, 512, 2048], P('layer', 'row', 'col'), may hold values from 0.019897461 to 2
- left_mask: int32 [8, 2, 4], P('row', 'layer', 'col'), may hold values 0 or 1
- batch_mask: int32 [2, 4, 16], P('layer', 'row', 'col'), may hold values 0 or 1
- prune_mask: int32 [8, 16], P('row', ('col', 'layer')), may hold values 0 or 1
Outputs:
- normalized: float32 [1024, 2048], P('row', ('col', 'layer'))
All inputs are finite; a program needn't handle non-finite values. No bound on the sum of `left_mask` or of `batch_mask` or of `prune_mask` on one device may be relied on, other than what follows from the above.
Results may differ from a plain program's by a relative error of at most 0.0003.
Values may be sent and summed in bfloat16 or wider, within the bound.
No kernel may reach another device: no remote copies, remote signals or barrier semaphores. Data moves between devices by JAX's collectives and lax.ppermute only.
A program may use at most 64 MiB of HBM per device.

v0:
```python
import jax
import jax.numpy as jnp
from jax import lax
from jax.sharding import PartitionSpec as P

epsilon = 1e-06


def widen_left(mask, tile_size):
    first, middle, last = mask.shape
    spread = jnp.broadcast_to(
        mask.astype(jnp.bfloat16)[:, None, :, :, None], (first, tile_size, middle, last, tile_size)
    )
    return spread.reshape(first * tile_size, middle, last * tile_size)


def widen_right(mask, tile_size):
    first, middle, last = mask.shape
    spread = jnp.broadcast_to(
        mask.astype(jnp.bfloat16)[:, :, None, :, None], (first, middle, tile_size, last, tile_size)
    )
    return spread.reshape(first, middle * tile_size, last * tile_size)


def widen_pair(mask, tile_size):
    first, last = mask.shape
    spread = jnp.broadcast_to(
        mask.astype(jnp.float32)[:, None, :, None], (first, tile_size, last, tile_size)
    )
    return spread.reshape(first * tile_size, last * tile_size)


def on_device(left_blocks, batch_blocks, left_mask, batch_mask, prune_mask):
    tile_size = left_blocks.shape[0] // left_mask.shape[0]
    left = left_blocks * widen_left(left_mask, tile_size)
    right = batch_blocks * widen_right(batch_mask, tile_size)
    row_count = left.shape[0]
    complete_right = lax.all_gather(right, "row", axis=1, tiled=True)[0]
    product = jnp.dot(
        lax.all_gather(left, "col", axis=2, tiled=True)[:, 0, :],
        complete_right,
        preferred_element_type=jnp.float32,
    )
    own_share = lax.psum_scatter(product, "layer", scatter_dimension=1, tiled=True)
    inflated = own_share * own_share * widen_pair(prune_mask, tile_size)
    col_sums = lax.psum(jnp.sum(inflated, axis=0), "row")
    total_rows = row_count * lax.axis_size("row")
    return inflated * (total_rows / (col_sums + epsilon))


def solution(mesh):
    placed = (
        P("row", "layer", "col"),
        P("layer", "row", "col"),
        P("row", "layer", "col"),
        P("layer", "row", "col"),
        P("row", ("col", "layer")),
    )
    return jax.shard_map(
        on_device, mesh=mesh, in_specs=placed, out_specs=P("row", ("col", "layer")), check_vma=False
    )
```

profile of v0, /device:TPU:0, one launch (start us, length us, event | category | flops | bytes accessed | tf_op | source)
XLA Modules:
  0.0 65.5 jit_solution(14072864131080891495)
XLA Ops:
  6.5 0.0 reduce-scatter.2.cloned.1.call-start
  6.5 0.7 %convert_bitcast_fusion = bf16[4]{0:T(256)(128)(2,1)S(1)} fusion(s32[1,1,4]{2,1,0:T(1,128)} %param.8), kind=kLoop, calls=%fused_computation.9 | loop fusion | flops 4 | bytes 24 | tf_op jit(solution)/shard_map/broadcast_in_dim | solution.py:19
  7.2 0.1 broadcast_bitcast_fusion
  7.3 0.9 %broadcast_multiply_fusion.1 = bf16[1,128,512]{2,1,0:T(8,128)(2,1)S(1)} fusion(bf16[1,128,512]{2,1,0:T(8,128)(2,1)} %param.6, bf16[512]{0:T(512)(128)(2,1)S(1)} %broadcast_bitcast_fusion), kind=kLoop, calls=%fused_computation.6 | loop fusion | flops 65536 | bytes 263168 | tf_op jit(solution)/shard_map/mul | solution.py:36
  8.2 0.0 copy-start.3
  8.2 0.0 copy-start.1
  8.2 17.5 %all_gather.7 = bf16[1,512,512]{2,1,0:T(8,128)(2,1)S(1)} all-gather(bf16[1,128,512]{2,1,0:T(8,128)(2,1)S(1)} %broadcast_multiply_fusion.1), channel_id=1, replica_groups=mesh['row'=4,'col'=4,'layer'=2] {'row'}, dimensions={1}, use_global_device_ids=true | all-gather | bytes 655360 | tf_op jit(solution)/shard_map/all_gather | solution.py:38
  25.7 0.0 copy-done.3
  25.7 0.1 broadcast_bitcast_fusion.1
  25.8 0.0 copy-done.1
  25.8 0.1 broadcast_multiply_fusion.2
  25.9 9.3 %all_gather.6 = bf16[256,1,512]{2,0,1:T(8,128)(2,1)S(1)} all-gather(bf16[256,1,128]{2,0,1:T(8,128)(2,1)S(1)} %broadcast_multiply_fusion.2), channel_id=1, replica_groups=mesh['row'=4,'col'=4,'layer'=2] {'col'}, dimensions={2}, use_global_device_ids=true | all-gather | bytes 327680 | tf_op jit(solution)/shard_map/all_gather | solution.py:40
  35.2 1.1 %fusion = f32[256,512]{1,0:T(8,128)} fusion(bf16[1,512,512]{2,1,0:T(8,128)(2,1)S(1)} %all_gather.7, bf16[256,1,512]{2,0,1:T(8,128)(2,1)S(1)} %all_gather.6), kind=kOutput, calls=%fused_computation | convolution fusion | flops 134217728 | bytes 1310720 | tf_op jit(solution)/shard_map/dot_general | solution.py:39
  36.3 0.0 copy-start.2
  36.3 0.0 reduce-scatter.2.cloned.1.call-update
  36.4 0.7 copy-done.2
  37.0 7.9 %reduce-scatter.2.cloned.1.call-done = f32[256,256]{1,0:T(8,128)} async-done(((f32[256,512]{1,0:T(8,128)}), f32[256,256]{1,0:T(8,128)}) %reduce-scatter.2.cloned.1.call-update) | async-done | bytes 262160 | tf_op jit(solution)/shard_map/reduce_scatter | solution.py:44
  44.9 0.0 copy-start
  44.9 0.1 broadcast_in_dim.39
  45.1 0.8 %copy-done = f32[256,256]{1,0:T(8,128)S(1)} copy-done((f32[256,256]{1,0:T(8,128)S(1)}, f32[256,256]{1,0:T(8,128)}, u32[]{:S(2)}) %copy-start) | copy-done | bytes 262168
  45.9 0.1 fusion.3
  45.9 11.9 %psum.7 = f32[256]{0:T(256)S(1)} all-reduce(f32[256]{0:T(256)S(1)} %fusion.3), channel_id=1, replica_groups=mesh['row'=4,'col'=4,'layer'=2] {'row'}, use_global_device_ids=true, to_apply=%region_2.0 | all-reduce | flops 256 | bytes 2048 | tf_op jit(solution)/shard_map/psum | solution.py:46
  57.9 0.7 %broadcast_multiply_fusion = f32[256,256]{1,0:T(8,128)} fusion(f32[256]{0:T(256)S(1)} %add_divide_fusion, f32[32,8,2,128]{3,2,1,0:T(2,128)S(1)} %bitcast.23, f32[256,256]{1,0:T(8,128)S(1)} %copy-done), kind=kLoop, calls=%fused_computation.4 | loop fusion | flops 196608 | bytes 787456 | tf_op jit(solution)/shard_map/mul | solution.py:48
  (3 shorter events, 0.0 us)
Async XLA Ops:
  6.5 38.4 %reduce-scatter.2.cloned.1.call-start = ((), (), s32[]{:S(2)}) async-start(), calls=%async_computation.1 | async-start | bytes 786432 | tf_op jit(solution)/shard_map/reduce_scatter | solution.py:44
  8.2 17.5 %copy-start.3 = (s32[2,1,1]{0,2,1:T(1,128)S(1)}, s32[2,1,1]{0,2,1:T(1,128)}, u32[]{:S(2)}) copy-start(s32[2,1,1]{0,2,1:T(1,128)} %param.7) | copy-start | bytes 28
  8.2 17.6 %copy-start.1 = (bf16[256,1,128]{2,0,1:T(8,128)(2,1)S(1)}, bf16[256,1,128]{2,0,1:T(8,128)(2,1)}, u32[]{:S(2)}) copy-start(bf16[256,1,128]{2,0,1:T(8,128)(2,1)} %param.5) | copy-start | bytes 196612
  36.3 0.7 %copy-start.2 = (s32[2,2]{1,0:T(2,128)S(1)}, s32[2,2]{1,0:T(2,128)}, u32[]{:S(2)}) copy-start(s32[2,2]{1,0:T(2,128)} %param.9) | copy-start | bytes 52
  44.9 0.9 %copy-start = (f32[256,256]{1,0:T(8,128)S(1)}, f32[256,256]{1,0:T(8,128)}, u32[]{:S(2)}) copy-start(f32[256,256]{1,0:T(8,128)} %reduce-scatter.2.cloned.1.call-done) | copy-start | bytes 786436
Sparse Core Ops, SparseCore 0:
  36.5 8.3 reduce-scatter.1
where the time goes:
time: 65.7 us; the launch traced here: 65.5 us
  blocking collectives  38.8 us (59%)
  between operations  13.4 us (20%)
  waiting for transfers between devices  7.91 us (12%)
  other arithmetic  2.49 us (4%)
  local copies, waits for them, and re-layouts  1.76 us (3%)
  matrix products  1.09 us (2%)
    all_gather x1, blocking collectives, on_device(): complete_right = lax.all_gather(right, 'row', axis=1, tiled=True)[0]  17.5 us
    psum x1, blocking collectives, on_device(): col_sums = lax.psum(jnp.sum(inflated, axis=0), 'row')  11.9 us
    all_gather x1, blocking collectives, on_device(): lax.all_gather(left, 'col', axis=2, tiled=True)[:, 0, :]  9.35 us
    reduce_scatter x1, waiting for transfers between devices, on_device(): lax.psum_scatter(product, 'layer', scatter_dimension=1, tiled=True)  7.9 us
    unnamed x8, local copies, waits for them, and re-layouts  1.48 us
  transfers between devices with their start and end apart: 1, of which 1 were waited for; matrix products, arithmetic and copies ran while one was open for 0% of the time, Pallas kernels for 0%

commit v1 on v0

v1 whole, which is shorter than its diff:
```python
import functools

import jax
import jax.numpy as jnp
from jax import lax
from jax.experimental import pallas as pl
from jax.experimental.pallas import tpu as pltpu
from jax.sharding import PartitionSpec as P

epsilon = 1e-06
SMEM = pl.BlockSpec(memory_space=pltpu.SMEM)
VMEM = pl.BlockSpec(memory_space=pltpu.VMEM)


def mask_kernel(mask, block, out):
    tall, wide = mask.shape
    high, broad = block.shape[0] // tall, block.shape[1] // wide
    for i in range(tall):
        for j in range(wide):
            at = (slice(i * high, (i + 1) * high), slice(j * broad, (j + 1) * broad))
            values = block[at]
            out[at] = jnp.where(mask[i, j] != 0, values, jnp.zeros_like(values))


def masked(mask, block):
    return pl.pallas_call(
        mask_kernel,
        out_shape=jax.ShapeDtypeStruct(block.shape, block.dtype),
        in_specs=[SMEM, VMEM],
        out_specs=VMEM,
        compiler_params=pltpu.CompilerParams(vmem_limit_bytes=4 << 20),
        name="mask_tiles",
    )(mask, block)


def swapped(value, axis, step):
    count = lax.axis_size(axis)
    return lax.ppermute(value, axis, [(i, i ^ step) for i in range(count)])


def product_kernel(place, *refs):
    count = (len(refs) - 3) // 2
    lefts, rights = refs[:count], refs[count : 2 * count]
    keep, give, held = refs[2 * count :]
    for s in range(count):
        held[s] = lefts[s][...]
    half = keep.shape[1]
    mine = pl.multiple_of(place[1] * half, half)
    other = pl.multiple_of((1 - place[1]) * half, half)
    for out, at in ((give, other), (keep, mine)):
        total = jnp.zeros(out.shape, jnp.float32)
        for t in range(count):
            total += jnp.dot(
                held[place[0] ^ t],
                rights[t][:, pl.ds(at, half)],
                preferred_element_type=jnp.float32,
            )
        out[...] = total


def inflate_kernel(mask, keep, got, inflated, sums):
    tall, wide = mask.shape
    high, broad = keep.shape[0] // tall, keep.shape[1] // wide
    for j in range(wide):
        total = jnp.zeros((1, broad), jnp.float32)
        for i in range(tall):
            at = (slice(i * high, (i + 1) * high), slice(j * broad, (j + 1) * broad))
            product = keep[at] + got[at]
            value = jnp.where(mask[i, j] != 0, product * product, 0.0)
            inflated[at] = value
            total += jnp.sum(value, axis=0, keepdims=True)
        sums[:, j * broad : (j + 1) * broad] = total


def on_device(left_blocks, batch_blocks, left_mask, batch_mask, prune_mask):
    f32 = jnp.float32
    rows, columns = left_blocks.shape[0], batch_blocks.shape[2]
    half = columns // 2
    left = masked(left_mask[:, 0, :], left_blocks[:, 0, :])
    right = masked(batch_mask[0], batch_blocks[0])
    count = lax.axis_size("row")
    rights = [right] + [swapped(right, "row", s) for s in range(1, count)]
    lefts = [left] + [swapped(left, "col", s) for s in range(1, count)]
    place = jnp.stack(
        [lax.axis_index("row") ^ lax.axis_index("col"), lax.axis_index("layer")]
    ).astype(jnp.int32)
    piece = jax.ShapeDtypeStruct((rows, half), f32)
    keep, give = pl.pallas_call(
        product_kernel,
        out_shape=[piece, piece],
        in_specs=[SMEM] + [VMEM] * (2 * count),
        out_specs=[VMEM, VMEM],
        scratch_shapes=[pltpu.VMEM((count,) + left.shape, left.dtype)],
        compiler_params=pltpu.CompilerParams(vmem_limit_bytes=4 << 20),
        name="product",
    )(place, *lefts, *rights)
    got = swapped(give, "layer", 1)
    inflated, sums = pl.pallas_call(
        inflate_kernel,
        out_shape=[piece, jax.ShapeDtypeStruct((1, half), f32)],
        in_specs=[SMEM, VMEM, VMEM],
        out_specs=[VMEM, VMEM],
        compiler_params=pltpu.CompilerParams(vmem_limit_bytes=4 << 20),
        name="inflate",
    )(prune_mask, keep, got)
    for s in (1, 2):
        sums = sums + swapped(sums, "row", s)
    total_rows = rows * count
    return inflated * (total_rows / (sums + epsilon))


def widen(mask, tile_size, dtype):
    first, last = mask.shape
    spread = jnp.broadcast_to(
        mask.astype(dtype)[:, None, :, None], (first, tile_size, last, tile_size)
    )
    return spread.reshape(first * tile_size, last * tile_size)


def on_any_device(left_blocks, batch_blocks, left_mask, batch_mask, prune_mask):
    tile_size = left_blocks.shape[0] // left_mask.shape[0]
    left = left_blocks[:, 0, :] * widen(left_mask[:, 0, :], tile_size, jnp.bfloat16)
    right = batch_blocks[0] * widen(batch_mask[0], tile_size, jnp.bfloat16)
    product = jnp.dot(
        lax.all_gather(left, "col", axis=1, tiled=True),
        lax.all_gather(right, "row", axis=0, tiled=True),
        preferred_element_type=jnp.float32,
    )
    own_share = lax.psum_scatter(product, "layer", scatter_dimension=1, tiled=True)
    inflated = own_share * own_share * widen(prune_mask, tile_size, jnp.float32)
    col_sums = lax.psum(jnp.sum(inflated, axis=0), "row")
    total_rows = left.shape[0] * lax.axis_size("row")
    return inflated * (total_rows / (col_sums + epsilon))


def solution(mesh):
    placed = (
        P("row", "layer", "col"),
        P("layer", "row", "col"),
        P("row", "layer", "col"),
        P("layer", "row", "col"),
        P("row", ("col", "layer")),
    )
    small = mesh.shape["row"] == 4 and mesh.shape["col"] == 4 and mesh.shape["layer"] == 2
    return jax.shard_map(
        on_device if small else on_any_device,
        mesh=mesh,
        in_specs=placed,
        out_specs=P("row", ("col", "layer")),
        check_vma=False,
    )
```

time: 65.7 us -> 34.1 us (0.52)
  blocking collectives: 38.8 us -> 0 us
  between operations: 13.4 us -> 0.06 us
  starting transfers between devices: 0.01 us -> 10.5 us
  waiting for transfers between devices: 7.91 us -> 17.6 us
  Pallas kernels: 0 us -> 2.71 us
  other arithmetic: 2.49 us -> 0.81 us
  matrix products: 1.09 us -> 0 us
    all_gather x2 -> x0, blocking collectives: 26.8 us -> none  [the longest x1 17.5 us: on_device(): complete_right = lax.all_gather(right, 'row', axis=1, tiled=True)[0]]
    ppermute x0 -> x9, waiting for transfers between devices: none -> 17.6 us  [swapped(): return lax.ppermute(value, axis, [(i, i ^ step) for i in range(count)])]
    psum x1 -> x0, blocking collectives: 11.9 us -> none  [on_device(): col_sums = lax.psum(jnp.sum(inflated, axis=0), 'row')]
    ppermute x0 -> x9, starting transfers between devices: none -> 10.5 us  [swapped(): return lax.ppermute(value, axis, [(i, i ^ step) for i in range(count)])]
    reduce_scatter x1 -> x0, waiting for transfers between devices: 7.9 us -> none  [on_device(): lax.psum_scatter(product, 'layer', scatter_dimension=1, tiled=True)]
    pallas_call x0 -> x4, Pallas kernels: none -> 2.71 us  [the longest x2 1.13 us: masked(): pl.pallas_call(mask_kernel, out_shape=jax.ShapeDtypeStruct(block.shape, b...]
    dot_general x1 -> x0, matrix products: 1.09 us -> none  [on_device(): jnp.dot(lax.all_gather(left, 'col', axis=2, tiled=True)[:, 0, :], complet...]
    mul x3 -> x1, other arithmetic: 1.76 us -> 0.73 us  [on_device(): return inflated * (total_rows / (sums + epsilon))]
  transfers between devices with their start and end apart: 1 -> 9, of which waited for: 1 -> 6; matrix products, arithmetic and copies ran while one was open for 0% -> 0% of each run, Pallas kernels for 0% -> 2%
where the time goes in v1:
time: 34.1 us; the launch traced here: 33.9 us
  waiting for transfers between devices  17.6 us (52%)
  starting transfers between devices  10.5 us (31%)
  Pallas kernels  2.71 us (8%)
  local copies, waits for them, and re-layouts  2.28 us (7%)
  other arithmetic  0.81 us (2%)
    ppermute x9, waiting for transfers between devices, swapped(): return lax.ppermute(value, axis, [(i, i ^ step) for i in range(count)])  17.6 us
    ppermute x9, starting transfers between devices, swapped(): return lax.ppermute(value, axis, [(i, i ^ step) for i in range(count)])  10.5 us
    unnamed x8, local copies, waits for them, and re-layouts  1.5 us
    pallas_call x2, Pallas kernels, masked(): pl.pallas_call(mask_kernel, out_shape=jax.ShapeDtypeStruct(block.shape, b...  1.13 us
    pallas_call x1, Pallas kernels, on_device(): pl.pallas_call(product_kernel, out_shape=[piece, piece], in_specs=[SMEM]...  0.96 us
    squeeze x1, local copies, waits for them, and re-layouts, on_device(): left = masked(left_mask[:, 0, :], left_blocks[:, 0, :])  0.78 us
    mul x1, other arithmetic, on_device(): return inflated * (total_rows / (sums + epsilon))  0.73 us
  transfers between devices with their start and end apart: 9, of which 6 were waited for; matrix products, arithmetic and copies ran while one was open for 0% of the time, Pallas kernels for 2%

profile of v1, /device:TPU:0, one launch (start us, length us, event | category | flops | bytes accessed | tf_op | source)
XLA Modules:
  0.0 33.9 jit_solution(7294368205406116030)
XLA Ops:
  0.0 0.8 %copy.6.mask = s32[2,1]{1,0:T(2,128)S(1)} copy(s32[2,1]{0,1:T(1,128)} %bitcast.11) | data formatting | bytes 16 | tf_op jit(solution)/shard_map/squeeze | solution.py:79
  0.8 0.8 %copy-done.1 = bf16[256,1,128]{2,0,1:T(8,128)(2,1)S(1)} copy-done((bf16[256,1,128]{2,0,1:T(8,128)(2,1)S(1)}, bf16[256,1,128]{2,0,1:T(8,128)(2,1)}, u32[]{:S(2)}) %copy-start.1) | copy-done | bytes 65560
  1.6 0.6 %mask_tiles.2.refs_0_ = bf16[256,128]{1,0:T(8,128)(2,1)S(1)} custom-call(s32[2,1]{1,0:T(2,128)S(1)} %copy.6.mask, bf16[256,128]{1,0:T(8,128)(2,1)S(1)} %bitcast.8), custom_call_target="tpu_custom_call" | custom-call | tf_op jit(solution)/shard_map/mask_tiles/pallas_call | solution.py:26
  2.2 4.0 %collective-permute-start.2 = (bf16[256,128]{1,0:T(8,128)(2,1)S(1)}, bf16[256,128]{1,0:T(8,128)(2,1)S(1)}, u32[]{:S(2)}, u32[]{:S(2)}) collective-permute-start(bf16[256,128]{1,0:T(8,128)(2,1)S(1)} %mask_tiles.2.refs_0_), channel_id=1, source_target_pairs={{0,6},{2,4},{4,2},{6,0},{1,7},{3,5},{5,3},{7,1},{8,14},{10,12},{12... | collective-permute-start | bytes 196616 | tf_op jit(solution)/shard_map/ppermute | solution.py:38
  6.2 0.7 %copy-done.3 = s32[1,1,4]{2,1,0:T(1,128)S(1)} copy-done((s32[1,1,4]{2,1,0:T(1,128)S(1)}, s32[1,1,4]{2,1,0:T(1,128)}, u32[]{:S(2)}) %copy-start.3) | copy-done | bytes 40
  6.8 0.6 %mask_tiles.3.refs_4_ = bf16[128,512]{1,0:T(8,128)(2,1)S(1)} custom-call(s32[1,4]{1,0:T(1,128)S(1)} %bitcast.9, bf16[128,512]{1,0:T(8,128)(2,1)S(1)} %bitcast.7), custom_call_target="tpu_custom_call" | custom-call | tf_op jit(solution)/shard_map/mask_tiles/pallas_call | solution.py:26
  7.4 3.7 %collective-permute-start.5 = (bf16[128,512]{1,0:T(8,128)(2,1)S(1)}, bf16[128,512]{1,0:T(8,128)(2,1)S(1)}, u32[]{:S(2)}, u32[]{:S(2)}) collective-permute-start(bf16[128,512]{1,0:T(8,128)(2,1)S(1)} %mask_tiles.3.refs_4_), channel_id=1, source_target_pairs={{0,24},{8,16},{16,8},{24,0},{1,25},{9,17},{17,9},{25,1},{2,26},{10... | collective-permute-start | bytes 393224 | tf_op jit(solution)/shard_map/ppermute | solution.py:38
  11.1 0.8 %collective-permute-start.3 = (bf16[128,512]{1,0:T(8,128)(2,1)S(1)}, bf16[128,512]{1,0:T(8,128)(2,1)S(1)}, u32[]{:S(2)}, u32[]{:S(2)}) collective-permute-start(bf16[128,512]{1,0:T(8,128)(2,1)S(1)} %mask_tiles.3.refs_4_), channel_id=1, source_target_pairs={{0,8},{8,0},{16,24},{24,16},{1,9},{9,1},{17,25},{25,17},{2,10},{10... | collective-permute-start | bytes 393224 | tf_op jit(solution)/shard_map/ppermute | solution.py:38
  11.8 0.5 %collective-permute-start.1 = (bf16[256,128]{1,0:T(8,128)(2,1)S(1)}, bf16[256,128]{1,0:T(8,128)(2,1)S(1)}, u32[]{:S(2)}, u32[]{:S(2)}) collective-permute-start(bf16[256,128]{1,0:T(8,128)(2,1)S(1)} %mask_tiles.2.refs_0_), channel_id=1, source_target_pairs={{0,4},{2,6},{4,0},{6,2},{1,5},{3,7},{5,1},{7,3},{8,12},{10,14},{12... | collective-permute-start | bytes 196616 | tf_op jit(solution)/shard_map/ppermute | solution.py:38
  12.3 0.4 %collective-permute-start = (bf16[256,128]{1,0:T(8,128)(2,1)S(1)}, bf16[256,128]{1,0:T(8,128)(2,1)S(1)}, u32[]{:S(2)}, u32[]{:S(2)}) collective-permute-start(bf16[256,128]{1,0:T(8,128)(2,1)S(1)} %mask_tiles.2.refs_0_), channel_id=1, source_target_pairs={{0,2},{2,0},{4,6},{6,4},{1,3},{3,1},{5,7},{7,5},{8,10},{10,8},{12,... | collective-permute-start | bytes 196616 | tf_op jit(solution)/shard_map/ppermute | solution.py:38
  12.7 0.1 pad_add_fusion.place
  12.8 3.3 %collective-permute-done.1.refs_2_ = bf16[256,128]{1,0:T(8,128)(2,1)S(1)} collective-permute-done((bf16[256,128]{1,0:T(8,128)(2,1)S(1)}, bf16[256,128]{1,0:T(8,128)(2,1)S(1)}, u32[]{:S(2)}, u32[]{:S(2)}) %collective-permute-start.1) | collective-permute-done | bytes 65568 | tf_op jit(solution)/shard_map/ppermute | solution.py:38
  16.1 0.5 %collective-permute-done.refs_1_ = bf16[256,128]{1,0:T(8,128)(2,1)S(1)} collective-permute-done((bf16[256,128]{1,0:T(8,128)(2,1)S(1)}, bf16[256,128]{1,0:T(8,128)(2,1)S(1)}, u32[]{:S(2)}, u32[]{:S(2)}) %collective-permute-start) | collective-permute-done | bytes 65568 | tf_op jit(solution)/shard_map/ppermute | solution.py:38
  16.6 5.2 %collective-permute-done.4.refs_6_ = bf16[128,512]{1,0:T(8,128)(2,1)S(1)} collective-permute-done((bf16[128,512]{1,0:T(8,128)(2,1)S(1)}, bf16[128,512]{1,0:T(8,128)(2,1)S(1)}, u32[]{:S(2)}, u32[]{:S(2)}) %collective-permute-start.4) | collective-permute-done | bytes 131104 | tf_op jit(solution)/shard_map/ppermute | solution.py:38
  21.9 1.0 %product.1 = (f32[256,256]{1,0:T(8,128)S(1)}, f32[256,256]{1,0:T(8,128)S(1)}) custom-call(s32[2]{0:T(128)S(1)} %pad_add_fusion.place, bf16[256,128]{1,0:T(8,128)(2,1)S(1)} %mask_tiles.2.refs_0_, bf16[256,128]{1,0:T(8,128)(2,1)S(1)} %collective-permute-done.refs_1_, bf16[256,128]{1,0:T(8,128)(2,1)S(1)} %collective-permute-done.1.refs_2_, ...), custom_call_target="tpu_custom_call" | custom-call | tf_op jit(solution)/shard_map/product/pallas_call | solution.py:88
  22.8 0.0 copy-start.2
  22.8 0.1 collective-permute-start.6
  22.9 1.5 %collective-permute-done.6.got = f32[256,256]{1,0:T(8,128)S(1)} collective-permute-done((f32[256,256]{1,0:T(8,128)S(1)}, f32[256,256]{1,0:T(8,128)S(1)}, u32[]{:S(2)}, u32[]{:S(2)}) %collective-permute-start.6) | collective-permute-done | bytes 262176 | tf_op jit(solution)/shard_map/ppermute | solution.py:38
  24.4 0.6 %inflate.1 = (f32[256,256]{1,0:T(8,128)S(1)}, f32[1,256]{1,0:T(1,128)S(1)}) custom-call(s32[2,2]{1,0:T(2,128)S(1)} %copy-done.2, f32[256,256]{1,0:T(8,128)S(1)} %get-tuple-element.9.keep, f32[256,256]{1,0:T(8,128)S(1)} %collective-permute-done.6.got), custom_call_target="tpu_custom_call" | custom-call | tf_op jit(solution)/shard_map/inflate/pallas_call | solution.py:98
  25.0 0.1 collective-permute-start.7
  25.1 3.6 %collective-permute-done.7 = f32[1,256]{1,0:T(1,128)S(1)} collective-permute-done((f32[1,256]{1,0:T(1,128)S(1)}, f32[1,256]{1,0:T(1,128)S(1)}, u32[]{:S(2)}, u32[]{:S(2)}) %collective-permute-start.7) | collective-permute-done | bytes 1056 | tf_op jit(solution)/shard_map/ppermute | solution.py:38
  28.7 1.0 %collective-permute-start.8 = (f32[1,256]{1,0:T(1,128)S(1)}, f32[1,256]{1,0:T(1,128)S(1)}, u32[]{:S(2)}, u32[]{:S(2)}) collective-permute-start(f32[1,256]{1,0:T(1,128)S(1)} %add.12), channel_id=1, source_target_pairs={{0,16},{8,24},{16,0},{24,8},{1,17},{9,25},{17,1},{25,9},{2,18},{10... | collective-permute-start | bytes 3080 | tf_op jit(solution)/shard_map/ppermute | solution.py:38
  29.7 3.4 %collective-permute-done.8 = f32[1,256]{1,0:T(1,128)S(1)} collective-permute-done((f32[1,256]{1,0:T(1,128)S(1)}, f32[1,256]{1,0:T(1,128)S(1)}, u32[]{:S(2)}, u32[]{:S(2)}) %collective-permute-start.8) | collective-permute-done | bytes 1056 | tf_op jit(solution)/shard_map/ppermute | solution.py:38
  33.2 0.7 %broadcast_multiply_fusion = f32[256,256]{1,0:T(8,128)} fusion(f32[256,256]{1,0:T(8,128)S(1)} %get-tuple-element.11, f32[256]{0:T(256)S(1)} %bitcast.10), kind=kLoop, calls=%fused_computation | loop fusion | flops 65536 | bytes 525312 | tf_op jit(solution)/shard_map/mul | solution.py:109
  (11 shorter events, 0.0 us)
Async XLA Ops:
  0.0 6.2 %copy-start = (bf16[1,128,512]{2,1,0:T(8,128)(2,1)S(1)}, bf16[1,128,512]{2,1,0:T(8,128)(2,1)}, u32[]{:S(2)}) copy-start(bf16[1,128,512]{2,1,0:T(8,128)(2,1)} %param.6) | copy-start | bytes 393220
  0.8 0.8 %copy-start.1 = (bf16[256,1,128]{2,0,1:T(8,128)(2,1)S(1)}, bf16[256,1,128]{2,0,1:T(8,128)(2,1)}, u32[]{:S(2)}) copy-start(bf16[256,1,128]{2,0,1:T(8,128)(2,1)} %param.5) | copy-start | bytes 196612
  2.2 10.2 %collective-permute-start.2 = (bf16[256,128]{1,0:T(8,128)(2,1)S(1)}, bf16[256,128]{1,0:T(8,128)(2,1)S(1)}, u32[]{:S(2)}, u32[]{:S(2)}) collective-permute-start(bf16[256,128]{1,0:T(8,128)(2,1)S(1)} %mask_tiles.2.refs_0_), channel_id=1, source_target_pairs={{0,6},{2,4},{4,2},{6,0},{1,7},{3,5},{5,3},{7,1},{8,14},{10,12},{12... | collective-permute-start | bytes 196616 | tf_op jit(solution)/shard_map/ppermute | solution.py:38
  6.2 0.7 %copy-start.3 = (s32[1,1,4]{2,1,0:T(1,128)S(1)}, s32[1,1,4]{2,1,0:T(1,128)}, u32[]{:S(2)}) copy-start(s32[1,1,4]{2,1,0:T(1,128)} %param.8) | copy-start | bytes 52
  7.4 9.2 %collective-permute-start.5 = (bf16[128,512]{1,0:T(8,128)(2,1)S(1)}, bf16[128,512]{1,0:T(8,128)(2,1)S(1)}, u32[]{:S(2)}, u32[]{:S(2)}) collective-permute-start(bf16[128,512]{1,0:T(8,128)(2,1)S(1)} %mask_tiles.3.refs_4_), channel_id=1, source_target_pairs={{0,24},{8,16},{16,8},{24,0},{1,25},{9,17},{17,9},{25,1},{2,26},{10... | collective-permute-start | bytes 393224 | tf_op jit(solution)/shard_map/ppermute | solution.py:38
  11.1 10.8 %collective-permute-start.4 = (bf16[128,512]{1,0:T(8,128)(2,1)S(1)}, bf16[128,512]{1,0:T(8,128)(2,1)S(1)}, u32[]{:S(2)}, u32[]{:S(2)}) collective-permute-start(bf16[128,512]{1,0:T(8,128)(2,1)S(1)} %mask_tiles.3.refs_4_), channel_id=1, source_target_pairs={{0,16},{8,24},{16,0},{24,8},{1,17},{9,25},{17,1},{25,9},{2,18},{10... | collective-permute-start | bytes 393224 | tf_op jit(solution)/shard_map/ppermute | solution.py:38
  11.1 10.8 %collective-permute-start.3 = (bf16[128,512]{1,0:T(8,128)(2,1)S(1)}, bf16[128,512]{1,0:T(8,128)(2,1)S(1)}, u32[]{:S(2)}, u32[]{:S(2)}) collective-permute-start(bf16[128,512]{1,0:T(8,128)(2,1)S(1)} %mask_tiles.3.refs_4_), channel_id=1, source_target_pairs={{0,8},{8,0},{16,24},{24,16},{1,9},{9,1},{17,25},{25,17},{2,10},{10... | collective-permute-start | bytes 393224 | tf_op jit(solution)/shard_map/ppermute | solution.py:38
  11.8 4.3 %collective-permute-start.1 = (bf16[256,128]{1,0:T(8,128)(2,1)S(1)}, bf16[256,128]{1,0:T(8,128)(2,1)S(1)}, u32[]{:S(2)}, u32[]{:S(2)}) collective-permute-start(bf16[256,128]{1,0:T(8,128)(2,1)S(1)} %mask_tiles.2.refs_0_), channel_id=1, source_target_pairs={{0,4},{2,6},{4,0},{6,2},{1,5},{3,7},{5,1},{7,3},{8,12},{10,14},{12... | collective-permute-start | bytes 196616 | tf_op jit(solution)/shard_map/ppermute | solution.py:38
  12.3 4.3 %collective-permute-start = (bf16[256,128]{1,0:T(8,128)(2,1)S(1)}, bf16[256,128]{1,0:T(8,128)(2,1)S(1)}, u32[]{:S(2)}, u32[]{:S(2)}) collective-permute-start(bf16[256,128]{1,0:T(8,128)(2,1)S(1)} %mask_tiles.2.refs_0_), channel_id=1, source_target_pairs={{0,2},{2,0},{4,6},{6,4},{1,3},{3,1},{5,7},{7,5},{8,10},{10,8},{12,... | collective-permute-start | bytes 196616 | tf_op jit(solution)/shard_map/ppermute | solution.py:38
  22.8 1.6 %copy-start.2 = (s32[2,2]{1,0:T(2,128)S(1)}, s32[2,2]{1,0:T(2,128)}, u32[]{:S(2)}) copy-start(s32[2,2]{1,0:T(2,128)} %mask.1) | copy-start | bytes 52
  22.8 1.6 %collective-permute-start.6 = (f32[256,256]{1,0:T(8,128)S(1)}, f32[256,256]{1,0:T(8,128)S(1)}, u32[]{:S(2)}, u32[]{:S(2)}) collective-permute-start(f32[256,256]{1,0:T(8,128)S(1)} %get-tuple-element.10), channel_id=1, source_target_pairs={{0,1},{1,0},{2,3},{3,2},{4,5},{5,4},{6,7},{7,6},{8,9},{9,8},{10,11... | collective-permute-start | bytes 786440 | tf_op jit(solution)/shard_map/ppermute | solution.py:38
  25.0 3.6 %collective-permute-start.7 = (f32[1,256]{1,0:T(1,128)S(1)}, f32[1,256]{1,0:T(1,128)S(1)}, u32[]{:S(2)}, u32[]{:S(2)}) collective-permute-start(f32[1,256]{1,0:T(1,128)S(1)} %get-tuple-element.12), channel_id=1, source_target_pairs={{0,8},{8,0},{16,24},{24,16},{1,9},{9,1},{17,25},{25,17},{2,10},{10... | collective-permute-start | bytes 3080 | tf_op jit(solution)/shard_map/ppermute | solution.py:38
  28.7 4.5 %collective-permute-start.8 = (f32[1,256]{1,0:T(1,128)S(1)}, f32[1,256]{1,0:T(1,128)S(1)}, u32[]{:S(2)}, u32[]{:S(2)}) collective-permute-start(f32[1,256]{1,0:T(1,128)S(1)} %add.12), channel_id=1, source_target_pairs={{0,16},{8,24},{16,0},{24,8},{1,17},{9,25},{17,1},{25,9},{2,18},{10... | collective-permute-start | bytes 3080 | tf_op jit(solution)/shard_map/ppermute | solution.py:38

commit v2 on v1

v2 whole, which is shorter than its diff:
```python
import functools

import jax
import jax.numpy as jnp
from jax import lax
from jax.experimental import pallas as pl
from jax.experimental.pallas import tpu as pltpu
from jax.sharding import PartitionSpec as P

epsilon = 1e-06
VMEM = pl.BlockSpec(memory_space=pltpu.VMEM)
room = pltpu.CompilerParams(vmem_limit_bytes=4 << 20)


def entry(mask, i, j):
    return mask[i : i + 1, j : j + 1] != 0


def keep_tiles(mask, turned, block, out):
    tall, wide = mask.shape[::-1] if turned else mask.shape
    high, broad = block.shape[0] // tall, block.shape[1] // wide
    for i in range(tall):
        for j in range(wide):
            at = (slice(i * high, (i + 1) * high), slice(j * broad, (j + 1) * broad))
            values = block[at]
            one = entry(mask, j, i) if turned else entry(mask, i, j)
            kept = jnp.broadcast_to(one, values.shape)
            out[at] = jnp.where(kept, values, jnp.zeros_like(values))


def tiles_kernel(*refs):
    operands, (right, left), held, arrived = refs[:4], refs[4:6], refs[6:10], refs[10]
    copies = [
        pltpu.make_async_copy(operands[n], held[n], arrived.at[n]) for n in range(4)
    ]
    for copy in copies:
        copy.start()
    copies[0].wait()
    copies[1].wait()
    keep_tiles(held[0], False, held[1], right)
    copies[2].wait()
    copies[3].wait()
    keep_tiles(held[2], True, held[3], left)


def tiles(*operands):
    held = [pltpu.VMEM(value.shape, value.dtype) for value in operands]
    return pl.pallas_call(
        tiles_kernel,
        out_shape=[
            jax.ShapeDtypeStruct(operands[n].shape, operands[n].dtype) for n in (1, 3)
        ],
        in_specs=[pl.BlockSpec(memory_space=pltpu.HBM)] * 4,
        out_specs=[VMEM, VMEM],
        scratch_shapes=held + [pltpu.SemaphoreType.DMA((4,))],
        compiler_params=room,
        name="tiles",
    )(*(pltpu.with_memory_space_constraint(value, pltpu.HBM) for value in operands))


def call(kernel, name, shapes, *operands, scratch=()):
    return pl.pallas_call(
        kernel,
        out_shape=shapes,
        in_specs=[VMEM] * len(operands),
        out_specs=jax.tree.map(lambda _: VMEM, shapes),
        scratch_shapes=scratch,
        compiler_params=room,
        name=name,
    )(*operands)


def swapped(value, axis, step):
    count = lax.axis_size(axis)
    return lax.ppermute(value, axis, [(i, i ^ step) for i in range(count)])


def product_kernel(*refs):
    count = (len(refs) - 3) // 2
    lefts, rights = refs[:count], refs[count : 2 * count]
    keep, give, held = refs[2 * count :]
    for s in range(count):
        held[s] = lefts[s][...]
    apart = lax.axis_index("row") ^ lax.axis_index("col")
    layer = lax.axis_index("layer")
    half = keep.shape[1]
    mine = pl.multiple_of(layer * half, half)
    other = pl.multiple_of((1 - layer) * half, half)
    for out, at in ((give, other), (keep, mine)):
        total = jnp.zeros(out.shape, jnp.float32)
        for t in range(count):
            total += jnp.dot(
                held[apart ^ t],
                rights[t][:, pl.ds(at, half)],
                preferred_element_type=jnp.float32,
            )
        out[...] = total


def inflate_kernel(mask, mine, got, out, sums):
    tall, wide = mask.shape
    high, broad = mine.shape[0] // tall, mine.shape[1] // wide
    for j in range(wide):
        total = jnp.zeros((1, broad), jnp.float32)
        columns = slice(j * broad, (j + 1) * broad)
        for i in range(tall):
            at = (slice(i * high, (i + 1) * high), columns)
            product = mine[at] + got[at]
            kept = jnp.broadcast_to(entry(mask, i, j), product.shape)
            value = jnp.where(kept, product * product, 0.0)
            out[at] = value
            total += jnp.sum(value, axis=0, keepdims=True)
        sums[:, columns] = total


def on_device(left_blocks, batch_blocks, left_mask, batch_mask, prune_mask):
    f32 = jnp.float32
    rows, columns = left_blocks.shape[0], batch_blocks.shape[2]
    half = columns // 2
    right, left = tiles(
        batch_mask[0],
        batch_blocks[0],
        jnp.transpose(left_mask, (1, 2, 0))[0],
        left_blocks[:, 0, :],
    )
    count = lax.axis_size("row")
    rights = [right] + [swapped(right, "row", s) for s in range(1, count)]
    lefts = [left, swapped(left, "col", 1), swapped(left, "col", 2)]
    lefts.append(swapped(lefts[1], "col", 2))
    piece = jax.ShapeDtypeStruct((rows, half), f32)
    keep, give = call(
        product_kernel,
        "product",
        [piece, piece],
        *lefts,
        *rights,
        scratch=[pltpu.VMEM((count,) + left.shape, left.dtype)],
    )
    got = swapped(give, "layer", 1)
    inflated, sums = call(
        inflate_kernel,
        "inflate",
        [piece, jax.ShapeDtypeStruct((1, half), f32)],
        prune_mask,
        keep,
        got,
    )
    for s in (1, 2):
        sums = sums + swapped(sums, "row", s)
    total_rows = rows * count
    return inflated * (total_rows / (sums + epsilon))


def widen(mask, tile_size, dtype):
    first, last = mask.shape
    spread = jnp.broadcast_to(
        mask.astype(dtype)[:, None, :, None], (first, tile_size, last, tile_size)
    )
    return spread.reshape(first * tile_size, last * tile_size)


def on_any_device(left_blocks, batch_blocks, left_mask, batch_mask, prune_mask):
    tile_size = left_blocks.shape[0] // left_mask.shape[0]
    left = left_blocks[:, 0, :] * widen(left_mask[:, 0, :], tile_size, jnp.bfloat16)
    right = batch_blocks[0] * widen(batch_mask[0], tile_size, jnp.bfloat16)
    product = jnp.dot(
        lax.all_gather(left, "col", axis=1, tiled=True),
        lax.all_gather(right, "row", axis=0, tiled=True),
        preferred_element_type=jnp.float32,
    )
    own_share = lax.psum_scatter(product, "layer", scatter_dimension=1, tiled=True)
    inflated = own_share * own_share * widen(prune_mask, tile_size, jnp.float32)
    col_sums = lax.psum(jnp.sum(inflated, axis=0), "row")
    total_rows = left.shape[0] * lax.axis_size("row")
    return inflated * (total_rows / (col_sums + epsilon))


def solution(mesh):
    placed = (
        P("row", "layer", "col"),
        P("layer", "row", "col"),
        P("row", "layer", "col"),
        P("layer", "row", "col"),
        P("row", ("col", "layer")),
    )
    small = mesh.shape["row"] == 4 and mesh.shape["col"] == 4 and mesh.shape["layer"] == 2
    return jax.shard_map(
        on_device if small else on_any_device,
        mesh=mesh,
        in_specs=placed,
        out_specs=P("row", ("col", "layer")),
        check_vma=False,
    )
```

time: 34.1 us -> 29.7 us (0.87)
  local copies, waits for them, and re-layouts: 2.28 us -> 0.01 us
  waiting for transfers between devices: 17.6 us -> 16.5 us
  Pallas kernels: 2.71 us -> 1.7 us
    unnamed x8 -> x2, local copies, waits for them, and re-layouts: 1.5 us -> 0.01 us
    ppermute x9, waiting for transfers between devices: 17.6 us -> 16.5 us  [swapped(): return lax.ppermute(value, axis, [(i, i ^ step) for i in range(count)])]
    pallas_call x4 -> x3, Pallas kernels: 2.71 us -> 1.7 us  [the longest x1 1.13 us: tiles(): pl.pallas_call(tiles_kernel, out_shape=[jax.ShapeDtypeStruct(operands[n]....]
    squeeze x1 -> x0, local copies, waits for them, and re-layouts: 0.78 us -> none  [on_device(): left = masked(left_mask[:, 0, :], left_blocks[:, 0, :])]
  transfers between devices with their start and end apart: 9 -> 9, of which waited for: 6 -> 6; matrix products, arithmetic and copies ran while one was open for 0% -> 0% of each run, Pallas kernels for 2% -> 0%
where the time goes in v2:
time: 29.7 us; the launch traced here: 29.6 us
  waiting for transfers between devices  16.5 us (56%)
  starting transfers between devices  10.6 us (36%)
  Pallas kernels  1.7 us (6%)
  other arithmetic  0.74 us (2%)
    ppermute x9, waiting for transfers between devices, swapped(): return lax.ppermute(value, axis, [(i, i ^ step) for i in range(count)])  16.5 us
    ppermute x9, starting transfers between devices, swapped(): return lax.ppermute(value, axis, [(i, i ^ step) for i in range(count)])  10.6 us
    pallas_call x1, Pallas kernels, tiles(): pl.pallas_call(tiles_kernel, out_shape=[jax.ShapeDtypeStruct(operands[n]....  1.13 us
    mul x1, other arithmetic, on_device(): return inflated * (total_rows / (sums + epsilon))  0.73 us
  transfers between devices with their start and end apart: 9, of which 6 were waited for; matrix products, arithmetic and copies ran while one was open for 0% of the time, Pallas kernels for 0%

profile of v2, /device:TPU:0, one launch (start us, length us, event | category | flops | bytes accessed | tf_op | source)
XLA Modules:
  0.0 29.6 jit_solution(10673463597816010219)
XLA Ops:
  0.0 1.1 %tiles.1 = (bf16[128,512]{1,0:T(8,128)(2,1)S(1)}, bf16[256,128]{1,0:T(8,128)(2,1)S(1)}) custom-call(s32[1,4]{1,0:T(1,128)} %bitcast.8, bf16[128,512]{1,0:T(8,128)(2,1)} %bitcast.5, s32[1,2]{1,0:T(1,128)} %bitcast.9, bf16[256,128]{1,0:T(8,128)(2,1)} %bitcast.6), custom_call_target="tpu_custom_call" | custom-call | tf_op jit(solution)/shard_map/tiles/pallas_call | solution.py:48
  1.1 3.0 %collective-permute-start = (bf16[256,128]{1,0:T(8,128)(2,1)S(1)}, bf16[256,128]{1,0:T(8,128)(2,1)S(1)}, u32[]{:S(2)}, u32[]{:S(2)}) collective-permute-start(bf16[256,128]{1,0:T(8,128)(2,1)S(1)} %get-tuple-element.11.refs_0_), channel_id=1, source_target_pairs={{0,2},{2,0},{4,6},{6,4},{1,3},{3,1},{5,7},{7,5},{8,10},{10,8},{12,... | collective-permute-start | bytes 196616 | tf_op jit(solution)/shard_map/ppermute | solution.py:75
  4.1 3.6 %collective-permute-start.5 = (bf16[128,512]{1,0:T(8,128)(2,1)S(1)}, bf16[128,512]{1,0:T(8,128)(2,1)S(1)}, u32[]{:S(2)}, u32[]{:S(2)}) collective-permute-start(bf16[128,512]{1,0:T(8,128)(2,1)S(1)} %get-tuple-element.12.refs_4_), channel_id=1, source_target_pairs={{0,24},{8,16},{16,8},{24,0},{1,25},{9,17},{17,9},{25,1},{2,26},{10... | collective-permute-start | bytes 393224 | tf_op jit(solution)/shard_map/ppermute | solution.py:75
  7.7 0.0 collective-permute-start.4
  7.7 0.8 %collective-permute-start.3 = (bf16[128,512]{1,0:T(8,128)(2,1)S(1)}, bf16[128,512]{1,0:T(8,128)(2,1)S(1)}, u32[]{:S(2)}, u32[]{:S(2)}) collective-permute-start(bf16[128,512]{1,0:T(8,128)(2,1)S(1)} %get-tuple-element.12.refs_4_), channel_id=1, source_target_pairs={{0,8},{8,0},{16,24},{24,16},{1,9},{9,1},{17,25},{25,17},{2,10},{10... | collective-permute-start | bytes 393224 | tf_op jit(solution)/shard_map/ppermute | solution.py:75
  8.5 1.5 %collective-permute-start.1 = (bf16[256,128]{1,0:T(8,128)(2,1)S(1)}, bf16[256,128]{1,0:T(8,128)(2,1)S(1)}, u32[]{:S(2)}, u32[]{:S(2)}) collective-permute-start(bf16[256,128]{1,0:T(8,128)(2,1)S(1)} %get-tuple-element.11.refs_0_), channel_id=1, source_target_pairs={{0,4},{2,6},{4,0},{6,2},{1,5},{3,7},{5,1},{7,3},{8,12},{10,14},{12... | collective-permute-start | bytes 196616 | tf_op jit(solution)/shard_map/ppermute | solution.py:75
  10.1 0.0 collective-permute-done.refs_1_
  10.1 0.5 %collective-permute-start.2 = (bf16[256,128]{1,0:T(8,128)(2,1)S(1)}, bf16[256,128]{1,0:T(8,128)(2,1)S(1)}, u32[]{:S(2)}, u32[]{:S(2)}) collective-permute-start(bf16[256,128]{1,0:T(8,128)(2,1)S(1)} %collective-permute-done.refs_1_), channel_id=1, source_target_pairs={{0,4},{2,6},{4,0},{6,2},{1,5},{3,7},{5,1},{7,3},{8,12},{10,14},{12... | collective-permute-start | bytes 196616 | tf_op jit(solution)/shard_map/ppermute | solution.py:75
  10.6 2.2 %collective-permute-done.1.refs_2_ = bf16[256,128]{1,0:T(8,128)(2,1)S(1)} collective-permute-done((bf16[256,128]{1,0:T(8,128)(2,1)S(1)}, bf16[256,128]{1,0:T(8,128)(2,1)S(1)}, u32[]{:S(2)}, u32[]{:S(2)}) %collective-permute-start.1) | collective-permute-done | bytes 65568 | tf_op jit(solution)/shard_map/ppermute | solution.py:75
  12.8 1.5 %collective-permute-done.2.refs_3_ = bf16[256,128]{1,0:T(8,128)(2,1)S(1)} collective-permute-done((bf16[256,128]{1,0:T(8,128)(2,1)S(1)}, bf16[256,128]{1,0:T(8,128)(2,1)S(1)}, u32[]{:S(2)}, u32[]{:S(2)}) %collective-permute-start.2) | collective-permute-done | bytes 65568 | tf_op jit(solution)/shard_map/ppermute | solution.py:75
  14.3 0.0 collective-permute-done.5.refs_7_
  14.3 4.2 %collective-permute-done.4.refs_6_ = bf16[128,512]{1,0:T(8,128)(2,1)S(1)} collective-permute-done((bf16[128,512]{1,0:T(8,128)(2,1)S(1)}, bf16[128,512]{1,0:T(8,128)(2,1)S(1)}, u32[]{:S(2)}, u32[]{:S(2)}) %collective-permute-start.4) | collective-permute-done | bytes 131104 | tf_op jit(solution)/shard_map/ppermute | solution.py:75
  18.5 0.0 collective-permute-done.3.refs_5_
  18.5 0.4 %product.1 = (f32[256,256]{1,0:T(8,128)S(1)}, f32[256,256]{1,0:T(8,128)S(1)}) custom-call(bf16[256,128]{1,0:T(8,128)(2,1)S(1)} %get-tuple-element.11.refs_0_, bf16[256,128]{1,0:T(8,128)(2,1)S(1)} %collective-permute-done.refs_1_, bf16[256,128]{1,0:T(8,128)(2,1)S(1)} %collective-permute-done.1.refs_2_, bf16[256,128]{1,0:T(8,128)(2,1)S(1)} %collective-permute-done.2.refs_3_, ...), custom_call_target="tpu_custom_call" | custom-call | tf_op jit(solution)/shard_map/product/pallas_call | solution.py:62
  19.0 0.0 copy-start
  19.0 0.1 collective-permute-start.6
  19.1 1.5 %collective-permute-done.6.got = f32[256,256]{1,0:T(8,128)S(1)} collective-permute-done((f32[256,256]{1,0:T(8,128)S(1)}, f32[256,256]{1,0:T(8,128)S(1)}, u32[]{:S(2)}, u32[]{:S(2)}) %collective-permute-start.6) | collective-permute-done | bytes 262176 | tf_op jit(solution)/shard_map/ppermute | solution.py:75
  20.6 0.0 copy-done
  20.6 0.1 inflate.1
  20.7 0.1 collective-permute-start.7
  20.8 3.6 %collective-permute-done.7 = f32[1,256]{1,0:T(1,128)S(1)} collective-permute-done((f32[1,256]{1,0:T(1,128)S(1)}, f32[1,256]{1,0:T(1,128)S(1)}, u32[]{:S(2)}, u32[]{:S(2)}) %collective-permute-start.7) | collective-permute-done | bytes 1056 | tf_op jit(solution)/shard_map/ppermute | solution.py:75
  24.4 1.0 %collective-permute-start.8 = (f32[1,256]{1,0:T(1,128)S(1)}, f32[1,256]{1,0:T(1,128)S(1)}, u32[]{:S(2)}, u32[]{:S(2)}) collective-permute-start(f32[1,256]{1,0:T(1,128)S(1)} %add.12), channel_id=1, source_target_pairs={{0,16},{8,24},{16,0},{24,8},{1,17},{9,25},{17,1},{25,9},{2,18},{10... | collective-permute-start | bytes 3080 | tf_op jit(solution)/shard_map/ppermute | solution.py:75
  25.4 3.4 %collective-permute-done.8 = f32[1,256]{1,0:T(1,128)S(1)} collective-permute-done((f32[1,256]{1,0:T(1,128)S(1)}, f32[1,256]{1,0:T(1,128)S(1)}, u32[]{:S(2)}, u32[]{:S(2)}) %collective-permute-start.8) | collective-permute-done | bytes 1056 | tf_op jit(solution)/shard_map/ppermute | solution.py:75
  28.8 0.7 %broadcast_multiply_fusion = f32[256,256]{1,0:T(8,128)} fusion(f32[256,256]{1,0:T(8,128)S(1)} %get-tuple-element.15, f32[256]{0:T(256)S(1)} %bitcast.7), kind=kLoop, calls=%fused_computation | loop fusion | flops 65536 | bytes 525312 | tf_op jit(solution)/shard_map/mul | solution.py:151
  (2 shorter events, 0.0 us)
Async XLA Ops:
  1.1 8.9 %collective-permute-start = (bf16[256,128]{1,0:T(8,128)(2,1)S(1)}, bf16[256,128]{1,0:T(8,128)(2,1)S(1)}, u32[]{:S(2)}, u32[]{:S(2)}) collective-permute-start(bf16[256,128]{1,0:T(8,128)(2,1)S(1)} %get-tuple-element.11.refs_0_), channel_id=1, source_target_pairs={{0,2},{2,0},{4,6},{6,4},{1,3},{3,1},{5,7},{7,5},{8,10},{10,8},{12,... | collective-permute-start | bytes 196616 | tf_op jit(solution)/shard_map/ppermute | solution.py:75
  4.1 10.2 %collective-permute-start.5 = (bf16[128,512]{1,0:T(8,128)(2,1)S(1)}, bf16[128,512]{1,0:T(8,128)(2,1)S(1)}, u32[]{:S(2)}, u32[]{:S(2)}) collective-permute-start(bf16[128,512]{1,0:T(8,128)(2,1)S(1)} %get-tuple-element.12.refs_4_), channel_id=1, source_target_pairs={{0,24},{8,16},{16,8},{24,0},{1,25},{9,17},{17,9},{25,1},{2,26},{10... | collective-permute-start | bytes 393224 | tf_op jit(solution)/shard_map/ppermute | solution.py:75
  7.7 10.8 %collective-permute-start.4 = (bf16[128,512]{1,0:T(8,128)(2,1)S(1)}, bf16[128,512]{1,0:T(8,128)(2,1)S(1)}, u32[]{:S(2)}, u32[]{:S(2)}) collective-permute-start(bf16[128,512]{1,0:T(8,128)(2,1)S(1)} %get-tuple-element.12.refs_4_), channel_id=1, source_target_pairs={{0,16},{8,24},{16,0},{24,8},{1,17},{9,25},{17,1},{25,9},{2,18},{10... | collective-permute-start | bytes 393224 | tf_op jit(solution)/shard_map/ppermute | solution.py:75
  7.7 10.8 %collective-permute-start.3 = (bf16[128,512]{1,0:T(8,128)(2,1)S(1)}, bf16[128,512]{1,0:T(8,128)(2,1)S(1)}, u32[]{:S(2)}, u32[]{:S(2)}) collective-permute-start(bf16[128,512]{1,0:T(8,128)(2,1)S(1)} %get-tuple-element.12.refs_4_), channel_id=1, source_target_pairs={{0,8},{8,0},{16,24},{24,16},{1,9},{9,1},{17,25},{25,17},{2,10},{10... | collective-permute-start | bytes 393224 | tf_op jit(solution)/shard_map/ppermute | solution.py:75
  8.5 4.3 %collective-permute-start.1 = (bf16[256,128]{1,0:T(8,128)(2,1)S(1)}, bf16[256,128]{1,0:T(8,128)(2,1)S(1)}, u32[]{:S(2)}, u32[]{:S(2)}) collective-permute-start(bf16[256,128]{1,0:T(8,128)(2,1)S(1)} %get-tuple-element.11.refs_0_), channel_id=1, source_target_pairs={{0,4},{2,6},{4,0},{6,2},{1,5},{3,7},{5,1},{7,3},{8,12},{10,14},{12... | collective-permute-start | bytes 196616 | tf_op jit(solution)/shard_map/ppermute | solution.py:75
  10.1 4.3 %collective-permute-start.2 = (bf16[256,128]{1,0:T(8,128)(2,1)S(1)}, bf16[256,128]{1,0:T(8,128)(2,1)S(1)}, u32[]{:S(2)}, u32[]{:S(2)}) collective-permute-start(bf16[256,128]{1,0:T(8,128)(2,1)S(1)} %collective-permute-done.refs_1_), channel_id=1, source_target_pairs={{0,4},{2,6},{4,0},{6,2},{1,5},{3,7},{5,1},{7,3},{8,12},{10,14},{12... | collective-permute-start | bytes 196616 | tf_op jit(solution)/shard_map/ppermute | solution.py:75
  19.0 1.6 %copy-start = (s32[2,2]{1,0:T(2,128)S(1)}, s32[2,2]{1,0:T(2,128)}, u32[]{:S(2)}) copy-start(s32[2,2]{1,0:T(2,128)} %mask.1) | copy-start | bytes 52
  19.0 1.6 %collective-permute-start.6 = (f32[256,256]{1,0:T(8,128)S(1)}, f32[256,256]{1,0:T(8,128)S(1)}, u32[]{:S(2)}, u32[]{:S(2)}) collective-permute-start(f32[256,256]{1,0:T(8,128)S(1)} %get-tuple-element.14), channel_id=1, source_target_pairs={{0,1},{1,0},{2,3},{3,2},{4,5},{5,4},{6,7},{7,6},{8,9},{9,8},{10,11... | collective-permute-start | bytes 786440 | tf_op jit(solution)/shard_map/ppermute | solution.py:75
  20.7 3.6 %collective-permute-start.7 = (f32[1,256]{1,0:T(1,128)S(1)}, f32[1,256]{1,0:T(1,128)S(1)}, u32[]{:S(2)}, u32[]{:S(2)}) collective-permute-start(f32[1,256]{1,0:T(1,128)S(1)} %get-tuple-element.16), channel_id=1, source_target_pairs={{0,8},{8,0},{16,24},{24,16},{1,9},{9,1},{17,25},{25,17},{2,10},{10... | collective-permute-start | bytes 3080 | tf_op jit(solution)/shard_map/ppermute | solution.py:75
  24.4 4.5 %collective-permute-start.8 = (f32[1,256]{1,0:T(1,128)S(1)}, f32[1,256]{1,0:T(1,128)S(1)}, u32[]{:S(2)}, u32[]{:S(2)}) collective-permute-start(f32[1,256]{1,0:T(1,128)S(1)} %add.12), channel_id=1, source_target_pairs={{0,16},{8,24},{16,0},{24,8},{1,17},{9,25},{17,1},{25,9},{2,18},{10... | collective-permute-start | bytes 3080 | tf_op jit(solution)/shard_map/ppermute | solution.py:75

commit v3 on v2

--- a/solution.py
+++ b/solution.py
@@ -76,23 +76,25 @@
 
 
 def product_kernel(*refs):
-    count = (len(refs) - 3) // 2
-    lefts, rights = refs[:count], refs[count : 2 * count]
-    keep, give, held = refs[2 * count :]
-    for s in range(count):
+    lefts, rights, (keep, give, held) = refs[:4], refs[4:9], refs[9:]
+    for s in range(4):
         held[s] = lefts[s][...]
-    apart = lax.axis_index("row") ^ lax.axis_index("col")
+    row, col = lax.axis_index("row"), lax.axis_index("col")
     layer = lax.axis_index("layer")
     half = keep.shape[1]
     mine = pl.multiple_of(layer * half, half)
     other = pl.multiple_of((1 - layer) * half, half)
+    first = lax.rem(2 * row + 1, 5)
+    inner = jnp.logical_or(row == 1, row == 2)
+    blocks = (row, first, first ^ 3, row ^ 3)
     for out, at in ((give, other), (keep, mine)):
         total = jnp.zeros(out.shape, jnp.float32)
-        for t in range(count):
+        for t in range(4):
+            block = rights[t][:, pl.ds(at, half)]
+            if t == 3:
+                block = jnp.where(inner, block, rights[4][:, pl.ds(at, half)])
             total += jnp.dot(
-                held[apart ^ t],
-                rights[t][:, pl.ds(at, half)],
-                preferred_element_type=jnp.float32,
+                held[blocks[t] ^ col], block, preferred_element_type=jnp.float32
             )
         out[...] = total
 
@@ -124,7 +126,12 @@
         left_blocks[:, 0, :],
     )
     count = lax.axis_size("row")
-    rights = [right] + [swapped(right, "row", s) for s in range(1, count)]
+    first = lax.ppermute(right, "row", [(0, 2), (3, 1), (1, 0), (2, 3)])
+    second = lax.ppermute(right, "row", [(0, 1), (3, 2), (1, 3), (2, 0)])
+    pairs = [(2, 4), (3, 5), (4, 2), (5, 3), (0, 1), (1, 0), (6, 7), (7, 6)]
+    inner = lax.ppermute(right, ("row", "layer"), pairs)
+    outer = lax.ppermute(first, "row", [(0, 1), (1, 0), (2, 3), (3, 2)])
+    rights = [right, first, second, inner, outer]
     lefts = [left, swapped(left, "col", 1), swapped(left, "col", 2)]
     lefts.append(swapped(lefts[1], "col", 2))
     piece = jax.ShapeDtypeStruct((rows, half), f32)

time: 29.7 us -> 27.8 us (0.936)
  waiting for transfers between devices: 16.5 us -> 12.4 us
  starting transfers between devices: 10.6 us -> 12.7 us
    ppermute x0 -> x4, starting transfers between devices: none -> 7.83 us  [the longest x1 4.09 us: on_device(): first = lax.ppermute(right, 'row', [(0, 2), (3, 1), (1, 0), (2, 3)])]
    ppermute x9 -> x6, starting transfers between devices: 10.6 us -> 4.91 us  [swapped(): return lax.ppermute(value, axis, [(i, i ^ step) for i in range(count)])]
    ppermute x9 -> x6, waiting for transfers between devices: 16.5 us -> 12.1 us  [swapped(): return lax.ppermute(value, axis, [(i, i ^ step) for i in range(count)])]
    ppermute x0 -> x4, waiting for transfers between devices: none -> 0.39 us  [the longest x1 0.38 us: on_device(): outer = lax.ppermute(first, 'row', [(0, 1), (1, 0), (2, 3), (3, 2)])]
  transfers between devices with their start and end apart: 9 -> 10, of which waited for: 6 -> 6; matrix products, arithmetic and copies ran while one was open for 0% -> 0% of each run, Pallas kernels for 0% -> 0%
where the time goes in v3:
time: 27.8 us; the launch traced here: 27.7 us
  starting transfers between devices  12.7 us (46%)
  waiting for transfers between devices  12.4 us (45%)
  Pallas kernels  1.7 us (6%)
  other arithmetic  0.74 us (3%)
    ppermute x6, waiting for transfers between devices, swapped(): return lax.ppermute(value, axis, [(i, i ^ step) for i in range(count)])  12.1 us
    ppermute x6, starting transfers between devices, swapped(): return lax.ppermute(value, axis, [(i, i ^ step) for i in range(count)])  4.91 us
    ppermute x1, starting transfers between devices, on_device(): first = lax.ppermute(right, 'row', [(0, 2), (3, 1), (1, 0), (2, 3)])  4.09 us
    ppermute x1, starting transfers between devices, on_device(): second = lax.ppermute(right, 'row', [(0, 1), (3, 2), (1, 3), (2, 0)])  2.14 us
    ppermute x1, starting transfers between devices, on_device(): outer = lax.ppermute(first, 'row', [(0, 1), (1, 0), (2, 3), (3, 2)])  1.6 us
    pallas_call x1, Pallas kernels, tiles(): pl.pallas_call(tiles_kernel, out_shape=[jax.ShapeDtypeStruct(operands[n]....  1.13 us
    mul x1, other arithmetic, on_device(): return inflated * (total_rows / (sums + epsilon))  0.73 us
    pallas_call x2, Pallas kernels, call(): pl.pallas_call(kernel, out_shape=shapes, in_specs=[VMEM] * len(operands),...  0.57 us
  transfers between devices with their start and end apart: 10, of which 6 were waited for; matrix products, arithmetic and copies ran while one was open for 0% of the time, Pallas kernels for 0%

profile of v3, /device:TPU:0, one launch (start us, length us, event | category | flops | bytes accessed | tf_op | source)
XLA Modules:
  0.0 27.7 jit_solution(13626898174227580776)
XLA Ops:
  0.0 1.1 %tiles.1 = (bf16[128,512]{1,0:T(8,128)(2,1)S(1)}, bf16[256,128]{1,0:T(8,128)(2,1)S(1)}) custom-call(s32[1,4]{1,0:T(1,128)} %bitcast.8, bf16[128,512]{1,0:T(8,128)(2,1)} %bitcast.5, s32[1,2]{1,0:T(1,128)} %bitcast.9, bf16[256,128]{1,0:T(8,128)(2,1)} %bitcast.6), custom_call_target="tpu_custom_call" | custom-call | tf_op jit(solution)/shard_map/tiles/pallas_call | solution.py:48
  1.1 4.1 %collective-permute-start.3 = (bf16[128,512]{1,0:T(8,128)(2,1)S(1)}, bf16[128,512]{1,0:T(8,128)(2,1)S(1)}, u32[]{:S(2)}, u32[]{:S(2)}) collective-permute-start(bf16[128,512]{1,0:T(8,128)(2,1)S(1)} %get-tuple-element.12.refs_4_), channel_id=1, source_target_pairs={{0,16},{24,8},{8,0},{16,24},{1,17},{25,9},{9,1},{17,25},{2,18},{26... | collective-permute-start | bytes 393224 | tf_op jit(solution)/shard_map/ppermute | solution.py:129
  5.2 1.5 %collective-permute-start = (bf16[256,128]{1,0:T(8,128)(2,1)S(1)}, bf16[256,128]{1,0:T(8,128)(2,1)S(1)}, u32[]{:S(2)}, u32[]{:S(2)}) collective-permute-start(bf16[256,128]{1,0:T(8,128)(2,1)S(1)} %get-tuple-element.11.refs_0_), channel_id=1, source_target_pairs={{0,2},{2,0},{4,6},{6,4},{1,3},{3,1},{5,7},{7,5},{8,10},{10,8},{12,... | collective-permute-start | bytes 196616 | tf_op jit(solution)/shard_map/ppermute | solution.py:75
  6.7 0.0 collective-permute-start.5
  6.7 2.1 %collective-permute-start.4 = (bf16[128,512]{1,0:T(8,128)(2,1)S(1)}, bf16[128,512]{1,0:T(8,128)(2,1)S(1)}, u32[]{:S(2)}, u32[]{:S(2)}) collective-permute-start(bf16[128,512]{1,0:T(8,128)(2,1)S(1)} %get-tuple-element.12.refs_4_), channel_id=1, source_target_pairs={{0,8},{24,16},{8,24},{16,0},{1,9},{25,17},{9,25},{17,1},{2,10},{26... | collective-permute-start | bytes 393224 | tf_op jit(solution)/shard_map/ppermute | solution.py:130
  8.9 0.0 collective-permute-done.3.refs_5_
  8.9 1.6 %collective-permute-start.6 = (bf16[128,512]{1,0:T(8,128)(2,1)S(1)}, bf16[128,512]{1,0:T(8,128)(2,1)S(1)}, u32[]{:S(2)}, u32[]{:S(2)}) collective-permute-start(bf16[128,512]{1,0:T(8,128)(2,1)S(1)} %collective-permute-done.3.refs_5_), channel_id=1, source_target_pairs={{0,8},{8,0},{16,24},{24,16},{1,9},{9,1},{17,25},{25,17},{2,10},{10... | collective-permute-start | bytes 393224 | tf_op jit(solution)/shard_map/ppermute | solution.py:133
  10.5 1.5 %collective-permute-start.1 = (bf16[256,128]{1,0:T(8,128)(2,1)S(1)}, bf16[256,128]{1,0:T(8,128)(2,1)S(1)}, u32[]{:S(2)}, u32[]{:S(2)}) collective-permute-start(bf16[256,128]{1,0:T(8,128)(2,1)S(1)} %get-tuple-element.11.refs_0_), channel_id=1, source_target_pairs={{0,4},{2,6},{4,0},{6,2},{1,5},{3,7},{5,1},{7,3},{8,12},{10,14},{12... | collective-permute-start | bytes 196616 | tf_op jit(solution)/shard_map/ppermute | solution.py:75
  12.0 0.0 collective-permute-done.refs_1_
  12.0 0.5 %collective-permute-start.2 = (bf16[256,128]{1,0:T(8,128)(2,1)S(1)}, bf16[256,128]{1,0:T(8,128)(2,1)S(1)}, u32[]{:S(2)}, u32[]{:S(2)}) collective-permute-start(bf16[256,128]{1,0:T(8,128)(2,1)S(1)} %collective-permute-done.refs_1_), channel_id=1, source_target_pairs={{0,4},{2,6},{4,0},{6,2},{1,5},{3,7},{5,1},{7,3},{8,12},{10,14},{12... | collective-permute-start | bytes 196616 | tf_op jit(solution)/shard_map/ppermute | solution.py:75
  12.5 2.2 %collective-permute-done.1.refs_2_ = bf16[256,128]{1,0:T(8,128)(2,1)S(1)} collective-permute-done((bf16[256,128]{1,0:T(8,128)(2,1)S(1)}, bf16[256,128]{1,0:T(8,128)(2,1)S(1)}, u32[]{:S(2)}, u32[]{:S(2)}) %collective-permute-start.1) | collective-permute-done | bytes 65568 | tf_op jit(solution)/shard_map/ppermute | solution.py:75
  14.7 1.5 %collective-permute-done.2.refs_3_ = bf16[256,128]{1,0:T(8,128)(2,1)S(1)} collective-permute-done((bf16[256,128]{1,0:T(8,128)(2,1)S(1)}, bf16[256,128]{1,0:T(8,128)(2,1)S(1)}, u32[]{:S(2)}, u32[]{:S(2)}) %collective-permute-start.2) | collective-permute-done | bytes 65568 | tf_op jit(solution)/shard_map/ppermute | solution.py:75
  16.3 0.0 collective-permute-done.5.refs_7_
  16.3 0.4 %collective-permute-done.6.refs_8_ = bf16[128,512]{1,0:T(8,128)(2,1)S(1)} collective-permute-done((bf16[128,512]{1,0:T(8,128)(2,1)S(1)}, bf16[128,512]{1,0:T(8,128)(2,1)S(1)}, u32[]{:S(2)}, u32[]{:S(2)}) %collective-permute-start.6) | collective-permute-done | bytes 131104 | tf_op jit(solution)/shard_map/ppermute | solution.py:133
  16.6 0.4 %product.1 = (f32[256,256]{1,0:T(8,128)S(1)}, f32[256,256]{1,0:T(8,128)S(1)}) custom-call(bf16[256,128]{1,0:T(8,128)(2,1)S(1)} %get-tuple-element.11.refs_0_, bf16[256,128]{1,0:T(8,128)(2,1)S(1)} %collective-permute-done.refs_1_, bf16[256,128]{1,0:T(8,128)(2,1)S(1)} %collective-permute-done.1.refs_2_, bf16[256,128]{1,0:T(8,128)(2,1)S(1)} %collective-permute-done.2.refs_3_, ...), custom_call_target="tpu_custom_call" | custom-call | tf_op jit(solution)/shard_map/product/pallas_call | solution.py:62
  17.1 0.0 copy-start
  17.1 0.1 collective-permute-start.7
  17.2 1.5 %collective-permute-done.7.got = f32[256,256]{1,0:T(8,128)S(1)} collective-permute-done((f32[256,256]{1,0:T(8,128)S(1)}, f32[256,256]{1,0:T(8,128)S(1)}, u32[]{:S(2)}, u32[]{:S(2)}) %collective-permute-start.7) | collective-permute-done | bytes 262176 | tf_op jit(solution)/shard_map/ppermute | solution.py:75
  18.7 0.1 inflate.1
  18.8 0.1 collective-permute-start.8
  18.9 3.5 %collective-permute-done.8 = f32[1,256]{1,0:T(1,128)S(1)} collective-permute-done((f32[1,256]{1,0:T(1,128)S(1)}, f32[1,256]{1,0:T(1,128)S(1)}, u32[]{:S(2)}, u32[]{:S(2)}) %collective-permute-start.8) | collective-permute-done | bytes 1056 | tf_op jit(solution)/shard_map/ppermute | solution.py:75
  22.5 1.2 %collective-permute-start.9 = (f32[1,256]{1,0:T(1,128)S(1)}, f32[1,256]{1,0:T(1,128)S(1)}, u32[]{:S(2)}, u32[]{:S(2)}) collective-permute-start(f32[1,256]{1,0:T(1,128)S(1)} %add.12), channel_id=1, source_target_pairs={{0,16},{8,24},{16,0},{24,8},{1,17},{9,25},{17,1},{25,9},{2,18},{10... | collective-permute-start | bytes 3080 | tf_op jit(solution)/shard_map/ppermute | solution.py:75
  23.7 3.3 %collective-permute-done.9 = f32[1,256]{1,0:T(1,128)S(1)} collective-permute-done((f32[1,256]{1,0:T(1,128)S(1)}, f32[1,256]{1,0:T(1,128)S(1)}, u32[]{:S(2)}, u32[]{:S(2)}) %collective-permute-start.9) | collective-permute-done | bytes 1056 | tf_op jit(solution)/shard_map/ppermute | solution.py:75
  26.9 0.7 %broadcast_multiply_fusion = f32[256,256]{1,0:T(8,128)} fusion(f32[256,256]{1,0:T(8,128)S(1)} %get-tuple-element.15, f32[256]{0:T(256)S(1)} %bitcast.7), kind=kLoop, calls=%fused_computation | loop fusion | flops 65536 | bytes 525312 | tf_op jit(solution)/shard_map/mul | solution.py:158
  (4 shorter events, 0.0 us)
Async XLA Ops:
  1.1 7.7 %collective-permute-start.3 = (bf16[128,512]{1,0:T(8,128)(2,1)S(1)}, bf16[128,512]{1,0:T(8,128)(2,1)S(1)}, u32[]{:S(2)}, u32[]{:S(2)}) collective-permute-start(bf16[128,512]{1,0:T(8,128)(2,1)S(1)} %get-tuple-element.12.refs_4_), channel_id=1, source_target_pairs={{0,16},{24,8},{8,0},{16,24},{1,17},{25,9},{9,1},{17,25},{2,18},{26... | collective-permute-start | bytes 393224 | tf_op jit(solution)/shard_map/ppermute | solution.py:129
  5.2 6.8 %collective-permute-start = (bf16[256,128]{1,0:T(8,128)(2,1)S(1)}, bf16[256,128]{1,0:T(8,128)(2,1)S(1)}, u32[]{:S(2)}, u32[]{:S(2)}) collective-permute-start(bf16[256,128]{1,0:T(8,128)(2,1)S(1)} %get-tuple-element.11.refs_0_), channel_id=1, source_target_pairs={{0,2},{2,0},{4,6},{6,4},{1,3},{3,1},{5,7},{7,5},{8,10},{10,8},{12,... | collective-permute-start | bytes 196616 | tf_op jit(solution)/shard_map/ppermute | solution.py:75
  6.7 9.5 %collective-permute-start.5 = (bf16[128,512]{1,0:T(8,128)(2,1)S(1)}, bf16[128,512]{1,0:T(8,128)(2,1)S(1)}, u32[]{:S(2)}, u32[]{:S(2)}) collective-permute-start(bf16[128,512]{1,0:T(8,128)(2,1)S(1)} %get-tuple-element.12.refs_4_), channel_id=1, source_target_pairs={{8,16},{9,17},{16,8},{17,9},{0,1},{1,0},{24,25},{25,24},{10,18},{1... | collective-permute-start | bytes 393224 | tf_op jit(solution)/shard_map/ppermute | solution.py:132
  6.7 9.5 %collective-permute-start.4 = (bf16[128,512]{1,0:T(8,128)(2,1)S(1)}, bf16[128,512]{1,0:T(8,128)(2,1)S(1)}, u32[]{:S(2)}, u32[]{:S(2)}) collective-permute-start(bf16[128,512]{1,0:T(8,128)(2,1)S(1)} %get-tuple-element.12.refs_4_), channel_id=1, source_target_pairs={{0,8},{24,16},{8,24},{16,0},{1,9},{25,17},{9,25},{17,1},{2,10},{26... | collective-permute-start | bytes 393224 | tf_op jit(solution)/shard_map/ppermute | solution.py:130
  8.9 7.8 %collective-permute-start.6 = (bf16[128,512]{1,0:T(8,128)(2,1)S(1)}, bf16[128,512]{1,0:T(8,128)(2,1)S(1)}, u32[]{:S(2)}, u32[]{:S(2)}) collective-permute-start(bf16[128,512]{1,0:T(8,128)(2,1)S(1)} %collective-permute-done.3.refs_5_), channel_id=1, source_target_pairs={{0,8},{8,0},{16,24},{24,16},{1,9},{9,1},{17,25},{25,17},{2,10},{10... | collective-permute-start | bytes 393224 | tf_op jit(solution)/shard_map/ppermute | solution.py:133
  10.5 4.3 %collective-permute-start.1 = (bf16[256,128]{1,0:T(8,128)(2,1)S(1)}, bf16[256,128]{1,0:T(8,128)(2,1)S(1)}, u32[]{:S(2)}, u32[]{:S(2)}) collective-permute-start(bf16[256,128]{1,0:T(8,128)(2,1)S(1)} %get-tuple-element.11.refs_0_), channel_id=1, source_target_pairs={{0,4},{2,6},{4,0},{6,2},{1,5},{3,7},{5,1},{7,3},{8,12},{10,14},{12... | collective-permute-start | bytes 196616 | tf_op jit(solution)/shard_map/ppermute | solution.py:75
  12.0 4.3 %collective-permute-start.2 = (bf16[256,128]{1,0:T(8,128)(2,1)S(1)}, bf16[256,128]{1,0:T(8,128)(2,1)S(1)}, u32[]{:S(2)}, u32[]{:S(2)}) collective-permute-start(bf16[256,128]{1,0:T(8,128)(2,1)S(1)} %collective-permute-done.refs_1_), channel_id=1, source_target_pairs={{0,4},{2,6},{4,0},{6,2},{1,5},{3,7},{5,1},{7,3},{8,12},{10,14},{12... | collective-permute-start | bytes 196616 | tf_op jit(solution)/shard_map/ppermute | solution.py:75
  17.1 1.6 %copy-start = (s32[2,2]{1,0:T(2,128)S(1)}, s32[2,2]{1,0:T(2,128)}, u32[]{:S(2)}) copy-start(s32[2,2]{1,0:T(2,128)} %mask.1) | copy-start | bytes 52
  17.1 1.6 %collective-permute-start.7 = (f32[256,256]{1,0:T(8,128)S(1)}, f32[256,256]{1,0:T(8,128)S(1)}, u32[]{:S(2)}, u32[]{:S(2)}) collective-permute-start(f32[256,256]{1,0:T(8,128)S(1)} %get-tuple-element.14), channel_id=1, source_target_pairs={{0,1},{1,0},{2,3},{3,2},{4,5},{5,4},{6,7},{7,6},{8,9},{9,8},{10,11... | collective-permute-start | bytes 786440 | tf_op jit(solution)/shard_map/ppermute | solution.py:75
  18.8 3.6 %collective-permute-start.8 = (f32[1,256]{1,0:T(1,128)S(1)}, f32[1,256]{1,0:T(1,128)S(1)}, u32[]{:S(2)}, u32[]{:S(2)}) collective-permute-start(f32[1,256]{1,0:T(1,128)S(1)} %get-tuple-element.16), channel_id=1, source_target_pairs={{0,8},{8,0},{16,24},{24,16},{1,9},{9,1},{17,25},{25,17},{2,10},{10... | collective-permute-start | bytes 3080 | tf_op jit(solution)/shard_map/ppermute | solution.py:75
  22.5 4.5 %collective-permute-start.9 = (f32[1,256]{1,0:T(1,128)S(1)}, f32[1,256]{1,0:T(1,128)S(1)}, u32[]{:S(2)}, u32[]{:S(2)}) collective-permute-start(f32[1,256]{1,0:T(1,128)S(1)} %add.12), channel_id=1, source_target_pairs={{0,16},{8,24},{16,0},{24,8},{1,17},{9,25},{17,1},{25,9},{2,18},{10... | collective-permute-start | bytes 3080 | tf_op jit(solution)/shard_map/ppermute | solution.py:75

commit v4 on v3

--- a/solution.py
+++ b/solution.py
@@ -75,44 +75,60 @@
     return lax.ppermute(value, axis, [(i, i ^ step) for i in range(count)])
 
 
-def product_kernel(*refs):
-    lefts, rights, (keep, give, held) = refs[:4], refs[4:9], refs[9:]
-    for s in range(4):
-        held[s] = lefts[s][...]
+def pair_kernel(here, beside, out):
+    out[0] = here[...]
+    out[1] = beside[...]
+
+
+def product_kernel(near, far, *refs):
+    rights, (mask, partial, held) = refs[:5], refs[5:]
+    held[0:2] = near[...]
+    held[2:4] = far[...]
     row, col = lax.axis_index("row"), lax.axis_index("col")
-    layer = lax.axis_index("layer")
-    half = keep.shape[1]
-    mine = pl.multiple_of(layer * half, half)
-    other = pl.multiple_of((1 - layer) * half, half)
     first = lax.rem(2 * row + 1, 5)
     inner = jnp.logical_or(row == 1, row == 2)
     blocks = (row, first, first ^ 3, row ^ 3)
-    for out, at in ((give, other), (keep, mine)):
-        total = jnp.zeros(out.shape, jnp.float32)
-        for t in range(4):
-            block = rights[t][:, pl.ds(at, half)]
-            if t == 3:
-                block = jnp.where(inner, block, rights[4][:, pl.ds(at, half)])
-            total += jnp.dot(
-                held[blocks[t] ^ col], block, preferred_element_type=jnp.float32
-            )
-        out[...] = total
-
-
-def inflate_kernel(mask, mine, got, out, sums):
+    rows, columns = held.shape[1], partial.shape[1]
+    total = jnp.zeros((rows, columns), jnp.float32)
+    for t in range(4):
+        block = rights[t][...]
+        if t == 3:
+            block = jnp.where(inner, block, rights[4][...])
+        total += jnp.dot(
+            held[blocks[t] ^ col], block, preferred_element_type=jnp.float32
+        )
+    partial[0:rows, :] = total
     tall, wide = mask.shape
-    high, broad = mine.shape[0] // tall, mine.shape[1] // wide
-    for j in range(wide):
-        total = jnp.zeros((1, broad), jnp.float32)
-        columns = slice(j * broad, (j + 1) * broad)
-        for i in range(tall):
-            at = (slice(i * high, (i + 1) * high), columns)
-            product = mine[at] + got[at]
-            kept = jnp.broadcast_to(entry(mask, i, j), product.shape)
-            value = jnp.where(kept, product * product, 0.0)
-            out[at] = value
-            total += jnp.sum(value, axis=0, keepdims=True)
-        sums[:, columns] = total
+    broad = columns // 2 // wide
+    for i in range(tall):
+        for j in range(2 * wide):
+            kept = entry(mask, i, j % wide).astype(jnp.float32)
+            at = (slice(rows + i, rows + i + 1), slice(j * broad, (j + 1) * broad))
+            partial[at] = jnp.broadcast_to(kept, (1, broad))
+
+
+def inflate_kernel(tall, wide, mine, got, out, sums):
+    rows, half = out.shape
+    high, broad = rows // tall, half // wide
+    layer = lax.axis_index("layer")
+    for side in range(2):
+        for j in range(wide):
+            columns = slice(side * half + j * broad, side * half + (j + 1) * broad)
+            total = jnp.zeros((1, broad), jnp.float32)
+            for i in range(tall):
+                at = (slice(i * high, (i + 1) * high), columns)
+                product = mine[at] + got[at]
+                entries = (slice(rows + i, rows + i + 1), columns)
+                kept = jnp.where(layer == side, mine[entries], got[entries]) != 0.0
+                kept = jnp.broadcast_to(kept, product.shape)
+                value = jnp.where(kept, product * product, 0.0)
+                total += jnp.sum(value, axis=0, keepdims=True)
+
+                @pl.when(layer == side)
+                def _():
+                    out[at[0], j * broad : (j + 1) * broad] = value
+
+            sums[:, columns] = total
 
 
 def on_device(left_blocks, batch_blocks, left_mask, batch_mask, prune_mask):
@@ -132,28 +148,38 @@
     inner = lax.ppermute(right, ("row", "layer"), pairs)
     outer = lax.ppermute(first, "row", [(0, 1), (1, 0), (2, 3), (3, 2)])
     rights = [right, first, second, inner, outer]
-    lefts = [left, swapped(left, "col", 1), swapped(left, "col", 2)]
-    lefts.append(swapped(lefts[1], "col", 2))
+    beside = swapped(left, "col", 1)
+    pair = call(
+        pair_kernel, "pair", jax.ShapeDtypeStruct((2,) + left.shape, left.dtype), left, beside
+    )
+    lefts = [pair, swapped(pair, "col", 2)]
     piece = jax.ShapeDtypeStruct((rows, half), f32)
-    keep, give = call(
+    tall, wide = prune_mask.shape
+    partial = call(
         product_kernel,
         "product",
-        [piece, piece],
+        jax.ShapeDtypeStruct((rows + (tall + 7) // 8 * 8, columns), f32),
         *lefts,
         *rights,
-        scratch=[pltpu.VMEM((count,) + left.shape, left.dtype)],
-    )
-    got = swapped(give, "layer", 1)
+        prune_mask,
+        scratch=[pltpu.VMEM((4,) + left.shape, left.dtype)],
+    )
+    got = swapped(partial, "layer", 1)
     inflated, sums = call(
-        inflate_kernel,
+        functools.partial(inflate_kernel, tall, wide),
         "inflate",
-        [piece, jax.ShapeDtypeStruct((1, half), f32)],
-        prune_mask,
-        keep,
+        [piece, jax.ShapeDtypeStruct((1, columns), f32)],
+        partial,
         got,
     )
-    for s in (1, 2):
-        sums = sums + swapped(sums, "row", s)
+    steps = [(2 * z + 1, 2 * (z ^ 1)) for z in range(4)] + [(2 * z, 2 * z + 1) for z in range(4)]
+    sums = sums + lax.ppermute(sums, ("row", "layer"), steps)
+    steps = [(2 * z, 2 * (z ^ 2) + 1) for z in range(4)] + [(2 * z + 1, 2 * z) for z in range(4)]
+    far = lax.ppermute(sums, ("row", "layer"), steps)
+    total = far + swapped(sums, "layer", 1)
+    total_low = swapped(total, "layer", 1)
+    low = lax.axis_index("layer") == 0
+    sums = jnp.where(low, total_low[:, :half], total[:, half:])
     total_rows = rows * count
     return inflated * (total_rows / (sums + epsilon))
 

time: 27.8 us -> 26.6 us (0.957)
  starting transfers between devices: 12.7 us -> 10.4 us
  waiting for transfers between devices: 12.4 us -> 13.5 us
    ppermute x6 -> x5, waiting for transfers between devices: 12.1 us -> 5.96 us  [swapped(): return lax.ppermute(value, axis, [(i, i ^ step) for i in range(count)])]
    ppermute x0 -> x2, waiting for transfers between devices: none -> 3.68 us  [the longest x1 2.87 us: on_device(): sums = sums + lax.ppermute(sums, ('row', 'layer'), steps)]
    ppermute x1, waiting for transfers between devices: 0.01 us -> 2.29 us  [on_device(): second = lax.ppermute(right, 'row', [(0, 1), (3, 2), (1, 3), (2, 0)])]
    ppermute x1, starting transfers between devices: 2.14 us -> 0.01 us  [on_device(): second = lax.ppermute(right, 'row', [(0, 1), (3, 2), (1, 3), (2, 0)])]
    ppermute x1, waiting for transfers between devices: 0.38 us -> 1.52 us  [on_device(): outer = lax.ppermute(first, 'row', [(0, 1), (1, 0), (2, 3), (3, 2)])]
    ppermute x1, starting transfers between devices: 1.6 us -> 0.72 us  [on_device(): outer = lax.ppermute(first, 'row', [(0, 1), (1, 0), (2, 3), (3, 2)])]
    ppermute x6 -> x5, starting transfers between devices: 4.91 us -> 5.35 us  [swapped(): return lax.ppermute(value, axis, [(i, i ^ step) for i in range(count)])]
    pallas_call x2 -> x3, Pallas kernels: 0.57 us -> 0.68 us  [call(): pl.pallas_call(kernel, out_shape=shapes, in_specs=[VMEM] * len(operands),...]
  transfers between devices with their start and end apart: 10 -> 11, of which waited for: 6 -> 8; matrix products, arithmetic and copies ran while one was open for 0% -> 0% of each run, Pallas kernels for 0% -> 0%
where the time goes in v4:
time: 26.6 us; the launch traced here: 26.4 us
  waiting for transfers between devices  13.5 us (51%)
  starting transfers between devices  10.4 us (39%)
  Pallas kernels  1.81 us (7%)
  other arithmetic  0.74 us (3%)
    ppermute x5, waiting for transfers between devices, swapped(): return lax.ppermute(value, axis, [(i, i ^ step) for i in range(count)])  5.96 us
    ppermute x5, starting transfers between devices, swapped(): return lax.ppermute(value, axis, [(i, i ^ step) for i in range(count)])  5.35 us
    ppermute x1, starting transfers between devices, on_device(): first = lax.ppermute(right, 'row', [(0, 2), (3, 1), (1, 0), (2, 3)])  4.09 us
    ppermute x1, waiting for transfers between devices, on_device(): sums = sums + lax.ppermute(sums, ('row', 'layer'), steps)  2.87 us
    ppermute x1, waiting for transfers between devices, on_device(): second = lax.ppermute(right, 'row', [(0, 1), (3, 2), (1, 3), (2, 0)])  2.29 us
    ppermute x1, waiting for transfers between devices, on_device(): outer = lax.ppermute(first, 'row', [(0, 1), (1, 0), (2, 3), (3, 2)])  1.52 us
    pallas_call x1, Pallas kernels, tiles(): pl.pallas_call(tiles_kernel, out_shape=[jax.ShapeDtypeStruct(operands[n]....  1.13 us
    ppermute x1, waiting for transfers between devices, on_device(): far = lax.ppermute(sums, ('row', 'layer'), steps)  0.8 us
  transfers between devices with their start and end apart: 11, of which 8 were waited for; matrix products, arithmetic and copies ran while one was open for 0% of the time, Pallas kernels for 0%

profile of v4, /device:TPU:0, one launch (start us, length us, event | category | flops | bytes accessed | tf_op | source)
XLA Modules:
  0.0 26.4 jit_solution(3880682108477830896)
XLA Ops:
  0.0 1.1 %tiles.1 = (bf16[128,512]{1,0:T(8,128)(2,1)S(1)}, bf16[256,128]{1,0:T(8,128)(2,1)S(1)}) custom-call(s32[1,4]{1,0:T(1,128)} %bitcast.8, bf16[128,512]{1,0:T(8,128)(2,1)} %bitcast.5, s32[1,2]{1,0:T(1,128)} %bitcast.9, bf16[256,128]{1,0:T(8,128)(2,1)} %bitcast.6), custom_call_target="tpu_custom_call" | custom-call | tf_op jit(solution)/shard_map/tiles/pallas_call | solution.py:48
  1.1 4.1 %collective-permute-start.2 = (bf16[128,512]{1,0:T(8,128)(2,1)S(1)}, bf16[128,512]{1,0:T(8,128)(2,1)S(1)}, u32[]{:S(2)}, u32[]{:S(2)}) collective-permute-start(bf16[128,512]{1,0:T(8,128)(2,1)S(1)} %get-tuple-element.10.refs_0_), channel_id=1, source_target_pairs={{0,16},{24,8},{8,0},{16,24},{1,17},{25,9},{9,1},{17,25},{2,18},{26... | collective-permute-start | bytes 393224 | tf_op jit(solution)/shard_map/ppermute | solution.py:145
  5.2 1.5 %collective-permute-start = (bf16[256,128]{1,0:T(8,128)(2,1)S(1)}, bf16[256,128]{1,0:T(8,128)(2,1)S(1)}, u32[]{:S(2)}, u32[]{:S(2)}) collective-permute-start(bf16[256,128]{1,0:T(8,128)(2,1)S(1)} %get-tuple-element.9.here), channel_id=1, source_target_pairs={{0,2},{2,0},{4,6},{6,4},{1,3},{3,1},{5,7},{7,5},{8,10},{10,8},{12,... | collective-permute-start | bytes 196616 | tf_op jit(solution)/shard_map/ppermute | solution.py:75
  6.7 0.0 collective-permute-start.3
  6.7 0.0 collective-permute-start.4
  6.7 2.8 %collective-permute-done.beside = bf16[256,128]{1,0:T(8,128)(2,1)S(1)} collective-permute-done((bf16[256,128]{1,0:T(8,128)(2,1)S(1)}, bf16[256,128]{1,0:T(8,128)(2,1)S(1)}, u32[]{:S(2)}, u32[]{:S(2)}) %collective-permute-start) | collective-permute-done | bytes 65568 | tf_op jit(solution)/shard_map/ppermute | solution.py:75
  9.5 1.6 %collective-permute-start.1 = (bf16[2,256,128]{2,1,0:T(8,128)(2,1)S(1)}, bf16[2,256,128]{2,1,0:T(8,128)(2,1)S(1)}, u32[]{:S(2)}, u32[]{:S(2)}) collective-permute-start(bf16[2,256,128]{2,1,0:T(8,128)(2,1)S(1)} %pair.1.near), channel_id=1, source_target_pairs={{0,4},{2,6},{4,0},{6,2},{1,5},{3,7},{5,1},{7,3},{8,12},{10,14},{12... | collective-permute-start | bytes 393224 | tf_op jit(solution)/shard_map/ppermute | solution.py:75
  11.1 0.0 collective-permute-done.2.refs_1_
  11.1 0.7 %collective-permute-start.5 = (bf16[128,512]{1,0:T(8,128)(2,1)S(1)}, bf16[128,512]{1,0:T(8,128)(2,1)S(1)}, u32[]{:S(2)}, u32[]{:S(2)}) collective-permute-start(bf16[128,512]{1,0:T(8,128)(2,1)S(1)} %collective-permute-done.2.refs_1_), channel_id=1, source_target_pairs={{0,8},{8,0},{16,24},{24,16},{1,9},{9,1},{17,25},{25,17},{2,10},{10... | collective-permute-start | bytes 393224 | tf_op jit(solution)/shard_map/ppermute | solution.py:149
  11.8 2.3 %collective-permute-done.3.refs_2_ = bf16[128,512]{1,0:T(8,128)(2,1)S(1)} collective-permute-done((bf16[128,512]{1,0:T(8,128)(2,1)S(1)}, bf16[128,512]{1,0:T(8,128)(2,1)S(1)}, u32[]{:S(2)}, u32[]{:S(2)}) %collective-permute-start.3) | collective-permute-done | bytes 131104 | tf_op jit(solution)/shard_map/ppermute | solution.py:146
  14.1 0.4 %collective-permute-done.1.far = bf16[2,256,128]{2,1,0:T(8,128)(2,1)S(1)} collective-permute-done((bf16[2,256,128]{2,1,0:T(8,128)(2,1)S(1)}, bf16[2,256,128]{2,1,0:T(8,128)(2,1)S(1)}, u32[]{:S(2)}, u32[]{:S(2)}) %collective-permute-start.1) | collective-permute-done | bytes 131104 | tf_op jit(solution)/shard_map/ppermute | solution.py:75
  14.5 1.5 %collective-permute-done.5.refs_4_ = bf16[128,512]{1,0:T(8,128)(2,1)S(1)} collective-permute-done((bf16[128,512]{1,0:T(8,128)(2,1)S(1)}, bf16[128,512]{1,0:T(8,128)(2,1)S(1)}, u32[]{:S(2)}, u32[]{:S(2)}) %collective-permute-start.5) | collective-permute-done | bytes 131104 | tf_op jit(solution)/shard_map/ppermute | solution.py:149
  16.1 0.4 %product.1.mine = f32[264,512]{1,0:T(8,128)S(1)} custom-call(bf16[2,256,128]{2,1,0:T(8,128)(2,1)S(1)} %pair.1.near, bf16[2,256,128]{2,1,0:T(8,128)(2,1)S(1)} %collective-permute-done.1.far, bf16[128,512]{1,0:T(8,128)(2,1)S(1)} %get-tuple-element.10.refs_0_, bf16[128,512]{1,0:T(8,128)(2,1)S(1)} %collective-permute-done.2.refs_1_, ...), custom_call_target="tpu_custom_call" | custom-call | tf_op jit(solution)/shard_map/product/pallas_call | solution.py:62
  16.5 0.1 collective-permute-start.6
  16.6 1.9 %collective-permute-done.6.got = f32[264,512]{1,0:T(8,128)S(1)} collective-permute-done((f32[264,512]{1,0:T(8,128)S(1)}, f32[264,512]{1,0:T(8,128)S(1)}, u32[]{:S(2)}, u32[]{:S(2)}) %collective-permute-start.6) | collective-permute-done | bytes 540704 | tf_op jit(solution)/shard_map/ppermute | solution.py:75
  18.5 0.2 inflate.1
  18.7 0.2 collective-permute-start.7
  18.9 2.9 %collective-permute-done.7 = f32[1,512]{1,0:T(1,128)S(1)} collective-permute-done((f32[1,512]{1,0:T(1,128)S(1)}, f32[1,512]{1,0:T(1,128)S(1)}, u32[]{:S(2)}, u32[]{:S(2)}) %collective-permute-start.7) | collective-permute-done | bytes 2080 | tf_op jit(solution)/shard_map/ppermute | solution.py:176
  21.8 0.5 %collective-permute-start.9 = (f32[1,512]{1,0:T(1,128)S(1)}, f32[1,512]{1,0:T(1,128)S(1)}, u32[]{:S(2)}, u32[]{:S(2)}) collective-permute-start(f32[1,512]{1,0:T(1,128)S(1)} %add.12), channel_id=1, source_target_pairs={{0,1},{1,0},{2,3},{3,2},{4,5},{5,4},{6,7},{7,6},{8,9},{9,8},{10,11... | collective-permute-start | bytes 6152 | tf_op jit(solution)/shard_map/ppermute | solution.py:75
  22.3 0.8 %collective-permute-done.8 = f32[1,512]{1,0:T(1,128)S(1)} collective-permute-done((f32[1,512]{1,0:T(1,128)S(1)}, f32[1,512]{1,0:T(1,128)S(1)}, u32[]{:S(2)}, u32[]{:S(2)}) %collective-permute-start.8) | collective-permute-done | bytes 2080 | tf_op jit(solution)/shard_map/ppermute | solution.py:178
  23.1 0.0 collective-permute-done.9
  23.1 1.7 %collective-permute-start.10 = (f32[1,512]{1,0:T(1,128)S(1)}, f32[1,512]{1,0:T(1,128)S(1)}, u32[]{:S(2)}, u32[]{:S(2)}) collective-permute-start(f32[1,512]{1,0:T(1,128)S(1)} %add.13), channel_id=1, source_target_pairs={{0,1},{1,0},{2,3},{3,2},{4,5},{5,4},{6,7},{7,6},{8,9},{9,8},{10,11... | collective-permute-start | bytes 6152 | tf_op jit(solution)/shard_map/ppermute | solution.py:75
  24.8 0.8 %collective-permute-done.10 = f32[1,512]{1,0:T(1,128)S(1)} collective-permute-done((f32[1,512]{1,0:T(1,128)S(1)}, f32[1,512]{1,0:T(1,128)S(1)}, u32[]{:S(2)}, u32[]{:S(2)}) %collective-permute-start.10) | collective-permute-done | bytes 2080 | tf_op jit(solution)/shard_map/ppermute | solution.py:75
  25.7 0.7 %broadcast_multiply_fusion = f32[256,256]{1,0:T(8,128)} fusion(f32[256,256]{1,0:T(8,128)S(1)} %get-tuple-element.11, f32[256]{0:T(256)S(1)} %bitcast.7), kind=kLoop, calls=%fused_computation | loop fusion | flops 65536 | bytes 525312 | tf_op jit(solution)/shard_map/mul | solution.py:184
  (8 shorter events, 0.0 us)
Async XLA Ops:
  1.1 10.0 %collective-permute-start.2 = (bf16[128,512]{1,0:T(8,128)(2,1)S(1)}, bf16[128,512]{1,0:T(8,128)(2,1)S(1)}, u32[]{:S(2)}, u32[]{:S(2)}) collective-permute-start(bf16[128,512]{1,0:T(8,128)(2,1)S(1)} %get-tuple-element.10.refs_0_), channel_id=1, source_target_pairs={{0,16},{24,8},{8,0},{16,24},{1,17},{25,9},{9,1},{17,25},{2,18},{26... | collective-permute-start | bytes 393224 | tf_op jit(solution)/shard_map/ppermute | solution.py:145
  5.2 10.8 %copy-start = (s32[2,2]{1,0:T(2,128)S(1)}, s32[2,2]{1,0:T(2,128)}, u32[]{:S(2)}) copy-start(s32[2,2]{1,0:T(2,128)} %refs_5_.1) | copy-start | bytes 52
  5.2 4.3 %collective-permute-start = (bf16[256,128]{1,0:T(8,128)(2,1)S(1)}, bf16[256,128]{1,0:T(8,128)(2,1)S(1)}, u32[]{:S(2)}, u32[]{:S(2)}) collective-permute-start(bf16[256,128]{1,0:T(8,128)(2,1)S(1)} %get-tuple-element.9.here), channel_id=1, source_target_pairs={{0,2},{2,0},{4,6},{6,4},{1,3},{3,1},{5,7},{7,5},{8,10},{10,8},{12,... | collective-permute-start | bytes 196616 | tf_op jit(solution)/shard_map/ppermute | solution.py:75
  6.7 7.4 %collective-permute-start.3 = (bf16[128,512]{1,0:T(8,128)(2,1)S(1)}, bf16[128,512]{1,0:T(8,128)(2,1)S(1)}, u32[]{:S(2)}, u32[]{:S(2)}) collective-permute-start(bf16[128,512]{1,0:T(8,128)(2,1)S(1)} %get-tuple-element.10.refs_0_), channel_id=1, source_target_pairs={{0,8},{24,16},{8,24},{16,0},{1,9},{25,17},{9,25},{17,1},{2,10},{26... | collective-permute-start | bytes 393224 | tf_op jit(solution)/shard_map/ppermute | solution.py:146
  6.7 7.4 %collective-permute-start.4 = (bf16[128,512]{1,0:T(8,128)(2,1)S(1)}, bf16[128,512]{1,0:T(8,128)(2,1)S(1)}, u32[]{:S(2)}, u32[]{:S(2)}) collective-permute-start(bf16[128,512]{1,0:T(8,128)(2,1)S(1)} %get-tuple-element.10.refs_0_), channel_id=1, source_target_pairs={{8,16},{9,17},{16,8},{17,9},{0,1},{1,0},{24,25},{25,24},{10,18},{1... | collective-permute-start | bytes 393224 | tf_op jit(solution)/shard_map/ppermute | solution.py:148
  9.5 5.0 %collective-permute-start.1 = (bf16[2,256,128]{2,1,0:T(8,128)(2,1)S(1)}, bf16[2,256,128]{2,1,0:T(8,128)(2,1)S(1)}, u32[]{:S(2)}, u32[]{:S(2)}) collective-permute-start(bf16[2,256,128]{2,1,0:T(8,128)(2,1)S(1)} %pair.1.near), channel_id=1, source_target_pairs={{0,4},{2,6},{4,0},{6,2},{1,5},{3,7},{5,1},{7,3},{8,12},{10,14},{12... | collective-permute-start | bytes 393224 | tf_op jit(solution)/shard_map/ppermute | solution.py:75
  11.1 5.0 %collective-permute-start.5 = (bf16[128,512]{1,0:T(8,128)(2,1)S(1)}, bf16[128,512]{1,0:T(8,128)(2,1)S(1)}, u32[]{:S(2)}, u32[]{:S(2)}) collective-permute-start(bf16[128,512]{1,0:T(8,128)(2,1)S(1)} %collective-permute-done.2.refs_1_), channel_id=1, source_target_pairs={{0,8},{8,0},{16,24},{24,16},{1,9},{9,1},{17,25},{25,17},{2,10},{10... | collective-permute-start | bytes 393224 | tf_op jit(solution)/shard_map/ppermute | solution.py:149
  16.5 2.0 %collective-permute-start.6 = (f32[264,512]{1,0:T(8,128)S(1)}, f32[264,512]{1,0:T(8,128)S(1)}, u32[]{:S(2)}, u32[]{:S(2)}) collective-permute-start(f32[264,512]{1,0:T(8,128)S(1)} %product.1.mine), channel_id=1, source_target_pairs={{0,1},{1,0},{2,3},{3,2},{4,5},{5,4},{6,7},{7,6},{8,9},{9,8},{10,11... | collective-permute-start | bytes 1622024 | tf_op jit(solution)/shard_map/ppermute | solution.py:75
  18.7 3.1 %collective-permute-start.7 = (f32[1,512]{1,0:T(1,128)S(1)}, f32[1,512]{1,0:T(1,128)S(1)}, u32[]{:S(2)}, u32[]{:S(2)}) collective-permute-start(f32[1,512]{1,0:T(1,128)S(1)} %get-tuple-element.12), channel_id=1, source_target_pairs={{1,8},{9,0},{17,24},{25,16},{0,1},{8,9},{16,17},{24,25},{3,10},{11... | collective-permute-start | bytes 6152 | tf_op jit(solution)/shard_map/ppermute | solution.py:176
  21.8 1.3 %collective-permute-start.8 = (f32[1,512]{1,0:T(1,128)S(1)}, f32[1,512]{1,0:T(1,128)S(1)}, u32[]{:S(2)}, u32[]{:S(2)}) collective-permute-start(f32[1,512]{1,0:T(1,128)S(1)} %add.12), channel_id=1, source_target_pairs={{0,17},{8,25},{16,1},{24,9},{1,0},{9,8},{17,16},{25,24},{2,19},{10... | collective-permute-start | bytes 6152 | tf_op jit(solution)/shard_map/ppermute | solution.py:178
  21.8 1.3 %collective-permute-start.9 = (f32[1,512]{1,0:T(1,128)S(1)}, f32[1,512]{1,0:T(1,128)S(1)}, u32[]{:S(2)}, u32[]{:S(2)}) collective-permute-start(f32[1,512]{1,0:T(1,128)S(1)} %add.12), channel_id=1, source_target_pairs={{0,1},{1,0},{2,3},{3,2},{4,5},{5,4},{6,7},{7,6},{8,9},{9,8},{10,11... | collective-permute-start | bytes 6152 | tf_op jit(solution)/shard_map/ppermute | solution.py:75
  23.1 2.5 %collective-permute-start.10 = (f32[1,512]{1,0:T(1,128)S(1)}, f32[1,512]{1,0:T(1,128)S(1)}, u32[]{:S(2)}, u32[]{:S(2)}) collective-permute-start(f32[1,512]{1,0:T(1,128)S(1)} %add.13), channel_id=1, source_target_pairs={{0,1},{1,0},{2,3},{3,2},{4,5},{5,4},{6,7},{7,6},{8,9},{9,8},{10,11... | collective-permute-start | bytes 6152 | tf_op jit(solution)/shard_map/ppermute | solution.py:75

commit v5 on v4

--- a/solution.py
+++ b/solution.py
@@ -30,16 +30,22 @@
 
 def tiles_kernel(*refs):
     operands, (right, left), held, arrived = refs[:4], refs[4:6], refs[6:10], refs[10]
-    copies = [
-        pltpu.make_async_copy(operands[n], held[n], arrived.at[n]) for n in range(4)
-    ]
-    for copy in copies:
-        copy.start()
-    copies[0].wait()
-    copies[1].wait()
+    copies = []
+    for n in range(4):
+        parts = 1 if n % 2 == 0 else 4
+        tall = operands[n].shape[0] // parts
+        for part in range(parts):
+            at = pl.ds(part * tall, tall)
+            copy = pltpu.make_async_copy(
+                operands[n].at[at], held[n].at[at], arrived.at[len(copies)]
+            )
+            copy.start()
+            copies.append(copy)
+    for copy in copies[:5]:
+        copy.wait()
     keep_tiles(held[0], False, held[1], right)
-    copies[2].wait()
-    copies[3].wait()
+    for copy in copies[5:]:
+        copy.wait()
     keep_tiles(held[2], True, held[3], left)
 
 
@@ -52,7 +58,7 @@
         ],
         in_specs=[pl.BlockSpec(memory_space=pltpu.HBM)] * 4,
         out_specs=[VMEM, VMEM],
-        scratch_shapes=held + [pltpu.SemaphoreType.DMA((4,))],
+        scratch_shapes=held + [pltpu.SemaphoreType.DMA((10,))],
         compiler_params=room,
         name="tiles",
     )(*(pltpu.with_memory_space_constraint(value, pltpu.HBM) for value in operands))
@@ -80,55 +86,87 @@
     out[1] = beside[...]
 
 
-def product_kernel(near, far, *refs):
-    rights, (mask, partial, held) = refs[:5], refs[5:]
+def early_kernel(near, far, right, first, second, inner, mask, out, left, held):
     held[0:2] = near[...]
     held[2:4] = far[...]
     row, col = lax.axis_index("row"), lax.axis_index("col")
-    first = lax.rem(2 * row + 1, 5)
-    inner = jnp.logical_or(row == 1, row == 2)
-    blocks = (row, first, first ^ 3, row ^ 3)
-    rows, columns = held.shape[1], partial.shape[1]
+    block = lax.rem(2 * row + 1, 5)
+    left[...] = held[row ^ 3 ^ col]
+    rows, columns = left.shape[0], out.shape[1]
     total = jnp.zeros((rows, columns), jnp.float32)
-    for t in range(4):
-        block = rights[t][...]
-        if t == 3:
-            block = jnp.where(inner, block, rights[4][...])
+    for here, values in ((row, right), (block, first), (block ^ 3, second)):
         total += jnp.dot(
-            held[blocks[t] ^ col], block, preferred_element_type=jnp.float32
+            held[here ^ col], values[...], preferred_element_type=jnp.float32
         )
-    partial[0:rows, :] = total
+    out[0:rows, :] = total
+
+    @pl.when(jnp.logical_or(row == 1, row == 2))
+    def _():
+        out[0:rows, :] += jnp.dot(
+            left[...], inner[...], preferred_element_type=jnp.float32
+        )
+
     tall, wide = mask.shape
     broad = columns // 2 // wide
     for i in range(tall):
         for j in range(2 * wide):
             kept = entry(mask, i, j % wide).astype(jnp.float32)
             at = (slice(rows + i, rows + i + 1), slice(j * broad, (j + 1) * broad))
-            partial[at] = jnp.broadcast_to(kept, (1, broad))
-
-
-def inflate_kernel(tall, wide, mine, got, out, sums):
-    rows, half = out.shape
-    high, broad = rows // tall, half // wide
-    layer = lax.axis_index("layer")
-    for side in range(2):
-        for j in range(wide):
-            columns = slice(side * half + j * broad, side * half + (j + 1) * broad)
-            total = jnp.zeros((1, broad), jnp.float32)
-            for i in range(tall):
-                at = (slice(i * high, (i + 1) * high), columns)
-                product = mine[at] + got[at]
-                entries = (slice(rows + i, rows + i + 1), columns)
-                kept = jnp.where(layer == side, mine[entries], got[entries]) != 0.0
-                kept = jnp.broadcast_to(kept, product.shape)
-                value = jnp.where(kept, product * product, 0.0)
+            out[at] = jnp.broadcast_to(kept, (1, broad))
+
+
+def product_kernel(early, left, outer, out):
+    row = lax.axis_index("row")
+    rows = left.shape[0]
+    out[...] = early[...]
+
+    @pl.when(jnp.logical_or(row == 0, row == 3))
+    def _():
+        out[0:rows, :] += jnp.dot(
+            left[...], outer[...], preferred_element_type=jnp.float32
+        )
+
+
+def inflate(own, side, rows, tall, wide, mine, got, out, sums):
+    half = mine.shape[1] // 2
+    broad = half // wide
+    for j in range(wide):
+        columns = slice(side * half + j * broad, side * half + (j + 1) * broad)
+        total = jnp.zeros((1, broad), jnp.float32)
+        for i in range(tall):
+            high = rows // tall
+            at = (slice(i * high, (i + 1) * high), columns)
+            product = mine[at] + got[at]
+            kept = (mine if own else got)[rows + i : rows + i + 1, columns] != 0.0
+            value = jnp.where(jnp.broadcast_to(kept, product.shape), product * product, 0.0)
+            if out is not None:
+                out[at[0], j * broad : (j + 1) * broad] = value
+            if sums is not None:
                 total += jnp.sum(value, axis=0, keepdims=True)
-
-                @pl.when(layer == side)
-                def _():
-                    out[at[0], j * broad : (j + 1) * broad] = value
-
+        if sums is not None:
             sums[:, columns] = total
+
+
+def sums_kernel(rows, tall, wide, mine, got, sums):
+    sums[...] = jnp.zeros_like(sums)
+
+    @pl.when(lax.axis_index("layer") == 1)
+    def _():
+        inflate(False, 0, rows, tall, wide, mine, got, None, sums)
+        inflate(True, 1, rows, tall, wide, mine, got, None, sums)
+
+
+def inflate_kernel(rows, tall, wide, mine, got, out, sums):
+    sums[...] = jnp.zeros_like(sums)
+
+    @pl.when(lax.axis_index("layer") == 0)
+    def _():
+        inflate(True, 0, rows, tall, wide, mine, got, out, sums)
+        inflate(False, 1, rows, tall, wide, mine, got, None, sums)
+
+    @pl.when(lax.axis_index("layer") == 1)
+    def _():
+        inflate(True, 1, rows, tall, wide, mine, got, out, None)
 
 
 def on_device(left_blocks, batch_blocks, left_mask, batch_mask, prune_mask):
@@ -147,39 +185,47 @@
     pairs = [(2, 4), (3, 5), (4, 2), (5, 3), (0, 1), (1, 0), (6, 7), (7, 6)]
     inner = lax.ppermute(right, ("row", "layer"), pairs)
     outer = lax.ppermute(first, "row", [(0, 1), (1, 0), (2, 3), (3, 2)])
-    rights = [right, first, second, inner, outer]
     beside = swapped(left, "col", 1)
     pair = call(
         pair_kernel, "pair", jax.ShapeDtypeStruct((2,) + left.shape, left.dtype), left, beside
     )
-    lefts = [pair, swapped(pair, "col", 2)]
     piece = jax.ShapeDtypeStruct((rows, half), f32)
     tall, wide = prune_mask.shape
-    partial = call(
-        product_kernel,
-        "product",
-        jax.ShapeDtypeStruct((rows + (tall + 7) // 8 * 8, columns), f32),
-        *lefts,
-        *rights,
+    whole = jax.ShapeDtypeStruct((rows + (tall + 7) // 8 * 8, columns), f32)
+    early, last = call(
+        early_kernel,
+        "early",
+        [whole, jax.ShapeDtypeStruct(left.shape, left.dtype)],
+        pair,
+        swapped(pair, "col", 2),
+        right,
+        first,
+        second,
+        inner,
         prune_mask,
         scratch=[pltpu.VMEM((4,) + left.shape, left.dtype)],
     )
+    partial = call(product_kernel, "product", whole, early, last, outer)
     got = swapped(partial, "layer", 1)
-    inflated, sums = call(
-        functools.partial(inflate_kernel, tall, wide),
+    line = jax.ShapeDtypeStruct((1, columns), f32)
+    sums = call(
+        functools.partial(sums_kernel, rows, tall, wide), "sums", line, partial, got
+    )
+    inflated, sums_here = call(
+        functools.partial(inflate_kernel, rows, tall, wide),
         "inflate",
-        [piece, jax.ShapeDtypeStruct((1, columns), f32)],
+        [piece, line],
         partial,
         got,
     )
     steps = [(2 * z + 1, 2 * (z ^ 1)) for z in range(4)] + [(2 * z, 2 * z + 1) for z in range(4)]
-    sums = sums + lax.ppermute(sums, ("row", "layer"), steps)
+    sums = sums_here + lax.ppermute(sums, ("row", "layer"), steps)
     steps = [(2 * z, 2 * (z ^ 2) + 1) for z in range(4)] + [(2 * z + 1, 2 * z) for z in range(4)]
     far = lax.ppermute(sums, ("row", "layer"), steps)
-    total = far + swapped(sums, "layer", 1)
-    total_low = swapped(total, "layer", 1)
     low = lax.axis_index("layer") == 0
-    sums = jnp.where(low, total_low[:, :half], total[:, half:])
+    half_sums = jnp.where(low, sums, far)
+    total = half_sums + swapped(half_sums, "layer", 1)
+    sums = jnp.where(low, total[:, :half], total[:, half:])
     total_rows = rows * count
     return inflated * (total_rows / (sums + epsilon))
 

time: 26.6 us -> 25.8 us (0.970)
  starting transfers between devices: 10.4 us -> 9.7 us
  waiting for transfers between devices: 13.5 us -> 13.2 us
    ppermute x5 -> x4, starting transfers between devices: 5.35 us -> 4.58 us  [swapped(): return lax.ppermute(value, axis, [(i, i ^ step) for i in range(count)])]
    ppermute x1, waiting for transfers between devices: 0.8 us -> 1.3 us  [on_device(): far = lax.ppermute(sums, ('row', 'layer'), steps)]
    ppermute x1, waiting for transfers between devices: 1.52 us -> 1.09 us  [on_device(): outer = lax.ppermute(first, 'row', [(0, 1), (1, 0), (2, 3), (3, 2)])]
    ppermute x1, waiting for transfers between devices: 2.87 us -> 2.58 us  [on_device(): sums = sums_here + lax.ppermute(sums, ('row', 'layer'), steps)]
    pallas_call x3 -> x5, Pallas kernels: 0.68 us -> 0.81 us  [call(): pl.pallas_call(kernel, out_shape=shapes, in_specs=[VMEM] * len(operands),...]
    ppermute x5 -> x4, waiting for transfers between devices: 5.96 us -> 5.94 us  [swapped(): return lax.ppermute(value, axis, [(i, i ^ step) for i in range(count)])]
  transfers between devices with their start and end apart: 11 -> 10, of which waited for: 8 -> 8; matrix products, arithmetic and copies ran while one was open for 0% -> 0% of each run, Pallas kernels for 0% -> 2%
where the time goes in v5:
time: 25.8 us; the launch traced here: 25.6 us
  waiting for transfers between devices  13.2 us (51%)
  starting transfers between devices  9.7 us (38%)
  Pallas kernels  1.9 us (7%)
  other arithmetic  0.75 us (3%)
    ppermute x4, waiting for transfers between devices, swapped(): return lax.ppermute(value, axis, [(i, i ^ step) for i in range(count)])  5.94 us
    ppermute x4, starting transfers between devices, swapped(): return lax.ppermute(value, axis, [(i, i ^ step) for i in range(count)])  4.58 us
    ppermute x1, starting transfers between devices, on_device(): first = lax.ppermute(right, 'row', [(0, 2), (3, 1), (1, 0), (2, 3)])  4.09 us
    ppermute x1, waiting for transfers between devices, on_device(): sums = sums_here + lax.ppermute(sums, ('row', 'layer'), steps)  2.58 us
    ppermute x1, waiting for transfers between devices, on_device(): second = lax.ppermute(right, 'row', [(0, 1), (3, 2), (1, 3), (2, 0)])  2.29 us
    ppermute x1, waiting for transfers between devices, on_device(): far = lax.ppermute(sums, ('row', 'layer'), steps)  1.3 us
    ppermute x1, waiting for transfers between devices, on_device(): outer = lax.ppermute(first, 'row', [(0, 1), (1, 0), (2, 3), (3, 2)])  1.09 us
    pallas_call x1, Pallas kernels, tiles(): pl.pallas_call(tiles_kernel, out_shape=[jax.ShapeDtypeStruct(operands[n]....  1.09 us
  transfers between devices with their start and end apart: 10, of which 8 were waited for; matrix products, arithmetic and copies ran while one was open for 0% of the time, Pallas kernels for 2%

profile of v5, /device:TPU:0, one launch (start us, length us, event | category | flops | bytes accessed | tf_op | source)
XLA Modules:
  0.0 25.6 jit_solution(8471521257136058546)
XLA Ops:
  0.0 1.1 %tiles.1 = (bf16[128,512]{1,0:T(8,128)(2,1)S(1)}, bf16[256,128]{1,0:T(8,128)(2,1)S(1)}) custom-call(s32[1,4]{1,0:T(1,128)} %bitcast.8, bf16[128,512]{1,0:T(8,128)(2,1)} %bitcast.5, s32[1,2]{1,0:T(1,128)} %bitcast.9, bf16[256,128]{1,0:T(8,128)(2,1)} %bitcast.6), custom_call_target="tpu_custom_call" | custom-call | tf_op jit(solution)/shard_map/tiles/pallas_call | solution.py:54
  1.1 4.1 %collective-permute-start.2 = (bf16[128,512]{1,0:T(8,128)(2,1)S(1)}, bf16[128,512]{1,0:T(8,128)(2,1)S(1)}, u32[]{:S(2)}, u32[]{:S(2)}) collective-permute-start(bf16[128,512]{1,0:T(8,128)(2,1)S(1)} %get-tuple-element.12.right), channel_id=1, source_target_pairs={{0,16},{24,8},{8,0},{16,24},{1,17},{25,9},{9,1},{17,25},{2,18},{26... | collective-permute-start | bytes 393224 | tf_op jit(solution)/shard_map/ppermute | solution.py:183
  5.2 1.5 %collective-permute-start = (bf16[256,128]{1,0:T(8,128)(2,1)S(1)}, bf16[256,128]{1,0:T(8,128)(2,1)S(1)}, u32[]{:S(2)}, u32[]{:S(2)}) collective-permute-start(bf16[256,128]{1,0:T(8,128)(2,1)S(1)} %get-tuple-element.11.here), channel_id=1, source_target_pairs={{0,2},{2,0},{4,6},{6,4},{1,3},{3,1},{5,7},{7,5},{8,10},{10,8},{12,... | collective-permute-start | bytes 196616 | tf_op jit(solution)/shard_map/ppermute | solution.py:81
  6.7 0.0 collective-permute-start.3
  6.7 0.0 collective-permute-start.4
  6.7 2.8 %collective-permute-done.beside = bf16[256,128]{1,0:T(8,128)(2,1)S(1)} collective-permute-done((bf16[256,128]{1,0:T(8,128)(2,1)S(1)}, bf16[256,128]{1,0:T(8,128)(2,1)S(1)}, u32[]{:S(2)}, u32[]{:S(2)}) %collective-permute-start) | collective-permute-done | bytes 65568 | tf_op jit(solution)/shard_map/ppermute | solution.py:81
  9.5 1.6 %collective-permute-start.1 = (bf16[2,256,128]{2,1,0:T(8,128)(2,1)S(1)}, bf16[2,256,128]{2,1,0:T(8,128)(2,1)S(1)}, u32[]{:S(2)}, u32[]{:S(2)}) collective-permute-start(bf16[2,256,128]{2,1,0:T(8,128)(2,1)S(1)} %pair.1.near), channel_id=1, source_target_pairs={{0,4},{2,6},{4,0},{6,2},{1,5},{3,7},{5,1},{7,3},{8,12},{10,14},{12... | collective-permute-start | bytes 393224 | tf_op jit(solution)/shard_map/ppermute | solution.py:81
  11.1 0.0 collective-permute-done.2.first
  11.1 0.7 %collective-permute-start.5 = (bf16[128,512]{1,0:T(8,128)(2,1)S(1)}, bf16[128,512]{1,0:T(8,128)(2,1)S(1)}, u32[]{:S(2)}, u32[]{:S(2)}) collective-permute-start(bf16[128,512]{1,0:T(8,128)(2,1)S(1)} %collective-permute-done.2.first), channel_id=1, source_target_pairs={{0,8},{8,0},{16,24},{24,16},{1,9},{9,1},{17,25},{25,17},{2,10},{10... | collective-permute-start | bytes 393224 | tf_op jit(solution)/shard_map/ppermute | solution.py:187
  11.8 2.3 %collective-permute-done.3.second = bf16[128,512]{1,0:T(8,128)(2,1)S(1)} collective-permute-done((bf16[128,512]{1,0:T(8,128)(2,1)S(1)}, bf16[128,512]{1,0:T(8,128)(2,1)S(1)}, u32[]{:S(2)}, u32[]{:S(2)}) %collective-permute-start.3) | collective-permute-done | bytes 131104 | tf_op jit(solution)/shard_map/ppermute | solution.py:184
  14.1 0.0 collective-permute-done.4.inner
  14.1 0.4 %collective-permute-done.1.far = bf16[2,256,128]{2,1,0:T(8,128)(2,1)S(1)} collective-permute-done((bf16[2,256,128]{2,1,0:T(8,128)(2,1)S(1)}, bf16[2,256,128]{2,1,0:T(8,128)(2,1)S(1)}, u32[]{:S(2)}, u32[]{:S(2)}) %collective-permute-start.1) | collective-permute-done | bytes 131104 | tf_op jit(solution)/shard_map/ppermute | solution.py:81
  14.5 0.4 %early.1 = (f32[264,512]{1,0:T(8,128)S(1)}, bf16[256,128]{1,0:T(8,128)(2,1)S(1)}) custom-call(bf16[2,256,128]{2,1,0:T(8,128)(2,1)S(1)} %pair.1.near, bf16[2,256,128]{2,1,0:T(8,128)(2,1)S(1)} %collective-permute-done.1.far, bf16[128,512]{1,0:T(8,128)(2,1)S(1)} %get-tuple-element.12.right, bf16[128,512]{1,0:T(8,128)(2,1)S(1)} %collective-permute-done.2.first, ...), custom_call_target="tpu_custom_call" | custom-call | tf_op jit(solution)/shard_map/early/pallas_call | solution.py:68
  14.9 1.1 %collective-permute-done.5.outer = bf16[128,512]{1,0:T(8,128)(2,1)S(1)} collective-permute-done((bf16[128,512]{1,0:T(8,128)(2,1)S(1)}, bf16[128,512]{1,0:T(8,128)(2,1)S(1)}, u32[]{:S(2)}, u32[]{:S(2)}) %collective-permute-start.5) | collective-permute-done | bytes 131104 | tf_op jit(solution)/shard_map/ppermute | solution.py:187
  16.0 0.2 product.1.mine
  16.3 0.1 collective-permute-start.6
  16.4 1.9 %collective-permute-done.6.got = f32[264,512]{1,0:T(8,128)S(1)} collective-permute-done((f32[264,512]{1,0:T(8,128)S(1)}, f32[264,512]{1,0:T(8,128)S(1)}, u32[]{:S(2)}, u32[]{:S(2)}) %collective-permute-start.6) | collective-permute-done | bytes 540704 | tf_op jit(solution)/shard_map/ppermute | solution.py:81
  18.3 0.3 %collective-permute-start.7 = (f32[1,512]{1,0:T(1,128)S(1)}, f32[1,512]{1,0:T(1,128)S(1)}, u32[]{:S(2)}, u32[]{:S(2)}) collective-permute-start(f32[1,512]{1,0:T(1,128)S(1)} %sums.1), channel_id=1, source_target_pairs={{1,8},{9,0},{17,24},{25,16},{0,1},{8,9},{16,17},{24,25},{3,10},{11... | collective-permute-start | bytes 6152 | tf_op jit(solution)/shard_map/ppermute | solution.py:222
  18.6 0.1 inflate.1
  18.7 2.6 %collective-permute-done.7 = f32[1,512]{1,0:T(1,128)S(1)} collective-permute-done((f32[1,512]{1,0:T(1,128)S(1)}, f32[1,512]{1,0:T(1,128)S(1)}, u32[]{:S(2)}, u32[]{:S(2)}) %collective-permute-start.7) | collective-permute-done | bytes 2080 | tf_op jit(solution)/shard_map/ppermute | solution.py:222
  21.3 1.3 %collective-permute-done.8 = f32[1,512]{1,0:T(1,128)S(1)} collective-permute-done((f32[1,512]{1,0:T(1,128)S(1)}, f32[1,512]{1,0:T(1,128)S(1)}, u32[]{:S(2)}, u32[]{:S(2)}) %collective-permute-start.8) | collective-permute-done | bytes 2080 | tf_op jit(solution)/shard_map/ppermute | solution.py:224
  22.6 1.4 %collective-permute-start.9 = (f32[1,512]{1,0:T(1,128)S(1)}, f32[1,512]{1,0:T(1,128)S(1)}, u32[]{:S(2)}, u32[]{:S(2)}) collective-permute-start(f32[1,512]{1,0:T(1,128)S(1)} %broadcast_select_fusion), channel_id=1, source_target_pairs={{0,1},{1,0},{2,3},{3,2},{4,5},{5,4},{6,7},{7,6},{8,9},{9,8},{10,11... | collective-permute-start | bytes 6152 | tf_op jit(solution)/shard_map/ppermute | solution.py:81
  24.1 0.8 %collective-permute-done.9 = f32[1,512]{1,0:T(1,128)S(1)} collective-permute-done((f32[1,512]{1,0:T(1,128)S(1)}, f32[1,512]{1,0:T(1,128)S(1)}, u32[]{:S(2)}, u32[]{:S(2)}) %collective-permute-start.9) | collective-permute-done | bytes 2080 | tf_op jit(solution)/shard_map/ppermute | solution.py:81
  24.9 0.7 %broadcast_multiply_fusion = f32[256,256]{1,0:T(8,128)} fusion(f32[256,256]{1,0:T(8,128)S(1)} %get-tuple-element.15, f32[256]{0:T(256)S(1)} %bitcast.7), kind=kLoop, calls=%fused_computation | loop fusion | flops 65536 | bytes 525312 | tf_op jit(solution)/shard_map/mul | solution.py:230
  (9 shorter events, 0.0 us)
Async XLA Ops:
  1.1 10.0 %collective-permute-start.2 = (bf16[128,512]{1,0:T(8,128)(2,1)S(1)}, bf16[128,512]{1,0:T(8,128)(2,1)S(1)}, u32[]{:S(2)}, u32[]{:S(2)}) collective-permute-start(bf16[128,512]{1,0:T(8,128)(2,1)S(1)} %get-tuple-element.12.right), channel_id=1, source_target_pairs={{0,16},{24,8},{8,0},{16,24},{1,17},{25,9},{9,1},{17,25},{2,18},{26... | collective-permute-start | bytes 393224 | tf_op jit(solution)/shard_map/ppermute | solution.py:183
  5.2 9.3 %copy-start = (s32[2,2]{1,0:T(2,128)S(1)}, s32[2,2]{1,0:T(2,128)}, u32[]{:S(2)}) copy-start(s32[2,2]{1,0:T(2,128)} %mask.1) | copy-start | bytes 52
  5.2 4.3 %collective-permute-start = (bf16[256,128]{1,0:T(8,128)(2,1)S(1)}, bf16[256,128]{1,0:T(8,128)(2,1)S(1)}, u32[]{:S(2)}, u32[]{:S(2)}) collective-permute-start(bf16[256,128]{1,0:T(8,128)(2,1)S(1)} %get-tuple-element.11.here), channel_id=1, source_target_pairs={{0,2},{2,0},{4,6},{6,4},{1,3},{3,1},{5,7},{7,5},{8,10},{10,8},{12,... | collective-permute-start | bytes 196616 | tf_op jit(solution)/shard_map/ppermute | solution.py:81
  6.7 7.4 %collective-permute-start.3 = (bf16[128,512]{1,0:T(8,128)(2,1)S(1)}, bf16[128,512]{1,0:T(8,128)(2,1)S(1)}, u32[]{:S(2)}, u32[]{:S(2)}) collective-permute-start(bf16[128,512]{1,0:T(8,128)(2,1)S(1)} %get-tuple-element.12.right), channel_id=1, source_target_pairs={{0,8},{24,16},{8,24},{16,0},{1,9},{25,17},{9,25},{17,1},{2,10},{26... | collective-permute-start | bytes 393224 | tf_op jit(solution)/shard_map/ppermute | solution.py:184
  6.7 7.4 %collective-permute-start.4 = (bf16[128,512]{1,0:T(8,128)(2,1)S(1)}, bf16[128,512]{1,0:T(8,128)(2,1)S(1)}, u32[]{:S(2)}, u32[]{:S(2)}) collective-permute-start(bf16[128,512]{1,0:T(8,128)(2,1)S(1)} %get-tuple-element.12.right), channel_id=1, source_target_pairs={{8,16},{9,17},{16,8},{17,9},{0,1},{1,0},{24,25},{25,24},{10,18},{1... | collective-permute-start | bytes 393224 | tf_op jit(solution)/shard_map/ppermute | solution.py:186
  9.5 5.0 %collective-permute-start.1 = (bf16[2,256,128]{2,1,0:T(8,128)(2,1)S(1)}, bf16[2,256,128]{2,1,0:T(8,128)(2,1)S(1)}, u32[]{:S(2)}, u32[]{:S(2)}) collective-permute-start(bf16[2,256,128]{2,1,0:T(8,128)(2,1)S(1)} %pair.1.near), channel_id=1, source_target_pairs={{0,4},{2,6},{4,0},{6,2},{1,5},{3,7},{5,1},{7,3},{8,12},{10,14},{12... | collective-permute-start | bytes 393224 | tf_op jit(solution)/shard_map/ppermute | solution.py:81
  11.1 5.0 %collective-permute-start.5 = (bf16[128,512]{1,0:T(8,128)(2,1)S(1)}, bf16[128,512]{1,0:T(8,128)(2,1)S(1)}, u32[]{:S(2)}, u32[]{:S(2)}) collective-permute-start(bf16[128,512]{1,0:T(8,128)(2,1)S(1)} %collective-permute-done.2.first), channel_id=1, source_target_pairs={{0,8},{8,0},{16,24},{24,16},{1,9},{9,1},{17,25},{25,17},{2,10},{10... | collective-permute-start | bytes 393224 | tf_op jit(solution)/shard_map/ppermute | solution.py:187
  16.3 2.0 %collective-permute-start.6 = (f32[264,512]{1,0:T(8,128)S(1)}, f32[264,512]{1,0:T(8,128)S(1)}, u32[]{:S(2)}, u32[]{:S(2)}) collective-permute-start(f32[264,512]{1,0:T(8,128)S(1)} %product.1.mine), channel_id=1, source_target_pairs={{0,1},{1,0},{2,3},{3,2},{4,5},{5,4},{6,7},{7,6},{8,9},{9,8},{10,11... | collective-permute-start | bytes 1622024 | tf_op jit(solution)/shard_map/ppermute | solution.py:81
  18.3 3.0 %collective-permute-start.7 = (f32[1,512]{1,0:T(1,128)S(1)}, f32[1,512]{1,0:T(1,128)S(1)}, u32[]{:S(2)}, u32[]{:S(2)}) collective-permute-start(f32[1,512]{1,0:T(1,128)S(1)} %sums.1), channel_id=1, source_target_pairs={{1,8},{9,0},{17,24},{25,16},{0,1},{8,9},{16,17},{24,25},{3,10},{11... | collective-permute-start | bytes 6152 | tf_op jit(solution)/shard_map/ppermute | solution.py:222
  21.3 1.3 %collective-permute-start.8 = (f32[1,512]{1,0:T(1,128)S(1)}, f32[1,512]{1,0:T(1,128)S(1)}, u32[]{:S(2)}, u32[]{:S(2)}) collective-permute-start(f32[1,512]{1,0:T(1,128)S(1)} %add.12), channel_id=1, source_target_pairs={{0,17},{8,25},{16,1},{24,9},{1,0},{9,8},{17,16},{25,24},{2,19},{10... | collective-permute-start | bytes 6152 | tf_op jit(solution)/shard_map/ppermute | solution.py:224
  22.6 2.3 %collective-permute-start.9 = (f32[1,512]{1,0:T(1,128)S(1)}, f32[1,512]{1,0:T(1,128)S(1)}, u32[]{:S(2)}, u32[]{:S(2)}) collective-permute-start(f32[1,512]{1,0:T(1,128)S(1)} %broadcast_select_fusion), channel_id=1, source_target_pairs={{0,1},{1,0},{2,3},{3,2},{4,5},{5,4},{6,7},{7,6},{8,9},{9,8},{10,11... | collective-permute-start | bytes 6152 | tf_op jit(solution)/shard_map/ppermute | solution.py:81

commit v6 on v5

--- a/solution.py
+++ b/solution.py
@@ -86,87 +86,95 @@
     out[1] = beside[...]
 
 
-def early_kernel(near, far, right, first, second, inner, mask, out, left, held):
+def early_kernel(near, far, right, first, second, inner, mask, *refs):
+    outs, left, handed, held = refs[:-3], refs[-3], refs[-2], refs[-1]
+    handed[...] = inner[...]
     held[0:2] = near[...]
     held[2:4] = far[...]
     row, col = lax.axis_index("row"), lax.axis_index("col")
     block = lax.rem(2 * row + 1, 5)
     left[...] = held[row ^ 3 ^ col]
-    rows, columns = left.shape[0], out.shape[1]
-    total = jnp.zeros((rows, columns), jnp.float32)
-    for here, values in ((row, right), (block, first), (block ^ 3, second)):
-        total += jnp.dot(
-            held[here ^ col], values[...], preferred_element_type=jnp.float32
+    (rows, depth), broad = left.shape, outs[0].shape[1]
+    tall, wide = mask.shape
+    share = rows // len(outs)
+    for n, out in enumerate(outs):
+        columns = slice(n * broad, (n + 1) * broad)
+        total = jnp.zeros((rows, broad), jnp.float32)
+        for here, values in ((row, right), (block, first), (block ^ 3, second)):
+            total += jnp.dot(
+                held[here ^ col], values[:, columns], preferred_element_type=jnp.float32
+            )
+        out[0:rows, :] = total
+        for i in range(tall):
+            kept = entry(mask, i, n % wide).astype(jnp.float32)
+            out[rows + i : rows + i + 1, :] = jnp.broadcast_to(kept, (1, broad))
+        out[out.shape[0] - share :, :] = left[n * share : (n + 1) * share, :].astype(
+            jnp.float32
         )
-    out[0:rows, :] = total
+
+
+def last_kernel(inner, outer, out):
+    row = lax.axis_index("row")
 
     @pl.when(jnp.logical_or(row == 1, row == 2))
     def _():
-        out[0:rows, :] += jnp.dot(
-            left[...], inner[...], preferred_element_type=jnp.float32
-        )
-
-    tall, wide = mask.shape
-    broad = columns // 2 // wide
-    for i in range(tall):
-        for j in range(2 * wide):
-            kept = entry(mask, i, j % wide).astype(jnp.float32)
-            at = (slice(rows + i, rows + i + 1), slice(j * broad, (j + 1) * broad))
-            out[at] = jnp.broadcast_to(kept, (1, broad))
-
-
-def product_kernel(early, left, outer, out):
-    row = lax.axis_index("row")
-    rows = left.shape[0]
-    out[...] = early[...]
+        out[...] = inner[...]
 
     @pl.when(jnp.logical_or(row == 0, row == 3))
     def _():
-        out[0:rows, :] += jnp.dot(
-            left[...], outer[...], preferred_element_type=jnp.float32
-        )
-
-
-def inflate(own, side, rows, tall, wide, mine, got, out, sums):
-    half = mine.shape[1] // 2
-    broad = half // wide
-    for j in range(wide):
-        columns = slice(side * half + j * broad, side * half + (j + 1) * broad)
+        out[...] = outer[...]
+
+
+def inflate(own, sides, sizes, ours, theirs, out, sums):
+    rows, half, tall, wide = sizes
+    high, broad = rows // tall, half // wide
+    share = rows // (2 * wide)
+    here = ours[-2][...]
+    there = jnp.concatenate([part[part.shape[0] - share :, :] for part in theirs[:-1]], axis=0)
+    left = jnp.concatenate([here, there.astype(here.dtype)], axis=1)
+    for n in range(2 * wide):
+        if n // wide not in sides:
+            continue
+        columns = slice(n * broad, (n + 1) * broad)
+        right = jnp.concatenate([ours[-1][:, columns], theirs[-1][:, columns]], axis=0)
+        product = ours[n][0:rows, :] + theirs[n][0:rows, :]
+        product += jnp.dot(left, right, preferred_element_type=jnp.float32)
         total = jnp.zeros((1, broad), jnp.float32)
+        across = slice(n % wide * broad, (n % wide + 1) * broad)
         for i in range(tall):
-            high = rows // tall
-            at = (slice(i * high, (i + 1) * high), columns)
-            product = mine[at] + got[at]
-            kept = (mine if own else got)[rows + i : rows + i + 1, columns] != 0.0
-            value = jnp.where(jnp.broadcast_to(kept, product.shape), product * product, 0.0)
-            if out is not None:
-                out[at[0], j * broad : (j + 1) * broad] = value
-            if sums is not None:
-                total += jnp.sum(value, axis=0, keepdims=True)
+            at = slice(i * high, (i + 1) * high)
+            kept = (ours if n // wide == own else theirs)[n][rows + i : rows + i + 1, :] != 0.0
+            kept = jnp.broadcast_to(kept, (high, broad))
+            value = jnp.where(kept, product[at, :] * product[at, :], 0.0)
+            if n // wide == own and out is not None:
+                out[at, across] = value
+            total += jnp.sum(value, axis=0, keepdims=True)
         if sums is not None:
             sums[:, columns] = total
 
 
-def sums_kernel(rows, tall, wide, mine, got, sums):
+def sums_kernel(sizes, *refs):
+    count = 2 * sizes[3]
+    ours, theirs, sums = refs[: count + 2], refs[count + 2 : -1], refs[-1]
     sums[...] = jnp.zeros_like(sums)
 
     @pl.when(lax.axis_index("layer") == 1)
     def _():
-        inflate(False, 0, rows, tall, wide, mine, got, None, sums)
-        inflate(True, 1, rows, tall, wide, mine, got, None, sums)
-
-
-def inflate_kernel(rows, tall, wide, mine, got, out, sums):
+        inflate(1, (0, 1), sizes, ours, theirs, None, sums)
+
+
+def inflate_kernel(sizes, *refs):
+    count = 2 * sizes[3]
+    ours, theirs, out, sums = refs[: count + 2], refs[count + 2 : -2], refs[-2], refs[-1]
     sums[...] = jnp.zeros_like(sums)
 
     @pl.when(lax.axis_index("layer") == 0)
     def _():
-        inflate(True, 0, rows, tall, wide, mine, got, out, sums)
-        inflate(False, 1, rows, tall, wide, mine, got, None, sums)
+        inflate(0, (0, 1), sizes, ours, theirs, out, sums)
 
     @pl.when(lax.axis_index("layer") == 1)
     def _():
-        inflate(True, 1, rows, tall, wide, mine, got, out, None)
+        inflate(1, (1,), sizes, ours, theirs, out, None)
 
 
 def on_device(left_blocks, batch_blocks, left_mask, batch_mask, prune_mask):
@@ -191,11 +199,13 @@
     )
     piece = jax.ShapeDtypeStruct((rows, half), f32)
     tall, wide = prune_mask.shape
-    whole = jax.ShapeDtypeStruct((rows + (tall + 7) // 8 * 8, columns), f32)
-    early, last = call(
+    parts = 2 * wide
+    share = rows // parts
+    part = jax.ShapeDtypeStruct((rows + (tall + 7) // 8 * 8 + share, columns // parts), f32)
+    ours = call(
         early_kernel,
         "early",
-        [whole, jax.ShapeDtypeStruct(left.shape, left.dtype)],
+        [part] * parts + [jax.ShapeDtypeStruct(v.shape, v.dtype) for v in (left, right)],
         pair,
         swapped(pair, "col", 2),
         right,
@@ -205,27 +215,25 @@
         prune_mask,
         scratch=[pltpu.VMEM((4,) + left.shape, left.dtype)],
     )
-    partial = call(product_kernel, "product", whole, early, last, outer)
-    got = swapped(partial, "layer", 1)
+    last = call(
+        last_kernel, "last", jax.ShapeDtypeStruct(right.shape, right.dtype), ours[-1], outer
+    )
+    operands = list(ours[:-1]) + [last]
+    operands += [swapped(value, "layer", 1) for value in ours[:-2]]
+    operands.append(swapped(last, "layer", 1))
+    sizes = (rows, half, tall, wide)
     line = jax.ShapeDtypeStruct((1, columns), f32)
-    sums = call(
-        functools.partial(sums_kernel, rows, tall, wide), "sums", line, partial, got
-    )
+    sums = call(functools.partial(sums_kernel, sizes), "sums", line, *operands)
     inflated, sums_here = call(
-        functools.partial(inflate_kernel, rows, tall, wide),
-        "inflate",
-        [piece, line],
-        partial,
-        got,
-    )
-    steps = [(2 * z + 1, 2 * (z ^ 1)) for z in range(4)] + [(2 * z, 2 * z + 1) for z in range(4)]
-    sums = sums_here + lax.ppermute(sums, ("row", "layer"), steps)
-    steps = [(2 * z, 2 * (z ^ 2) + 1) for z in range(4)] + [(2 * z + 1, 2 * z) for z in range(4)]
-    far = lax.ppermute(sums, ("row", "layer"), steps)
+        functools.partial(inflate_kernel, sizes), "inflate", [piece, line], *operands
+    )
+    total = sums_here
+    for step in (1, 2, 3):
+        pairs = [(2 * z + 1, 2 * (z ^ step)) for z in range(count)]
+        pairs += [(2 * z, 2 * z + 1) for z in range(count)]
+        total = total + lax.ppermute(sums, ("row", "layer"), pairs)
     low = lax.axis_index("layer") == 0
-    half_sums = jnp.where(low, sums, far)
-    total = half_sums + swapped(half_sums, "layer", 1)
-    sums = jnp.where(low, total[:, :half], total[:, half:])
+    sums = jnp.where(low, total[:, :half], swapped(total[:, half:], "layer", 1))
     total_rows = rows * count
     return inflated * (total_rows / (sums + epsilon))
 

time: 25.8 us -> 24.6 us (0.953)
  waiting for transfers between devices: 13.2 us -> 9.61 us
  starting transfers between devices: 9.7 us -> 12.1 us
    ppermute x2 -> x3, starting transfers between devices: 0.31 us -> 3.01 us  [on_device(): total = total + lax.ppermute(sums, ('row', 'layer'), pairs)]
    ppermute x2 -> x3, waiting for transfers between devices: 3.88 us -> 1.61 us  [on_device(): total = total + lax.ppermute(sums, ('row', 'layer'), pairs)]
    ppermute x1, waiting for transfers between devices: 1.09 us -> 0.06 us  [on_device(): outer = lax.ppermute(first, 'row', [(0, 1), (1, 0), (2, 3), (3, 2)])]
    ppermute x4 -> x8, waiting for transfers between devices: 5.94 us -> 5.65 us  [swapped(): return lax.ppermute(value, axis, [(i, i ^ step) for i in range(count)])]
    ppermute x4 -> x8, starting transfers between devices: 4.58 us -> 4.31 us  [swapped(): return lax.ppermute(value, axis, [(i, i ^ step) for i in range(count)])]
  transfers between devices with their start and end apart: 10 -> 15, of which waited for: 8 -> 12; matrix products, arithmetic and copies ran while one was open for 0% -> 0% of each run, Pallas kernels for 2% -> 3%
where the time goes in v6:
time: 24.6 us; the launch traced here: 24.4 us
  starting transfers between devices  12.1 us (49%)
  waiting for transfers between devices  9.61 us (39%)
  Pallas kernels  1.79 us (7%)
  other arithmetic  0.74 us (3%)
    ppermute x8, waiting for transfers between devices, swapped(): return lax.ppermute(value, axis, [(i, i ^ step) for i in range(count)])  5.65 us
    ppermute x8, starting transfers between devices, swapped(): return lax.ppermute(value, axis, [(i, i ^ step) for i in range(count)])  4.31 us
    ppermute x1, starting transfers between devices, on_device(): first = lax.ppermute(right, 'row', [(0, 2), (3, 1), (1, 0), (2, 3)])  4.09 us
    ppermute x3, starting transfers between devices, on_device(): total = total + lax.ppermute(sums, ('row', 'layer'), pairs)  3.01 us
    ppermute x1, waiting for transfers between devices, on_device(): second = lax.ppermute(right, 'row', [(0, 1), (3, 2), (1, 3), (2, 0)])  2.29 us
    ppermute x3, waiting for transfers between devices, on_device(): total = total + lax.ppermute(sums, ('row', 'layer'), pairs)  1.61 us
    pallas_call x1, Pallas kernels, tiles(): pl.pallas_call(tiles_kernel, out_shape=[jax.ShapeDtypeStruct(operands[n]....  1.09 us
    mul x1, other arithmetic, on_device(): return inflated * (total_rows / (sums + epsilon))  0.73 us
  transfers between devices with their start and end apart: 15, of which 12 were waited for; matrix products, arithmetic and copies ran while one was open for 0% of the time, Pallas kernels for 3%

profile of v6, /device:TPU:0, one launch (start us, length us, event | category | flops | bytes accessed | tf_op | source)
XLA Modules:
  0.0 24.4 jit_solution(12933824950823480084)
XLA Ops:
  0.0 1.1 %tiles.1 = (bf16[128,512]{1,0:T(8,128)(2,1)S(1)}, bf16[256,128]{1,0:T(8,128)(2,1)S(1)}) custom-call(s32[1,4]{1,0:T(1,128)} %bitcast.8, bf16[128,512]{1,0:T(8,128)(2,1)} %bitcast.5, s32[1,2]{1,0:T(1,128)} %bitcast.9, bf16[256,128]{1,0:T(8,128)(2,1)} %bitcast.6), custom_call_target="tpu_custom_call" | custom-call | tf_op jit(solution)/shard_map/tiles/pallas_call | solution.py:54
  1.1 4.1 %collective-permute-start.2 = (bf16[128,512]{1,0:T(8,128)(2,1)S(1)}, bf16[128,512]{1,0:T(8,128)(2,1)S(1)}, u32[]{:S(2)}, u32[]{:S(2)}) collective-permute-start(bf16[128,512]{1,0:T(8,128)(2,1)S(1)} %get-tuple-element.16.right), channel_id=1, source_target_pairs={{0,16},{24,8},{8,0},{16,24},{1,17},{25,9},{9,1},{17,25},{2,18},{26... | collective-permute-start | bytes 393224 | tf_op jit(solution)/shard_map/ppermute | solution.py:191
  5.2 1.5 %collective-permute-start = (bf16[256,128]{1,0:T(8,128)(2,1)S(1)}, bf16[256,128]{1,0:T(8,128)(2,1)S(1)}, u32[]{:S(2)}, u32[]{:S(2)}) collective-permute-start(bf16[256,128]{1,0:T(8,128)(2,1)S(1)} %get-tuple-element.15.here), channel_id=1, source_target_pairs={{0,2},{2,0},{4,6},{6,4},{1,3},{3,1},{5,7},{7,5},{8,10},{10,8},{12,... | collective-permute-start | bytes 196616 | tf_op jit(solution)/shard_map/ppermute | solution.py:81
  6.7 2.8 %collective-permute-done.beside = bf16[256,128]{1,0:T(8,128)(2,1)S(1)} collective-permute-done((bf16[256,128]{1,0:T(8,128)(2,1)S(1)}, bf16[256,128]{1,0:T(8,128)(2,1)S(1)}, u32[]{:S(2)}, u32[]{:S(2)}) %collective-permute-start) | collective-permute-done | bytes 65568 | tf_op jit(solution)/shard_map/ppermute | solution.py:81
  9.5 1.6 %collective-permute-start.1 = (bf16[2,256,128]{2,1,0:T(8,128)(2,1)S(1)}, bf16[2,256,128]{2,1,0:T(8,128)(2,1)S(1)}, u32[]{:S(2)}, u32[]{:S(2)}) collective-permute-start(bf16[2,256,128]{2,1,0:T(8,128)(2,1)S(1)} %pair.1.near), channel_id=1, source_target_pairs={{0,4},{2,6},{4,0},{6,2},{1,5},{3,7},{5,1},{7,3},{8,12},{10,14},{12... | collective-permute-start | bytes 393224 | tf_op jit(solution)/shard_map/ppermute | solution.py:81
  11.1 0.7 %collective-permute-start.5 = (bf16[128,512]{1,0:T(8,128)(2,1)S(1)}, bf16[128,512]{1,0:T(8,128)(2,1)S(1)}, u32[]{:S(2)}, u32[]{:S(2)}) collective-permute-start(bf16[128,512]{1,0:T(8,128)(2,1)S(1)} %collective-permute-done.2.first), channel_id=1, source_target_pairs={{0,8},{8,0},{16,24},{24,16},{1,9},{9,1},{17,25},{25,17},{2,10},{10... | collective-permute-start | bytes 393224 | tf_op jit(solution)/shard_map/ppermute | solution.py:195
  11.8 2.3 %collective-permute-done.3.second = bf16[128,512]{1,0:T(8,128)(2,1)S(1)} collective-permute-done((bf16[128,512]{1,0:T(8,128)(2,1)S(1)}, bf16[128,512]{1,0:T(8,128)(2,1)S(1)}, u32[]{:S(2)}, u32[]{:S(2)}) %collective-permute-start.3) | collective-permute-done | bytes 131104 | tf_op jit(solution)/shard_map/ppermute | solution.py:192
  14.1 0.4 %collective-permute-done.1.far = bf16[2,256,128]{2,1,0:T(8,128)(2,1)S(1)} collective-permute-done((bf16[2,256,128]{2,1,0:T(8,128)(2,1)S(1)}, bf16[2,256,128]{2,1,0:T(8,128)(2,1)S(1)}, u32[]{:S(2)}, u32[]{:S(2)}) %collective-permute-start.1) | collective-permute-done | bytes 131104 | tf_op jit(solution)/shard_map/ppermute | solution.py:81
  14.5 0.4 %early.1 = (f32[328,128]{1,0:T(8,128)S(1)}, f32[328,128]{1,0:T(8,128)S(1)}, f32[328,128]{1,0:T(8,128)S(1)}, f32[328,128]{1,0:T(8,128)S(1)}, bf16[256,128]{1,0:T(8,128)(2,1)S(1)}, /*index=5*/bf16[128,512]{1,0:T(8,128)(2,1)S(1)}) custom-call(bf16[2,256,128]{2,1,0:T(8,128)(2,1)S(1)} %pair.1.near, bf16[2,256,128]{2,1,0:T(8,128)(2,1)S(1)} %collective-permute-done.1.far, ...), custom_call_target="tpu_custom_call" | custom-call | tf_op jit(solution)/shard_map/early/pallas_call | solution.py:68
  15.0 0.5 %collective-permute-start.7 = (f32[328,128]{1,0:T(8,128)S(1)}, f32[328,128]{1,0:T(8,128)S(1)}, u32[]{:S(2)}, u32[]{:S(2)}) collective-permute-start(f32[328,128]{1,0:T(8,128)S(1)} %get-tuple-element.18.refs_1_), channel_id=1, source_target_pairs={{0,1},{1,0},{2,3},{3,2},{4,5},{5,4},{6,7},{7,6},{8,9},{9,8},{10,11... | collective-permute-start | bytes 503816 | tf_op jit(solution)/shard_map/ppermute | solution.py:81
  15.5 0.4 %collective-permute-start.9 = (f32[328,128]{1,0:T(8,128)S(1)}, f32[328,128]{1,0:T(8,128)S(1)}, u32[]{:S(2)}, u32[]{:S(2)}) collective-permute-start(f32[328,128]{1,0:T(8,128)S(1)} %get-tuple-element.20.refs_3_), channel_id=1, source_target_pairs={{0,1},{1,0},{2,3},{3,2},{4,5},{5,4},{6,7},{7,6},{8,9},{9,8},{10,11... | collective-permute-start | bytes 503816 | tf_op jit(solution)/shard_map/ppermute | solution.py:81
  16.1 0.2 collective-permute-done.6.refs_6_
  16.3 0.2 collective-permute-done.7.refs_7_
  16.6 0.3 %collective-permute-done.8.refs_8_ = f32[328,128]{1,0:T(8,128)S(1)} collective-permute-done((f32[328,128]{1,0:T(8,128)S(1)}, f32[328,128]{1,0:T(8,128)S(1)}, u32[]{:S(2)}, u32[]{:S(2)}) %collective-permute-start.8) | collective-permute-done | bytes 167968 | tf_op jit(solution)/shard_map/ppermute | solution.py:81
  16.9 0.2 collective-permute-done.9.refs_9_
  17.1 0.4 %collective-permute-done.10.refs_10_ = bf16[128,512]{1,0:T(8,128)(2,1)S(1)} collective-permute-done((bf16[128,512]{1,0:T(8,128)(2,1)S(1)}, bf16[128,512]{1,0:T(8,128)(2,1)S(1)}, u32[]{:S(2)}, u32[]{:S(2)}) %collective-permute-start.10) | collective-permute-done | bytes 131104 | tf_op jit(solution)/shard_map/ppermute | solution.py:81
  17.5 0.5 %collective-permute-start.13 = (f32[1,512]{1,0:T(1,128)S(1)}, f32[1,512]{1,0:T(1,128)S(1)}, u32[]{:S(2)}, u32[]{:S(2)}) collective-permute-start(f32[1,512]{1,0:T(1,128)S(1)} %sums.1), channel_id=1, source_target_pairs={{1,24},{9,16},{17,8},{25,0},{0,1},{8,9},{16,17},{24,25},{3,26},{11... | collective-permute-start | bytes 6152 | tf_op jit(solution)/shard_map/ppermute | solution.py:234
  18.0 1.4 %collective-permute-start.12 = (f32[1,512]{1,0:T(1,128)S(1)}, f32[1,512]{1,0:T(1,128)S(1)}, u32[]{:S(2)}, u32[]{:S(2)}) collective-permute-start(f32[1,512]{1,0:T(1,128)S(1)} %sums.1), channel_id=1, source_target_pairs={{1,16},{9,24},{17,0},{25,8},{0,1},{8,9},{16,17},{24,25},{3,18},{11... | collective-permute-start | bytes 6152 | tf_op jit(solution)/shard_map/ppermute | solution.py:234
  19.4 1.1 %collective-permute-start.11 = (f32[1,512]{1,0:T(1,128)S(1)}, f32[1,512]{1,0:T(1,128)S(1)}, u32[]{:S(2)}, u32[]{:S(2)}) collective-permute-start(f32[1,512]{1,0:T(1,128)S(1)} %sums.1), channel_id=1, source_target_pairs={{1,8},{9,0},{17,24},{25,16},{0,1},{8,9},{16,17},{24,25},{3,10},{11... | collective-permute-start | bytes 6152 | tf_op jit(solution)/shard_map/ppermute | solution.py:234
  20.5 0.3 %inflate.1 = (f32[256,256]{1,0:T(8,128)S(1)}, f32[1,512]{1,0:T(1,128)S(1)}) custom-call(f32[328,128]{1,0:T(8,128)S(1)} %get-tuple-element.17.refs_0_, f32[328,128]{1,0:T(8,128)S(1)} %get-tuple-element.18.refs_1_, f32[328,128]{1,0:T(8,128)S(1)} %get-tuple-element.19.refs_2_, f32[328,128]{1,0:T(8,128)S(1)} %get-tuple-element.20.refs_3_, ...), custom_call_target="tpu_custom_call" | custom-call | tf_op jit(solution)/shard_map/inflate/pallas_call | solution.py:68
  20.8 1.5 %collective-permute-done.13 = f32[1,512]{1,0:T(1,128)S(1)} collective-permute-done((f32[1,512]{1,0:T(1,128)S(1)}, f32[1,512]{1,0:T(1,128)S(1)}, u32[]{:S(2)}, u32[]{:S(2)}) %collective-permute-start.13) | collective-permute-done | bytes 2080 | tf_op jit(solution)/shard_map/ppermute | solution.py:234
  22.3 0.1 collective-permute-done.11
  22.5 1.1 %collective-permute-done.14 = f32[1,256]{1,0:T(1,128)S(1)} collective-permute-done((f32[1,256]{1,0:T(1,128)S(1)}, f32[1,256]{1,0:T(1,128)S(1)}, u32[]{:S(2)}, u32[]{:S(2)}) %collective-permute-start.14) | collective-permute-done | bytes 1056 | tf_op jit(solution)/shard_map/ppermute | solution.py:81
  23.6 0.7 %broadcast_multiply_fusion = f32[256,256]{1,0:T(8,128)} fusion(f32[256,256]{1,0:T(8,128)S(1)} %get-tuple-element.23, f32[256]{0:T(256)S(1)} %bitcast.7), kind=kLoop, calls=%fused_computation | loop fusion | flops 65536 | bytes 525312 | tf_op jit(solution)/shard_map/mul | solution.py:238
  (18 shorter events, 0.4 us)
Async XLA Ops:
  1.1 10.0 %collective-permute-start.2 = (bf16[128,512]{1,0:T(8,128)(2,1)S(1)}, bf16[128,512]{1,0:T(8,128)(2,1)S(1)}, u32[]{:S(2)}, u32[]{:S(2)}) collective-permute-start(bf16[128,512]{1,0:T(8,128)(2,1)S(1)} %get-tuple-element.16.right), channel_id=1, source_target_pairs={{0,16},{24,8},{8,0},{16,24},{1,17},{25,9},{9,1},{17,25},{2,18},{26... | collective-permute-start | bytes 393224 | tf_op jit(solution)/shard_map/ppermute | solution.py:191
  5.2 9.3 %copy-start = (s32[2,2]{1,0:T(2,128)S(1)}, s32[2,2]{1,0:T(2,128)}, u32[]{:S(2)}) copy-start(s32[2,2]{1,0:T(2,128)} %mask.1) | copy-start | bytes 52
  5.2 4.3 %collective-permute-start = (bf16[256,128]{1,0:T(8,128)(2,1)S(1)}, bf16[256,128]{1,0:T(8,128)(2,1)S(1)}, u32[]{:S(2)}, u32[]{:S(2)}) collective-permute-start(bf16[256,128]{1,0:T(8,128)(2,1)S(1)} %get-tuple-element.15.here), channel_id=1, source_target_pairs={{0,2},{2,0},{4,6},{6,4},{1,3},{3,1},{5,7},{7,5},{8,10},{10,8},{12,... | collective-permute-start | bytes 196616 | tf_op jit(solution)/shard_map/ppermute | solution.py:81
  6.7 7.4 %collective-permute-start.3 = (bf16[128,512]{1,0:T(8,128)(2,1)S(1)}, bf16[128,512]{1,0:T(8,128)(2,1)S(1)}, u32[]{:S(2)}, u32[]{:S(2)}) collective-permute-start(bf16[128,512]{1,0:T(8,128)(2,1)S(1)} %get-tuple-element.16.right), channel_id=1, source_target_pairs={{0,8},{24,16},{8,24},{16,0},{1,9},{25,17},{9,25},{17,1},{2,10},{26... | collective-permute-start | bytes 393224 | tf_op jit(solution)/shard_map/ppermute | solution.py:192
  6.7 7.4 %collective-permute-start.4 = (bf16[128,512]{1,0:T(8,128)(2,1)S(1)}, bf16[128,512]{1,0:T(8,128)(2,1)S(1)}, u32[]{:S(2)}, u32[]{:S(2)}) collective-permute-start(bf16[128,512]{1,0:T(8,128)(2,1)S(1)} %get-tuple-element.16.right), channel_id=1, source_target_pairs={{8,16},{9,17},{16,8},{17,9},{0,1},{1,0},{24,25},{25,24},{10,18},{1... | collective-permute-start | bytes 393224 | tf_op jit(solution)/shard_map/ppermute | solution.py:194
  9.5 5.0 %collective-permute-start.1 = (bf16[2,256,128]{2,1,0:T(8,128)(2,1)S(1)}, bf16[2,256,128]{2,1,0:T(8,128)(2,1)S(1)}, u32[]{:S(2)}, u32[]{:S(2)}) collective-permute-start(bf16[2,256,128]{2,1,0:T(8,128)(2,1)S(1)} %pair.1.near), channel_id=1, source_target_pairs={{0,4},{2,6},{4,0},{6,2},{1,5},{3,7},{5,1},{7,3},{8,12},{10,14},{12... | collective-permute-start | bytes 393224 | tf_op jit(solution)/shard_map/ppermute | solution.py:81
  11.1 5.0 %collective-permute-start.5 = (bf16[128,512]{1,0:T(8,128)(2,1)S(1)}, bf16[128,512]{1,0:T(8,128)(2,1)S(1)}, u32[]{:S(2)}, u32[]{:S(2)}) collective-permute-start(bf16[128,512]{1,0:T(8,128)(2,1)S(1)} %collective-permute-done.2.first), channel_id=1, source_target_pairs={{0,8},{8,0},{16,24},{24,16},{1,9},{9,1},{17,25},{25,17},{2,10},{10... | collective-permute-start | bytes 393224 | tf_op jit(solution)/shard_map/ppermute | solution.py:195
  14.9 1.5 %collective-permute-start.6 = (f32[328,128]{1,0:T(8,128)S(1)}, f32[328,128]{1,0:T(8,128)S(1)}, u32[]{:S(2)}, u32[]{:S(2)}) collective-permute-start(f32[328,128]{1,0:T(8,128)S(1)} %get-tuple-element.17.refs_0_), channel_id=1, source_target_pairs={{0,1},{1,0},{2,3},{3,2},{4,5},{5,4},{6,7},{7,6},{8,9},{9,8},{10,11... | collective-permute-start | bytes 503816 | tf_op jit(solution)/shard_map/ppermute | solution.py:81
  15.0 1.6 %collective-permute-start.7 = (f32[328,128]{1,0:T(8,128)S(1)}, f32[328,128]{1,0:T(8,128)S(1)}, u32[]{:S(2)}, u32[]{:S(2)}) collective-permute-start(f32[328,128]{1,0:T(8,128)S(1)} %get-tuple-element.18.refs_1_), channel_id=1, source_target_pairs={{0,1},{1,0},{2,3},{3,2},{4,5},{5,4},{6,7},{7,6},{8,9},{9,8},{10,11... | collective-permute-start | bytes 503816 | tf_op jit(solution)/shard_map/ppermute | solution.py:81
  15.5 1.4 %collective-permute-start.8 = (f32[328,128]{1,0:T(8,128)S(1)}, f32[328,128]{1,0:T(8,128)S(1)}, u32[]{:S(2)}, u32[]{:S(2)}) collective-permute-start(f32[328,128]{1,0:T(8,128)S(1)} %get-tuple-element.19.refs_2_), channel_id=1, source_target_pairs={{0,1},{1,0},{2,3},{3,2},{4,5},{5,4},{6,7},{7,6},{8,9},{9,8},{10,11... | collective-permute-start | bytes 503816 | tf_op jit(solution)/shard_map/ppermute | solution.py:81
  15.5 1.6 %collective-permute-start.9 = (f32[328,128]{1,0:T(8,128)S(1)}, f32[328,128]{1,0:T(8,128)S(1)}, u32[]{:S(2)}, u32[]{:S(2)}) collective-permute-start(f32[328,128]{1,0:T(8,128)S(1)} %get-tuple-element.20.refs_3_), channel_id=1, source_target_pairs={{0,1},{1,0},{2,3},{3,2},{4,5},{5,4},{6,7},{7,6},{8,9},{9,8},{10,11... | collective-permute-start | bytes 503816 | tf_op jit(solution)/shard_map/ppermute | solution.py:81
  16.0 1.4 %collective-permute-start.10 = (bf16[128,512]{1,0:T(8,128)(2,1)S(1)}, bf16[128,512]{1,0:T(8,128)(2,1)S(1)}, u32[]{:S(2)}, u32[]{:S(2)}) collective-permute-start(bf16[128,512]{1,0:T(8,128)(2,1)S(1)} %last.1.refs_5_), channel_id=1, source_target_pairs={{0,1},{1,0},{2,3},{3,2},{4,5},{5,4},{6,7},{7,6},{8,9},{9,8},{10,11... | collective-permute-start | bytes 393224 | tf_op jit(solution)/shard_map/ppermute | solution.py:81
  17.5 4.8 %collective-permute-start.13 = (f32[1,512]{1,0:T(1,128)S(1)}, f32[1,512]{1,0:T(1,128)S(1)}, u32[]{:S(2)}, u32[]{:S(2)}) collective-permute-start(f32[1,512]{1,0:T(1,128)S(1)} %sums.1), channel_id=1, source_target_pairs={{1,24},{9,16},{17,8},{25,0},{0,1},{8,9},{16,17},{24,25},{3,26},{11... | collective-permute-start | bytes 6152 | tf_op jit(solution)/shard_map/ppermute | solution.py:234
  18.0 4.3 %collective-permute-start.12 = (f32[1,512]{1,0:T(1,128)S(1)}, f32[1,512]{1,0:T(1,128)S(1)}, u32[]{:S(2)}, u32[]{:S(2)}) collective-permute-start(f32[1,512]{1,0:T(1,128)S(1)} %sums.1), channel_id=1, source_target_pairs={{1,16},{9,24},{17,0},{25,8},{0,1},{8,9},{16,17},{24,25},{3,18},{11... | collective-permute-start | bytes 6152 | tf_op jit(solution)/shard_map/ppermute | solution.py:234
  19.4 3.0 %collective-permute-start.11 = (f32[1,512]{1,0:T(1,128)S(1)}, f32[1,512]{1,0:T(1,128)S(1)}, u32[]{:S(2)}, u32[]{:S(2)}) collective-permute-start(f32[1,512]{1,0:T(1,128)S(1)} %sums.1), channel_id=1, source_target_pairs={{1,8},{9,0},{17,24},{25,16},{0,1},{8,9},{16,17},{24,25},{3,10},{11... | collective-permute-start | bytes 6152 | tf_op jit(solution)/shard_map/ppermute | solution.py:234
  22.4 1.2 %collective-permute-start.14 = (f32[1,256]{1,0:T(1,128)S(1)}, f32[1,256]{1,0:T(1,128)S(1)}, u32[]{:S(2)}, u32[]{:S(2)}) collective-permute-start(f32[1,256]{1,0:T(1,128)S(1)} %slice.9), channel_id=1, source_target_pairs={{0,1},{1,0},{2,3},{3,2},{4,5},{5,4},{6,7},{7,6},{8,9},{9,8},{10,11... | collective-permute-start | bytes 3080 | tf_op jit(solution)/shard_map/ppermute | solution.py:81

commit v7 on v6

--- a/solution.py
+++ b/solution.py
@@ -29,15 +29,15 @@
 
 
 def tiles_kernel(*refs):
-    operands, (right, left), held, arrived = refs[:4], refs[4:6], refs[6:10], refs[10]
+    operands, (right, left, prune), held, arrived = refs[:5], refs[5:8], refs[8:12], refs[12]
     copies = []
-    for n in range(4):
-        parts = 1 if n % 2 == 0 else 4
+    for n, target in enumerate(held + (prune,)):
+        parts = 4 if n in (1, 3) else 1
         tall = operands[n].shape[0] // parts
         for part in range(parts):
             at = pl.ds(part * tall, tall)
             copy = pltpu.make_async_copy(
-                operands[n].at[at], held[n].at[at], arrived.at[len(copies)]
+                operands[n].at[at], target.at[at], arrived.at[len(copies)]
             )
             copy.start()
             copies.append(copy)
@@ -50,15 +50,15 @@
 
 
 def tiles(*operands):
-    held = [pltpu.VMEM(value.shape, value.dtype) for value in operands]
+    held = [pltpu.VMEM(value.shape, value.dtype) for value in operands[:4]]
     return pl.pallas_call(
         tiles_kernel,
         out_shape=[
-            jax.ShapeDtypeStruct(operands[n].shape, operands[n].dtype) for n in (1, 3)
+            jax.ShapeDtypeStruct(operands[n].shape, operands[n].dtype) for n in (1, 3, 4)
         ],
-        in_specs=[pl.BlockSpec(memory_space=pltpu.HBM)] * 4,
-        out_specs=[VMEM, VMEM],
-        scratch_shapes=held + [pltpu.SemaphoreType.DMA((10,))],
+        in_specs=[pl.BlockSpec(memory_space=pltpu.HBM)] * 5,
+        out_specs=[VMEM, VMEM, VMEM],
+        scratch_shapes=held + [pltpu.SemaphoreType.DMA((11,))],
         compiler_params=room,
         name="tiles",
     )(*(pltpu.with_memory_space_constraint(value, pltpu.HBM) for value in operands))
@@ -86,9 +86,17 @@
     out[1] = beside[...]
 
 
-def early_kernel(near, far, right, first, second, inner, mask, *refs):
-    outs, left, handed, held = refs[:-3], refs[-3], refs[-2], refs[-1]
-    handed[...] = inner[...]
+def stack_kernel(*refs):
+    for n, block in enumerate(refs[:-1]):
+        refs[-1][n] = block[...]
+
+
+def hand_kernel(block, after, out):
+    out[...] = block[...]
+
+
+def early_kernel(near, far, rights, after, mask, *refs):
+    outs, left, held = refs[:-2], refs[-2], refs[-1]
     held[0:2] = near[...]
     held[2:4] = far[...]
     row, col = lax.axis_index("row"), lax.axis_index("col")
@@ -97,14 +105,14 @@
     (rows, depth), broad = left.shape, outs[0].shape[1]
     tall, wide = mask.shape
     share = rows // len(outs)
+    lefts = [held[here ^ col] for here in (row, block, block ^ 3)]
+    total = jnp.dot(
+        jnp.concatenate(lefts, axis=1),
+        rights[...].reshape(3 * depth, -1),
+        preferred_element_type=jnp.float32,
+    )
     for n, out in enumerate(outs):
-        columns = slice(n * broad, (n + 1) * broad)
-        total = jnp.zeros((rows, broad), jnp.float32)
-        for here, values in ((row, right), (block, first), (block ^ 3, second)):
-            total += jnp.dot(
-                held[here ^ col], values[:, columns], preferred_element_type=jnp.float32
-            )
-        out[0:rows, :] = total
+        out[0:rows, :] = total[:, n * broad : (n + 1) * broad]
         for i in range(tall):
             kept = entry(mask, i, n % wide).astype(jnp.float32)
             out[rows + i : rows + i + 1, :] = jnp.broadcast_to(kept, (1, broad))
@@ -177,15 +185,53 @@
         inflate(1, (1,), sizes, ours, theirs, out, None)
 
 
+def scale_kernel(turn, total_rows, inflated, sums, *refs):
+    out, scaled, sent = refs[-3:]
+    rows = inflated.shape[0]
+    parts = sent.shape[0]
+
+    @pl.when(lax.axis_index("layer") == turn)
+    def _():
+        scale = total_rows / (sums[...] + epsilon)
+        copies = []
+        for part in range(parts):
+            at = pl.ds(part * (rows // parts), rows // parts)
+            scaled[at, :] = inflated[at, :] * scale
+            copies.append(pltpu.make_async_copy(scaled.at[at], out.at[at], sent.at[part]))
+            copies[-1].start()
+        for copy in copies:
+            copy.wait()
+
+
+def scaled_on(turn, total_rows, inflated, sums, before=()):
+    hbm = pl.BlockSpec(memory_space=pltpu.HBM)
+    size = inflated.size
+    return pl.pallas_call(
+        functools.partial(scale_kernel, turn, total_rows),
+        out_shape=jax.ShapeDtypeStruct(inflated.shape, inflated.dtype),
+        in_specs=[VMEM, VMEM] + [hbm] * len(before),
+        out_specs=hbm,
+        scratch_shapes=[
+            pltpu.VMEM(inflated.shape, inflated.dtype),
+            pltpu.SemaphoreType.DMA((2,)),
+        ],
+        input_output_aliases={2: 0} if before else {},
+        cost_estimate=pl.CostEstimate(flops=size, bytes_accessed=8 * size, transcendentals=0),
+        compiler_params=room,
+        name=f"scale_{turn}",
+    )(inflated, sums, *before)
+
+
 def on_device(left_blocks, batch_blocks, left_mask, batch_mask, prune_mask):
     f32 = jnp.float32
     rows, columns = left_blocks.shape[0], batch_blocks.shape[2]
     half = columns // 2
-    right, left = tiles(
+    right, left, prune_mask = tiles(
         batch_mask[0],
         batch_blocks[0],
         jnp.transpose(left_mask, (1, 2, 0))[0],
         left_blocks[:, 0, :],
+        prune_mask,
     )
     count = lax.axis_size("row")
     first = lax.ppermute(right, "row", [(0, 2), (3, 1), (1, 0), (2, 3)])
@@ -202,24 +248,26 @@
     parts = 2 * wide
     share = rows // parts
     part = jax.ShapeDtypeStruct((rows + (tall + 7) // 8 * 8 + share, columns // parts), f32)
+    block = jax.ShapeDtypeStruct(right.shape, right.dtype)
+    rights = jax.ShapeDtypeStruct((3,) + right.shape, right.dtype)
+    rights = call(stack_kernel, "rights", rights, right, first, second)
+    handed = call(hand_kernel, "inner", block, inner, rights)
     ours = call(
         early_kernel,
         "early",
-        [part] * parts + [jax.ShapeDtypeStruct(v.shape, v.dtype) for v in (left, right)],
+        [part] * parts + [jax.ShapeDtypeStruct(left.shape, left.dtype)],
         pair,
         swapped(pair, "col", 2),
-        right,
-        first,
-        second,
-        inner,
+        rights,
+        handed,
         prune_mask,
         scratch=[pltpu.VMEM((4,) + left.shape, left.dtype)],
     )
     last = call(
-        last_kernel, "last", jax.ShapeDtypeStruct(right.shape, right.dtype), ours[-1], outer
-    )
-    operands = list(ours[:-1]) + [last]
-    operands += [swapped(value, "layer", 1) for value in ours[:-2]]
+        last_kernel, "last", block, handed, outer
+    )
+    operands = list(ours) + [last]
+    operands += [swapped(value, "layer", 1) for value in ours[:-1]]
     operands.append(swapped(last, "layer", 1))
     sizes = (rows, half, tall, wide)
     line = jax.ShapeDtypeStruct((1, columns), f32)
@@ -232,10 +280,10 @@
         pairs = [(2 * z + 1, 2 * (z ^ step)) for z in range(count)]
         pairs += [(2 * z, 2 * z + 1) for z in range(count)]
         total = total + lax.ppermute(sums, ("row", "layer"), pairs)
-    low = lax.axis_index("layer") == 0
-    sums = jnp.where(low, total[:, :half], swapped(total[:, half:], "layer", 1))
     total_rows = rows * count
-    return inflated * (total_rows / (sums + epsilon))
+    scaled = scaled_on(0, total_rows, inflated, total[:, :half])
+    total_high = swapped(total[:, half:], "layer", 1)
+    return scaled_on(1, total_rows, inflated, total_high, (scaled,))
 
 
 def widen(mask, tile_size, dtype):

time: 24.6 us -> 24.3 us (0.988)
  the two profiles are of different devices: /device:TPU:0 before, /device:TPU:1 now
where the time goes in v7:
time: 24.3 us; the launch traced here: 24.1 us
  starting transfers between devices  16 us (66%)
  waiting for transfers between devices  5.27 us (22%)
  Pallas kernels  2.74 us (11%)
    ppermute x8, starting transfers between devices, swapped(): return lax.ppermute(value, axis, [(i, i ^ step) for i in range(count)])  8.22 us
    ppermute x8, waiting for transfers between devices, swapped(): return lax.ppermute(value, axis, [(i, i ^ step) for i in range(count)])  3.46 us
    ppermute x1, starting transfers between devices, on_device(): first = lax.ppermute(right, 'row', [(0, 2), (3, 1), (1, 0), (2, 3)])  3.19 us
    ppermute x3, starting transfers between devices, on_device(): total = total + lax.ppermute(sums, ('row', 'layer'), pairs)  2.69 us
    ppermute x1, starting transfers between devices, on_device(): inner = lax.ppermute(right, ('row', 'layer'), pairs)  1.24 us
    pallas_call x1, Pallas kernels, tiles(): pl.pallas_call(tiles_kernel, out_shape=[jax.ShapeDtypeStruct(operands[n]....  1.1 us
    ppermute x1, waiting for transfers between devices, on_device(): second = lax.ppermute(right, 'row', [(0, 1), (3, 2), (1, 3), (2, 0)])  1.04 us
    pallas_call x7, Pallas kernels, call(): pl.pallas_call(kernel, out_shape=shapes, in_specs=[VMEM] * len(operands),...  0.89 us
  transfers between devices with their start and end apart: 15, of which 10 were waited for; matrix products, arithmetic and copies ran while one was open for 0% of the time, Pallas kernels for 2%

profile of v7, /device:TPU:1, one launch (start us, length us, event | category | flops | bytes accessed | tf_op | source)
XLA Modules:
  0.0 24.1 jit_solution(8179183602493531826)
XLA Ops:
  0.0 1.1 %tiles.1 = (bf16[128,512]{1,0:T(8,128)(2,1)S(1)}, bf16[256,128]{1,0:T(8,128)(2,1)S(1)}, s32[2,2]{1,0:T(2,128)S(1)}) custom-call(s32[1,4]{1,0:T(1,128)} %bitcast.6, bf16[128,512]{1,0:T(8,128)(2,1)} %bitcast.4, s32[1,2]{1,0:T(1,128)} %bitcast.7, bf16[256,128]{1,0:T(8,128)(2,1)} %bitcast.5, s32[2,2]{1,0:T(2,128)} %refs_4_.1), custom_call_target="tpu_custom_call" | custom-call | tf_op jit(solution)/shard_map/tiles/pallas_call | solution.py:54
  1.1 3.2 %collective-permute-start.2 = (bf16[128,512]{1,0:T(8,128)(2,1)S(1)}, bf16[128,512]{1,0:T(8,128)(2,1)S(1)}, u32[]{:S(2)}, u32[]{:S(2)}) collective-permute-start(bf16[128,512]{1,0:T(8,128)(2,1)S(1)} %get-tuple-element.16.refs_0_), channel_id=1, source_target_pairs={{0,16},{24,8},{8,0},{16,24},{1,17},{25,9},{9,1},{17,25},{2,18},{26... | collective-permute-start | bytes 393224 | tf_op jit(solution)/shard_map/ppermute | solution.py:237
  4.3 1.2 %collective-permute-start = (bf16[256,128]{1,0:T(8,128)(2,1)S(1)}, bf16[256,128]{1,0:T(8,128)(2,1)S(1)}, u32[]{:S(2)}, u32[]{:S(2)}) collective-permute-start(bf16[256,128]{1,0:T(8,128)(2,1)S(1)} %get-tuple-element.15.here), channel_id=1, source_target_pairs={{0,2},{2,0},{4,6},{6,4},{1,3},{3,1},{5,7},{7,5},{8,10},{10,8},{12,... | collective-permute-start | bytes 196616 | tf_op jit(solution)/shard_map/ppermute | solution.py:81
  5.5 1.2 %collective-permute-start.4 = (bf16[128,512]{1,0:T(8,128)(2,1)S(1)}, bf16[128,512]{1,0:T(8,128)(2,1)S(1)}, u32[]{:S(2)}, u32[]{:S(2)}) collective-permute-start(bf16[128,512]{1,0:T(8,128)(2,1)S(1)} %get-tuple-element.16.refs_0_), channel_id=1, source_target_pairs={{8,16},{9,17},{16,8},{17,9},{0,1},{1,0},{24,25},{25,24},{10,18},{1... | collective-permute-start | bytes 393224 | tf_op jit(solution)/shard_map/ppermute | solution.py:240
  6.8 0.7 %collective-permute-done.beside = bf16[256,128]{1,0:T(8,128)(2,1)S(1)} collective-permute-done((bf16[256,128]{1,0:T(8,128)(2,1)S(1)}, bf16[256,128]{1,0:T(8,128)(2,1)S(1)}, u32[]{:S(2)}, u32[]{:S(2)}) %collective-permute-start) | collective-permute-done | bytes 65568 | tf_op jit(solution)/shard_map/ppermute | solution.py:81
  7.4 1.4 %collective-permute-start.1 = (bf16[2,256,128]{2,1,0:T(8,128)(2,1)S(1)}, bf16[2,256,128]{2,1,0:T(8,128)(2,1)S(1)}, u32[]{:S(2)}, u32[]{:S(2)}) collective-permute-start(bf16[2,256,128]{2,1,0:T(8,128)(2,1)S(1)} %pair.1.near), channel_id=1, source_target_pairs={{0,4},{2,6},{4,0},{6,2},{1,5},{3,7},{5,1},{7,3},{8,12},{10,14},{12... | collective-permute-start | bytes 393224 | tf_op jit(solution)/shard_map/ppermute | solution.py:81
  8.8 0.7 %collective-permute-start.5 = (bf16[128,512]{1,0:T(8,128)(2,1)S(1)}, bf16[128,512]{1,0:T(8,128)(2,1)S(1)}, u32[]{:S(2)}, u32[]{:S(2)}) collective-permute-start(bf16[128,512]{1,0:T(8,128)(2,1)S(1)} %collective-permute-done.2.refs_1_), channel_id=1, source_target_pairs={{0,8},{8,0},{16,24},{24,16},{1,9},{9,1},{17,25},{25,17},{2,10},{10... | collective-permute-start | bytes 393224 | tf_op jit(solution)/shard_map/ppermute | solution.py:241
  9.5 1.0 %collective-permute-done.3.refs_2_ = bf16[128,512]{1,0:T(8,128)(2,1)S(1)} collective-permute-done((bf16[128,512]{1,0:T(8,128)(2,1)S(1)}, bf16[128,512]{1,0:T(8,128)(2,1)S(1)}, u32[]{:S(2)}, u32[]{:S(2)}) %collective-permute-start.3) | collective-permute-done | bytes 131104 | tf_op jit(solution)/shard_map/ppermute | solution.py:238
  10.6 1.0 %collective-permute-done.1.far = bf16[2,256,128]{2,1,0:T(8,128)(2,1)S(1)} collective-permute-done((bf16[2,256,128]{2,1,0:T(8,128)(2,1)S(1)}, bf16[2,256,128]{2,1,0:T(8,128)(2,1)S(1)}, u32[]{:S(2)}, u32[]{:S(2)}) %collective-permute-start.1) | collective-permute-done | bytes 131104 | tf_op jit(solution)/shard_map/ppermute | solution.py:81
  11.6 0.3 %early.1 = (f32[328,128]{1,0:T(8,128)S(1)}, f32[328,128]{1,0:T(8,128)S(1)}, f32[328,128]{1,0:T(8,128)S(1)}, f32[328,128]{1,0:T(8,128)S(1)}, bf16[256,128]{1,0:T(8,128)(2,1)S(1)}) custom-call(bf16[2,256,128]{2,1,0:T(8,128)(2,1)S(1)} %pair.1.near, bf16[2,256,128]{2,1,0:T(8,128)(2,1)S(1)} %collective-permute-done.1.far, bf16[3,128,512]{2,1,0:T(8,128)(2,1)S(1)} %rights.1.after, ...), custom_call_target="tpu_custom_call" | custom-call | tf_op jit(solution)/shard_map/early/pallas_call | solution.py:68
  11.9 3.0 %collective-permute-start.6 = (f32[328,128]{1,0:T(8,128)S(1)}, f32[328,128]{1,0:T(8,128)S(1)}, u32[]{:S(2)}, u32[]{:S(2)}) collective-permute-start(f32[328,128]{1,0:T(8,128)S(1)} %get-tuple-element.18.refs_0_), channel_id=1, source_target_pairs={{0,1},{1,0},{2,3},{3,2},{4,5},{5,4},{6,7},{7,6},{8,9},{9,8},{10,11... | collective-permute-start | bytes 503816 | tf_op jit(solution)/shard_map/ppermute | solution.py:81
  15.0 0.4 %collective-permute-start.8 = (f32[328,128]{1,0:T(8,128)S(1)}, f32[328,128]{1,0:T(8,128)S(1)}, u32[]{:S(2)}, u32[]{:S(2)}) collective-permute-start(f32[328,128]{1,0:T(8,128)S(1)} %get-tuple-element.20.refs_2_), channel_id=1, source_target_pairs={{0,1},{1,0},{2,3},{3,2},{4,5},{5,4},{6,7},{7,6},{8,9},{9,8},{10,11... | collective-permute-start | bytes 503816 | tf_op jit(solution)/shard_map/ppermute | solution.py:81
  15.5 0.6 %collective-permute-start.10 = (bf16[128,512]{1,0:T(8,128)(2,1)S(1)}, bf16[128,512]{1,0:T(8,128)(2,1)S(1)}, u32[]{:S(2)}, u32[]{:S(2)}) collective-permute-start(bf16[128,512]{1,0:T(8,128)(2,1)S(1)} %last.1.refs_5_), channel_id=1, source_target_pairs={{0,1},{1,0},{2,3},{3,2},{4,5},{5,4},{6,7},{7,6},{8,9},{9,8},{10,11... | collective-permute-start | bytes 393224 | tf_op jit(solution)/shard_map/ppermute | solution.py:81
  16.3 0.2 collective-permute-done.8.refs_8_
  16.6 0.3 %collective-permute-done.9.refs_9_ = f32[328,128]{1,0:T(8,128)S(1)} collective-permute-done((f32[328,128]{1,0:T(8,128)S(1)}, f32[328,128]{1,0:T(8,128)S(1)}, u32[]{:S(2)}, u32[]{:S(2)}) %collective-permute-start.9) | collective-permute-done | bytes 167968 | tf_op jit(solution)/shard_map/ppermute | solution.py:81
  16.9 0.3 %collective-permute-done.10.refs_10_ = bf16[128,512]{1,0:T(8,128)(2,1)S(1)} collective-permute-done((bf16[128,512]{1,0:T(8,128)(2,1)S(1)}, bf16[128,512]{1,0:T(8,128)(2,1)S(1)}, u32[]{:S(2)}, u32[]{:S(2)}) %collective-permute-start.10) | collective-permute-done | bytes 131104 | tf_op jit(solution)/shard_map/ppermute | solution.py:81
  17.2 0.3 %sums.1 = f32[1,512]{1,0:T(1,128)S(1)} custom-call(f32[328,128]{1,0:T(8,128)S(1)} %get-tuple-element.18.refs_0_, f32[328,128]{1,0:T(8,128)S(1)} %get-tuple-element.19.refs_1_, f32[328,128]{1,0:T(8,128)S(1)} %get-tuple-element.20.refs_2_, f32[328,128]{1,0:T(8,128)S(1)} %get-tuple-element.21.refs_3_, bf16[256,128]{1,0:T(8,128)(2,1)S(1)} %get-tuple-element.22.refs_4_, ...), custom_call_target="tpu_custom_call" | custom-call | tf_op jit(solution)/shard_map/sums/pallas_call | solution.py:68
  17.5 1.5 %collective-permute-start.13 = (f32[1,512]{1,0:T(1,128)S(1)}, f32[1,512]{1,0:T(1,128)S(1)}, u32[]{:S(2)}, u32[]{:S(2)}) collective-permute-start(f32[1,512]{1,0:T(1,128)S(1)} %sums.1), channel_id=1, source_target_pairs={{1,24},{9,16},{17,8},{25,0},{0,1},{8,9},{16,17},{24,25},{3,26},{11... | collective-permute-start | bytes 6152 | tf_op jit(solution)/shard_map/ppermute | solution.py:282
  18.9 1.0 %collective-permute-start.12 = (f32[1,512]{1,0:T(1,128)S(1)}, f32[1,512]{1,0:T(1,128)S(1)}, u32[]{:S(2)}, u32[]{:S(2)}) collective-permute-start(f32[1,512]{1,0:T(1,128)S(1)} %sums.1), channel_id=1, source_target_pairs={{1,16},{9,24},{17,0},{25,8},{0,1},{8,9},{16,17},{24,25},{3,18},{11... | collective-permute-start | bytes 6152 | tf_op jit(solution)/shard_map/ppermute | solution.py:282
  20.4 0.3 %collective-permute-done.12 = f32[1,512]{1,0:T(1,128)S(1)} collective-permute-done((f32[1,512]{1,0:T(1,128)S(1)}, f32[1,512]{1,0:T(1,128)S(1)}, u32[]{:S(2)}, u32[]{:S(2)}) %collective-permute-start.12) | collective-permute-done | bytes 2080 | tf_op jit(solution)/shard_map/ppermute | solution.py:282
  20.7 0.4 %collective-permute-done.11 = f32[1,512]{1,0:T(1,128)S(1)} collective-permute-done((f32[1,512]{1,0:T(1,128)S(1)}, f32[1,512]{1,0:T(1,128)S(1)}, u32[]{:S(2)}, u32[]{:S(2)}) %collective-permute-start.11) | collective-permute-done | bytes 2080 | tf_op jit(solution)/shard_map/ppermute | solution.py:282
  21.2 1.4 %collective-permute-start.14 = (f32[1,256]{1,0:T(1,128)S(1)}, f32[1,256]{1,0:T(1,128)S(1)}, u32[]{:S(2)}, u32[]{:S(2)}) collective-permute-start(f32[1,256]{1,0:T(1,128)S(1)} %get-tuple-element.26), channel_id=1, source_target_pairs={{0,1},{1,0},{2,3},{3,2},{4,5},{5,4},{6,7},{7,6},{8,9},{9,8},{10,11... | collective-permute-start | bytes 3080 | tf_op jit(solution)/shard_map/ppermute | solution.py:81
  22.6 0.8 %collective-permute-done.14.sums = f32[1,256]{1,0:T(1,128)S(1)} collective-permute-done((f32[1,256]{1,0:T(1,128)S(1)}, f32[1,256]{1,0:T(1,128)S(1)}, u32[]{:S(2)}, u32[]{:S(2)}) %collective-permute-start.14) | collective-permute-done | bytes 1056 | tf_op jit(solution)/shard_map/ppermute | solution.py:81
  23.4 0.7 %scale_1.1 = f32[256,256]{1,0:T(8,128)} custom-call(f32[256,256]{1,0:T(8,128)S(1)} %get-tuple-element.23.inflated, f32[1,256]{1,0:T(1,128)S(1)} %collective-permute-done.14.sums, f32[256,256]{1,0:T(8,128)} %scale_0.1.refs_0_), custom_call_target="tpu_custom_call", output_to_operand_aliasing={{}: (2, {})} | custom-call | flops 65536 | bytes 524288 | tf_op jit(solution)/shard_map/scale_1/pallas_call | solution.py:209
  (18 shorter events, 0.8 us)
Async XLA Ops:
  1.1 7.7 %collective-permute-start.2 = (bf16[128,512]{1,0:T(8,128)(2,1)S(1)}, bf16[128,512]{1,0:T(8,128)(2,1)S(1)}, u32[]{:S(2)}, u32[]{:S(2)}) collective-permute-start(bf16[128,512]{1,0:T(8,128)(2,1)S(1)} %get-tuple-element.16.refs_0_), channel_id=1, source_target_pairs={{0,16},{24,8},{8,0},{16,24},{1,17},{25,9},{9,1},{17,25},{2,18},{26... | collective-permute-start | bytes 393224 | tf_op jit(solution)/shard_map/ppermute | solution.py:237
  4.3 3.1 %collective-permute-start = (bf16[256,128]{1,0:T(8,128)(2,1)S(1)}, bf16[256,128]{1,0:T(8,128)(2,1)S(1)}, u32[]{:S(2)}, u32[]{:S(2)}) collective-permute-start(bf16[256,128]{1,0:T(8,128)(2,1)S(1)} %get-tuple-element.15.here), channel_id=1, source_target_pairs={{0,2},{2,0},{4,6},{6,4},{1,3},{3,1},{5,7},{7,5},{8,10},{10,8},{12,... | collective-permute-start | bytes 196616 | tf_op jit(solution)/shard_map/ppermute | solution.py:81
  5.5 5.0 %collective-permute-start.3 = (bf16[128,512]{1,0:T(8,128)(2,1)S(1)}, bf16[128,512]{1,0:T(8,128)(2,1)S(1)}, u32[]{:S(2)}, u32[]{:S(2)}) collective-permute-start(bf16[128,512]{1,0:T(8,128)(2,1)S(1)} %get-tuple-element.16.refs_0_), channel_id=1, source_target_pairs={{0,8},{24,16},{8,24},{16,0},{1,9},{25,17},{9,25},{17,1},{2,10},{26... | collective-permute-start | bytes 393224 | tf_op jit(solution)/shard_map/ppermute | solution.py:238
  5.5 5.0 %collective-permute-start.4 = (bf16[128,512]{1,0:T(8,128)(2,1)S(1)}, bf16[128,512]{1,0:T(8,128)(2,1)S(1)}, u32[]{:S(2)}, u32[]{:S(2)}) collective-permute-start(bf16[128,512]{1,0:T(8,128)(2,1)S(1)} %get-tuple-element.16.refs_0_), channel_id=1, source_target_pairs={{8,16},{9,17},{16,8},{17,9},{0,1},{1,0},{24,25},{25,24},{10,18},{1... | collective-permute-start | bytes 393224 | tf_op jit(solution)/shard_map/ppermute | solution.py:240
  7.4 4.2 %collective-permute-start.1 = (bf16[2,256,128]{2,1,0:T(8,128)(2,1)S(1)}, bf16[2,256,128]{2,1,0:T(8,128)(2,1)S(1)}, u32[]{:S(2)}, u32[]{:S(2)}) collective-permute-start(bf16[2,256,128]{2,1,0:T(8,128)(2,1)S(1)} %pair.1.near), channel_id=1, source_target_pairs={{0,4},{2,6},{4,0},{6,2},{1,5},{3,7},{5,1},{7,3},{8,12},{10,14},{12... | collective-permute-start | bytes 393224 | tf_op jit(solution)/shard_map/ppermute | solution.py:81
  8.8 6.7 %collective-permute-start.5 = (bf16[128,512]{1,0:T(8,128)(2,1)S(1)}, bf16[128,512]{1,0:T(8,128)(2,1)S(1)}, u32[]{:S(2)}, u32[]{:S(2)}) collective-permute-start(bf16[128,512]{1,0:T(8,128)(2,1)S(1)} %collective-permute-done.2.refs_1_), channel_id=1, source_target_pairs={{0,8},{8,0},{16,24},{24,16},{1,9},{9,1},{17,25},{25,17},{2,10},{10... | collective-permute-start | bytes 393224 | tf_op jit(solution)/shard_map/ppermute | solution.py:241
  11.9 4.3 %collective-permute-start.6 = (f32[328,128]{1,0:T(8,128)S(1)}, f32[328,128]{1,0:T(8,128)S(1)}, u32[]{:S(2)}, u32[]{:S(2)}) collective-permute-start(f32[328,128]{1,0:T(8,128)S(1)} %get-tuple-element.18.refs_0_), channel_id=1, source_target_pairs={{0,1},{1,0},{2,3},{3,2},{4,5},{5,4},{6,7},{7,6},{8,9},{9,8},{10,11... | collective-permute-start | bytes 503816 | tf_op jit(solution)/shard_map/ppermute | solution.py:81
  14.9 1.4 %collective-permute-start.7 = (f32[328,128]{1,0:T(8,128)S(1)}, f32[328,128]{1,0:T(8,128)S(1)}, u32[]{:S(2)}, u32[]{:S(2)}) collective-permute-start(f32[328,128]{1,0:T(8,128)S(1)} %get-tuple-element.19.refs_1_), channel_id=1, source_target_pairs={{0,1},{1,0},{2,3},{3,2},{4,5},{5,4},{6,7},{7,6},{8,9},{9,8},{10,11... | collective-permute-start | bytes 503816 | tf_op jit(solution)/shard_map/ppermute | solution.py:81
  15.0 1.6 %collective-permute-start.8 = (f32[328,128]{1,0:T(8,128)S(1)}, f32[328,128]{1,0:T(8,128)S(1)}, u32[]{:S(2)}, u32[]{:S(2)}) collective-permute-start(f32[328,128]{1,0:T(8,128)S(1)} %get-tuple-element.20.refs_2_), channel_id=1, source_target_pairs={{0,1},{1,0},{2,3},{3,2},{4,5},{5,4},{6,7},{7,6},{8,9},{9,8},{10,11... | collective-permute-start | bytes 503816 | tf_op jit(solution)/shard_map/ppermute | solution.py:81
  15.5 1.4 %collective-permute-start.9 = (f32[328,128]{1,0:T(8,128)S(1)}, f32[328,128]{1,0:T(8,128)S(1)}, u32[]{:S(2)}, u32[]{:S(2)}) collective-permute-start(f32[328,128]{1,0:T(8,128)S(1)} %get-tuple-element.21.refs_3_), channel_id=1, source_target_pairs={{0,1},{1,0},{2,3},{3,2},{4,5},{5,4},{6,7},{7,6},{8,9},{9,8},{10,11... | collective-permute-start | bytes 503816 | tf_op jit(solution)/shard_map/ppermute | solution.py:81
  15.5 1.6 %collective-permute-start.10 = (bf16[128,512]{1,0:T(8,128)(2,1)S(1)}, bf16[128,512]{1,0:T(8,128)(2,1)S(1)}, u32[]{:S(2)}, u32[]{:S(2)}) collective-permute-start(bf16[128,512]{1,0:T(8,128)(2,1)S(1)} %last.1.refs_5_), channel_id=1, source_target_pairs={{0,1},{1,0},{2,3},{3,2},{4,5},{5,4},{6,7},{7,6},{8,9},{9,8},{10,11... | collective-permute-start | bytes 393224 | tf_op jit(solution)/shard_map/ppermute | solution.py:81
  17.5 2.9 %collective-permute-start.13 = (f32[1,512]{1,0:T(1,128)S(1)}, f32[1,512]{1,0:T(1,128)S(1)}, u32[]{:S(2)}, u32[]{:S(2)}) collective-permute-start(f32[1,512]{1,0:T(1,128)S(1)} %sums.1), channel_id=1, source_target_pairs={{1,24},{9,16},{17,8},{25,0},{0,1},{8,9},{16,17},{24,25},{3,26},{11... | collective-permute-start | bytes 6152 | tf_op jit(solution)/shard_map/ppermute | solution.py:282
  18.9 1.8 %collective-permute-start.12 = (f32[1,512]{1,0:T(1,128)S(1)}, f32[1,512]{1,0:T(1,128)S(1)}, u32[]{:S(2)}, u32[]{:S(2)}) collective-permute-start(f32[1,512]{1,0:T(1,128)S(1)} %sums.1), channel_id=1, source_target_pairs={{1,16},{9,24},{17,0},{25,8},{0,1},{8,9},{16,17},{24,25},{3,18},{11... | collective-permute-start | bytes 6152 | tf_op jit(solution)/shard_map/ppermute | solution.py:282
  20.0 1.2 %collective-permute-start.11 = (f32[1,512]{1,0:T(1,128)S(1)}, f32[1,512]{1,0:T(1,128)S(1)}, u32[]{:S(2)}, u32[]{:S(2)}) collective-permute-start(f32[1,512]{1,0:T(1,128)S(1)} %sums.1), channel_id=1, source_target_pairs={{1,8},{9,0},{17,24},{25,16},{0,1},{8,9},{16,17},{24,25},{3,10},{11... | collective-permute-start | bytes 6152 | tf_op jit(solution)/shard_map/ppermute | solution.py:282
  21.2 2.2 %collective-permute-start.14 = (f32[1,256]{1,0:T(1,128)S(1)}, f32[1,256]{1,0:T(1,128)S(1)}, u32[]{:S(2)}, u32[]{:S(2)}) collective-permute-start(f32[1,256]{1,0:T(1,128)S(1)} %get-tuple-element.26), channel_id=1, source_target_pairs={{0,1},{1,0},{2,3},{3,2},{4,5},{5,4},{6,7},{7,6},{8,9},{9,8},{10,11... | collective-permute-start | bytes 3080 | tf_op jit(solution)/shard_map/ppermute | solution.py:81

commit v8 on v7

--- a/solution.py
+++ b/solution.py
@@ -113,6 +113,9 @@
     )
     for n, out in enumerate(outs):
         out[0:rows, :] = total[:, n * broad : (n + 1) * broad]
+        out[rows : out.shape[0] - share, :] = jnp.zeros_like(
+            out[rows : out.shape[0] - share, :]
+        )
         for i in range(tall):
             kept = entry(mask, i, n % wide).astype(jnp.float32)
             out[rows + i : rows + i + 1, :] = jnp.broadcast_to(kept, (1, broad))
@@ -133,93 +136,62 @@
         out[...] = outer[...]
 
 
-def inflate(own, sides, sizes, ours, theirs, out, sums):
+def join_kernel(sizes, *refs):
     rows, half, tall, wide = sizes
-    high, broad = rows // tall, half // wide
-    share = rows // (2 * wide)
-    here = ours[-2][...]
-    there = jnp.concatenate([part[part.shape[0] - share :, :] for part in theirs[:-1]], axis=0)
-    left = jnp.concatenate([here, there.astype(here.dtype)], axis=1)
-    for n in range(2 * wide):
-        if n // wide not in sides:
-            continue
+    count = 2 * wide
+    ours, left, theirs = refs[:count], refs[count], refs[count + 1 : -3]
+    total, kept, lefts = refs[-3:]
+    broad = half // wide
+    share = rows // count
+    depth = left.shape[1]
+    layer = lax.axis_index("layer")
+    lefts[:, 0:depth] = left[...]
+    for n in range(count):
         columns = slice(n * broad, (n + 1) * broad)
-        right = jnp.concatenate([ours[-1][:, columns], theirs[-1][:, columns]], axis=0)
-        product = ours[n][0:rows, :] + theirs[n][0:rows, :]
-        product += jnp.dot(left, right, preferred_element_type=jnp.float32)
-        total = jnp.zeros((1, broad), jnp.float32)
-        across = slice(n % wide * broad, (n % wide + 1) * broad)
-        for i in range(tall):
-            at = slice(i * high, (i + 1) * high)
-            kept = (ours if n // wide == own else theirs)[n][rows + i : rows + i + 1, :] != 0.0
-            kept = jnp.broadcast_to(kept, (high, broad))
-            value = jnp.where(kept, product[at, :] * product[at, :], 0.0)
-            if n // wide == own and out is not None:
-                out[at, across] = value
-            total += jnp.sum(value, axis=0, keepdims=True)
-        if sums is not None:
-            sums[:, columns] = total
+        total[:, columns] = ours[n][0:rows, :] + theirs[n][0:rows, :]
+        entries = slice(rows, rows + kept.shape[0])
+        own = layer == n // wide
+        kept[:, columns] = jnp.where(own, ours[n][entries, :], theirs[n][entries, :])
+        lefts[n * share : (n + 1) * share, depth:] = theirs[n][
+            theirs[n].shape[0] - share :, :
+        ].astype(left.dtype)
+
+
+def inflate(side, sizes, joined, out, sums):
+    rows, half, tall, wide = sizes
+    early, kept, lefts, here, there = joined
+    high = rows // tall
+    columns = slice(side * half, (side + 1) * half)
+    product = early[:, columns] + jnp.dot(
+        lefts[...],
+        jnp.concatenate([here[:, columns], there[:, columns]], axis=0),
+        preferred_element_type=jnp.float32,
+    )
+    total = jnp.zeros((1, half), jnp.float32)
+    for i in range(tall):
+        at = slice(i * high, (i + 1) * high)
+        keep = jnp.broadcast_to(kept[i : i + 1, columns] != 0.0, (high, half))
+        value = jnp.where(keep, product[at, :] * product[at, :], 0.0)
+        if out is not None:
+            out[at, :] = value
+        total += jnp.sum(value, axis=0, keepdims=True)
+    sums[...] = total
 
 
 def sums_kernel(sizes, *refs):
-    count = 2 * sizes[3]
-    ours, theirs, sums = refs[: count + 2], refs[count + 2 : -1], refs[-1]
-    sums[...] = jnp.zeros_like(sums)
-
-    @pl.when(lax.axis_index("layer") == 1)
-    def _():
-        inflate(1, (0, 1), sizes, ours, theirs, None, sums)
+    for core in range(2):
+
+        @pl.when(lax.axis_index("layer") == core)
+        def _():
+            inflate(1 - core, sizes, refs[:-1], None, refs[-1])
 
 
 def inflate_kernel(sizes, *refs):
-    count = 2 * sizes[3]
-    ours, theirs, out, sums = refs[: count + 2], refs[count + 2 : -2], refs[-2], refs[-1]
-    sums[...] = jnp.zeros_like(sums)
-
-    @pl.when(lax.axis_index("layer") == 0)
-    def _():
-        inflate(0, (0, 1), sizes, ours, theirs, out, sums)
-
-    @pl.when(lax.axis_index("layer") == 1)
-    def _():
-        inflate(1, (1,), sizes, ours, theirs, out, None)
-
-
-def scale_kernel(turn, total_rows, inflated, sums, *refs):
-    out, scaled, sent = refs[-3:]
-    rows = inflated.shape[0]
-    parts = sent.shape[0]
-
-    @pl.when(lax.axis_index("layer") == turn)
-    def _():
-        scale = total_rows / (sums[...] + epsilon)
-        copies = []
-        for part in range(parts):
-            at = pl.ds(part * (rows // parts), rows // parts)
-            scaled[at, :] = inflated[at, :] * scale
-            copies.append(pltpu.make_async_copy(scaled.at[at], out.at[at], sent.at[part]))
-            copies[-1].start()
-        for copy in copies:
-            copy.wait()
-
-
-def scaled_on(turn, total_rows, inflated, sums, before=()):
-    hbm = pl.BlockSpec(memory_space=pltpu.HBM)
-    size = inflated.size
-    return pl.pallas_call(
-        functools.partial(scale_kernel, turn, total_rows),
-        out_shape=jax.ShapeDtypeStruct(inflated.shape, inflated.dtype),
-        in_specs=[VMEM, VMEM] + [hbm] * len(before),
-        out_specs=hbm,
-        scratch_shapes=[
-            pltpu.VMEM(inflated.shape, inflated.dtype),
-            pltpu.SemaphoreType.DMA((2,)),
-        ],
-        input_output_aliases={2: 0} if before else {},
-        cost_estimate=pl.CostEstimate(flops=size, bytes_accessed=8 * size, transcendentals=0),
-        compiler_params=room,
-        name=f"scale_{turn}",
-    )(inflated, sums, *before)
+    for core in range(2):
+
+        @pl.when(lax.axis_index("layer") == core)
+        def _():
+            inflate(core, sizes, refs[:-2], refs[-2], refs[-1])
 
 
 def on_device(left_blocks, batch_blocks, left_mask, batch_mask, prune_mask):
@@ -266,24 +238,33 @@
     last = call(
         last_kernel, "last", block, handed, outer
     )
-    operands = list(ours) + [last]
-    operands += [swapped(value, "layer", 1) for value in ours[:-1]]
-    operands.append(swapped(last, "layer", 1))
     sizes = (rows, half, tall, wide)
-    line = jax.ShapeDtypeStruct((1, columns), f32)
+    operands = list(call(
+        functools.partial(join_kernel, sizes),
+        "join",
+        [
+            jax.ShapeDtypeStruct((rows, columns), f32),
+            jax.ShapeDtypeStruct(((tall + 7) // 8 * 8, columns), f32),
+            jax.ShapeDtypeStruct((rows, 2 * left.shape[1]), left.dtype),
+        ],
+        *ours,
+        *(swapped(value, "layer", 1) for value in ours[:-1]),
+    ))
+    operands += [last, swapped(last, "layer", 1)]
+    line = jax.ShapeDtypeStruct((1, half), f32)
     sums = call(functools.partial(sums_kernel, sizes), "sums", line, *operands)
     inflated, sums_here = call(
         functools.partial(inflate_kernel, sizes), "inflate", [piece, line], *operands
     )
     total = sums_here
     for step in (1, 2, 3):
-        pairs = [(2 * z + 1, 2 * (z ^ step)) for z in range(count)]
-        pairs += [(2 * z, 2 * z + 1) for z in range(count)]
+        pairs = [
+            (2 * z + core, 2 * (z ^ step) + 1 - core)
+            for z in range(count)
+            for core in range(2)
+        ]
         total = total + lax.ppermute(sums, ("row", "layer"), pairs)
-    total_rows = rows * count
-    scaled = scaled_on(0, total_rows, inflated, total[:, :half])
-    total_high = swapped(total[:, half:], "layer", 1)
-    return scaled_on(1, total_rows, inflated, total_high, (scaled,))
+    return inflated * (rows * count / (total + epsilon))
 
 
 def widen(mask, tile_size, dtype):

time: 24.3 us -> 24.2 us (level)
  the two profiles are of different devices: /device:TPU:1 before, /device:TPU:0 now
where the time goes in v8:
time: 24.2 us; the launch traced here: 24 us
  starting transfers between devices  13 us (54%)
  waiting for transfers between devices  8.23 us (34%)
  Pallas kernels  1.96 us (8%)
  other arithmetic  0.74 us (3%)
    ppermute x7, waiting for transfers between devices, swapped(): return lax.ppermute(value, axis, [(i, i ^ step) for i in range(count)])  4.37 us
    ppermute x7, starting transfers between devices, swapped(): return lax.ppermute(value, axis, [(i, i ^ step) for i in range(count)])  4.22 us
    ppermute x1, starting transfers between devices, on_device(): first = lax.ppermute(right, 'row', [(0, 2), (3, 1), (1, 0), (2, 3)])  4.09 us
    ppermute x3, starting transfers between devices, on_device(): total = total + lax.ppermute(sums, ('row', 'layer'), pairs)  3.93 us
    ppermute x1, waiting for transfers between devices, on_device(): second = lax.ppermute(right, 'row', [(0, 1), (3, 2), (1, 3), (2, 0)])  2.29 us
    ppermute x3, waiting for transfers between devices, on_device(): total = total + lax.ppermute(sums, ('row', 'layer'), pairs)  1.43 us
    pallas_call x1, Pallas kernels, tiles(): pl.pallas_call(tiles_kernel, out_shape=[jax.ShapeDtypeStruct(operands[n]....  1.1 us
    pallas_call x8, Pallas kernels, call(): pl.pallas_call(kernel, out_shape=shapes, in_specs=[VMEM] * len(operands),...  0.86 us
  transfers between devices with their start and end apart: 14, of which 11 were waited for; matrix products, arithmetic and copies ran while one was open for 0% of the time, Pallas kernels for 3%

profile of v8, /device:TPU:0, one launch (start us, length us, event | category | flops | bytes accessed | tf_op | source)
XLA Modules:
  0.0 24.0 jit_solution(10331150077859982900)
XLA Ops:
  0.0 1.1 %tiles.1 = (bf16[128,512]{1,0:T(8,128)(2,1)S(1)}, bf16[256,128]{1,0:T(8,128)(2,1)S(1)}, s32[2,2]{1,0:T(2,128)S(1)}) custom-call(s32[1,4]{1,0:T(1,128)} %bitcast.8, bf16[128,512]{1,0:T(8,128)(2,1)} %bitcast.5, s32[1,2]{1,0:T(1,128)} %bitcast.9, bf16[256,128]{1,0:T(8,128)(2,1)} %bitcast.6, s32[2,2]{1,0:T(2,128)} %refs_4_.1), custom_call_target="tpu_custom_call" | custom-call | tf_op jit(solution)/shard_map/tiles/pallas_call | solution.py:54
  1.1 4.1 %collective-permute-start.2 = (bf16[128,512]{1,0:T(8,128)(2,1)S(1)}, bf16[128,512]{1,0:T(8,128)(2,1)S(1)}, u32[]{:S(2)}, u32[]{:S(2)}) collective-permute-start(bf16[128,512]{1,0:T(8,128)(2,1)S(1)} %get-tuple-element.19.refs_0_), channel_id=1, source_target_pairs={{0,16},{24,8},{8,0},{16,24},{1,17},{25,9},{9,1},{17,25},{2,18},{26... | collective-permute-start | bytes 393224 | tf_op jit(solution)/shard_map/ppermute | solution.py:209
  5.2 1.5 %collective-permute-start = (bf16[256,128]{1,0:T(8,128)(2,1)S(1)}, bf16[256,128]{1,0:T(8,128)(2,1)S(1)}, u32[]{:S(2)}, u32[]{:S(2)}) collective-permute-start(bf16[256,128]{1,0:T(8,128)(2,1)S(1)} %get-tuple-element.18.here), channel_id=1, source_target_pairs={{0,2},{2,0},{4,6},{6,4},{1,3},{3,1},{5,7},{7,5},{8,10},{10,8},{12,... | collective-permute-start | bytes 196616 | tf_op jit(solution)/shard_map/ppermute | solution.py:81
  6.7 2.8 %collective-permute-done.beside = bf16[256,128]{1,0:T(8,128)(2,1)S(1)} collective-permute-done((bf16[256,128]{1,0:T(8,128)(2,1)S(1)}, bf16[256,128]{1,0:T(8,128)(2,1)S(1)}, u32[]{:S(2)}, u32[]{:S(2)}) %collective-permute-start) | collective-permute-done | bytes 65568 | tf_op jit(solution)/shard_map/ppermute | solution.py:81
  9.5 1.6 %collective-permute-start.1 = (bf16[2,256,128]{2,1,0:T(8,128)(2,1)S(1)}, bf16[2,256,128]{2,1,0:T(8,128)(2,1)S(1)}, u32[]{:S(2)}, u32[]{:S(2)}) collective-permute-start(bf16[2,256,128]{2,1,0:T(8,128)(2,1)S(1)} %pair.1.near), channel_id=1, source_target_pairs={{0,4},{2,6},{4,0},{6,2},{1,5},{3,7},{5,1},{7,3},{8,12},{10,14},{12... | collective-permute-start | bytes 393224 | tf_op jit(solution)/shard_map/ppermute | solution.py:81
  11.1 0.7 %collective-permute-start.9 = (bf16[128,512]{1,0:T(8,128)(2,1)S(1)}, bf16[128,512]{1,0:T(8,128)(2,1)S(1)}, u32[]{:S(2)}, u32[]{:S(2)}) collective-permute-start(bf16[128,512]{1,0:T(8,128)(2,1)S(1)} %collective-permute-done.2.refs_1_), channel_id=1, source_target_pairs={{0,8},{8,0},{16,24},{24,16},{1,9},{9,1},{17,25},{25,17},{2,10},{10... | collective-permute-start | bytes 393224 | tf_op jit(solution)/shard_map/ppermute | solution.py:213
  11.8 2.3 %collective-permute-done.3.refs_2_ = bf16[128,512]{1,0:T(8,128)(2,1)S(1)} collective-permute-done((bf16[128,512]{1,0:T(8,128)(2,1)S(1)}, bf16[128,512]{1,0:T(8,128)(2,1)S(1)}, u32[]{:S(2)}, u32[]{:S(2)}) %collective-permute-start.3) | collective-permute-done | bytes 131104 | tf_op jit(solution)/shard_map/ppermute | solution.py:210
  14.1 0.4 %collective-permute-done.1.far = bf16[2,256,128]{2,1,0:T(8,128)(2,1)S(1)} collective-permute-done((bf16[2,256,128]{2,1,0:T(8,128)(2,1)S(1)}, bf16[2,256,128]{2,1,0:T(8,128)(2,1)S(1)}, u32[]{:S(2)}, u32[]{:S(2)}) %collective-permute-start.1) | collective-permute-done | bytes 131104 | tf_op jit(solution)/shard_map/ppermute | solution.py:81
  14.5 0.3 %early.1 = (f32[328,128]{1,0:T(8,128)S(1)}, f32[328,128]{1,0:T(8,128)S(1)}, f32[328,128]{1,0:T(8,128)S(1)}, f32[328,128]{1,0:T(8,128)S(1)}, bf16[256,128]{1,0:T(8,128)(2,1)S(1)}) custom-call(bf16[2,256,128]{2,1,0:T(8,128)(2,1)S(1)} %pair.1.near, bf16[2,256,128]{2,1,0:T(8,128)(2,1)S(1)} %collective-permute-done.1.far, bf16[3,128,512]{2,1,0:T(8,128)(2,1)S(1)} %rights.1.after, ...), custom_call_target="tpu_custom_call" | custom-call | tf_op jit(solution)/shard_map/early/pallas_call | solution.py:68
  14.9 0.5 %collective-permute-start.6 = (f32[328,128]{1,0:T(8,128)S(1)}, f32[328,128]{1,0:T(8,128)S(1)}, u32[]{:S(2)}, u32[]{:S(2)}) collective-permute-start(f32[328,128]{1,0:T(8,128)S(1)} %get-tuple-element.22.refs_1_), channel_id=1, source_target_pairs={{0,1},{1,0},{2,3},{3,2},{4,5},{5,4},{6,7},{7,6},{8,9},{9,8},{10,11... | collective-permute-start | bytes 503816 | tf_op jit(solution)/shard_map/ppermute | solution.py:81
  15.5 0.4 %collective-permute-start.8 = (f32[328,128]{1,0:T(8,128)S(1)}, f32[328,128]{1,0:T(8,128)S(1)}, u32[]{:S(2)}, u32[]{:S(2)}) collective-permute-start(f32[328,128]{1,0:T(8,128)S(1)} %get-tuple-element.24.refs_3_), channel_id=1, source_target_pairs={{0,1},{1,0},{2,3},{3,2},{4,5},{5,4},{6,7},{7,6},{8,9},{9,8},{10,11... | collective-permute-start | bytes 503816 | tf_op jit(solution)/shard_map/ppermute | solution.py:81
  16.1 0.2 collective-permute-done.5.refs_5_
  16.3 0.2 collective-permute-done.6.refs_6_
  16.5 0.3 %collective-permute-done.7.refs_7_ = f32[328,128]{1,0:T(8,128)S(1)} collective-permute-done((f32[328,128]{1,0:T(8,128)S(1)}, f32[328,128]{1,0:T(8,128)S(1)}, u32[]{:S(2)}, u32[]{:S(2)}) %collective-permute-start.7) | collective-permute-done | bytes 167968 | tf_op jit(solution)/shard_map/ppermute | solution.py:81
  16.8 0.2 collective-permute-done.8.refs_8_
  17.1 0.3 %collective-permute-done.10.refs_4_ = bf16[128,512]{1,0:T(8,128)(2,1)S(1)} collective-permute-done((bf16[128,512]{1,0:T(8,128)(2,1)S(1)}, bf16[128,512]{1,0:T(8,128)(2,1)S(1)}, u32[]{:S(2)}, u32[]{:S(2)}) %collective-permute-start.10) | collective-permute-done | bytes 131104 | tf_op jit(solution)/shard_map/ppermute | solution.py:81
  17.5 0.2 sums.1
  17.7 1.6 %collective-permute-start.13 = (f32[1,256]{1,0:T(1,128)S(1)}, f32[1,256]{1,0:T(1,128)S(1)}, u32[]{:S(2)}, u32[]{:S(2)}) collective-permute-start(f32[1,256]{1,0:T(1,128)S(1)} %sums.1), channel_id=1, source_target_pairs={{0,25},{1,24},{8,17},{9,16},{16,9},{17,8},{24,1},{25,0},{2,27},{3,... | collective-permute-start | bytes 3080 | tf_op jit(solution)/shard_map/ppermute | solution.py:266
  19.3 1.0 %collective-permute-start.12 = (f32[1,256]{1,0:T(1,128)S(1)}, f32[1,256]{1,0:T(1,128)S(1)}, u32[]{:S(2)}, u32[]{:S(2)}) collective-permute-start(f32[1,256]{1,0:T(1,128)S(1)} %sums.1), channel_id=1, source_target_pairs={{0,17},{1,16},{8,25},{9,24},{16,1},{17,0},{24,9},{25,8},{2,19},{3,... | collective-permute-start | bytes 3080 | tf_op jit(solution)/shard_map/ppermute | solution.py:266
  20.3 1.3 %collective-permute-start.11 = (f32[1,256]{1,0:T(1,128)S(1)}, f32[1,256]{1,0:T(1,128)S(1)}, u32[]{:S(2)}, u32[]{:S(2)}) collective-permute-start(f32[1,256]{1,0:T(1,128)S(1)} %sums.1), channel_id=1, source_target_pairs={{0,9},{1,8},{8,1},{9,0},{16,25},{17,24},{24,17},{25,16},{2,11},{3,... | collective-permute-start | bytes 3080 | tf_op jit(solution)/shard_map/ppermute | solution.py:266
  21.6 0.2 inflate.1
  21.8 0.7 %collective-permute-done.13 = f32[1,256]{1,0:T(1,128)S(1)} collective-permute-done((f32[1,256]{1,0:T(1,128)S(1)}, f32[1,256]{1,0:T(1,128)S(1)}, u32[]{:S(2)}, u32[]{:S(2)}) %collective-permute-start.13) | collective-permute-done | bytes 1056 | tf_op jit(solution)/shard_map/ppermute | solution.py:266
  22.5 0.7 %collective-permute-done.12 = f32[1,256]{1,0:T(1,128)S(1)} collective-permute-done((f32[1,256]{1,0:T(1,128)S(1)}, f32[1,256]{1,0:T(1,128)S(1)}, u32[]{:S(2)}, u32[]{:S(2)}) %collective-permute-start.12) | collective-permute-done | bytes 1056 | tf_op jit(solution)/shard_map/ppermute | solution.py:266
  23.3 0.7 %broadcast_multiply_fusion = f32[256,256]{1,0:T(8,128)} fusion(f32[256,256]{1,0:T(8,128)S(1)} %get-tuple-element.29, f32[256]{0:T(256)S(1)} %bitcast.7), kind=kLoop, calls=%fused_computation | loop fusion | flops 65536 | bytes 525312 | tf_op jit(solution)/shard_map/mul | solution.py:267
  (15 shorter events, 0.6 us)
Async XLA Ops:
  1.1 10.0 %collective-permute-start.2 = (bf16[128,512]{1,0:T(8,128)(2,1)S(1)}, bf16[128,512]{1,0:T(8,128)(2,1)S(1)}, u32[]{:S(2)}, u32[]{:S(2)}) collective-permute-start(bf16[128,512]{1,0:T(8,128)(2,1)S(1)} %get-tuple-element.19.refs_0_), channel_id=1, source_target_pairs={{0,16},{24,8},{8,0},{16,24},{1,17},{25,9},{9,1},{17,25},{2,18},{26... | collective-permute-start | bytes 393224 | tf_op jit(solution)/shard_map/ppermute | solution.py:209
  5.2 4.3 %collective-permute-start = (bf16[256,128]{1,0:T(8,128)(2,1)S(1)}, bf16[256,128]{1,0:T(8,128)(2,1)S(1)}, u32[]{:S(2)}, u32[]{:S(2)}) collective-permute-start(bf16[256,128]{1,0:T(8,128)(2,1)S(1)} %get-tuple-element.18.here), channel_id=1, source_target_pairs={{0,2},{2,0},{4,6},{6,4},{1,3},{3,1},{5,7},{7,5},{8,10},{10,8},{12,... | collective-permute-start | bytes 196616 | tf_op jit(solution)/shard_map/ppermute | solution.py:81
  6.7 7.4 %collective-permute-start.3 = (bf16[128,512]{1,0:T(8,128)(2,1)S(1)}, bf16[128,512]{1,0:T(8,128)(2,1)S(1)}, u32[]{:S(2)}, u32[]{:S(2)}) collective-permute-start(bf16[128,512]{1,0:T(8,128)(2,1)S(1)} %get-tuple-element.19.refs_0_), channel_id=1, source_target_pairs={{0,8},{24,16},{8,24},{16,0},{1,9},{25,17},{9,25},{17,1},{2,10},{26... | collective-permute-start | bytes 393224 | tf_op jit(solution)/shard_map/ppermute | solution.py:210
  6.7 7.4 %collective-permute-start.4 = (bf16[128,512]{1,0:T(8,128)(2,1)S(1)}, bf16[128,512]{1,0:T(8,128)(2,1)S(1)}, u32[]{:S(2)}, u32[]{:S(2)}) collective-permute-start(bf16[128,512]{1,0:T(8,128)(2,1)S(1)} %get-tuple-element.19.refs_0_), channel_id=1, source_target_pairs={{8,16},{9,17},{16,8},{17,9},{0,1},{1,0},{24,25},{25,24},{10,18},{1... | collective-permute-start | bytes 393224 | tf_op jit(solution)/shard_map/ppermute | solution.py:212
  9.5 5.0 %collective-permute-start.1 = (bf16[2,256,128]{2,1,0:T(8,128)(2,1)S(1)}, bf16[2,256,128]{2,1,0:T(8,128)(2,1)S(1)}, u32[]{:S(2)}, u32[]{:S(2)}) collective-permute-start(bf16[2,256,128]{2,1,0:T(8,128)(2,1)S(1)} %pair.1.near), channel_id=1, source_target_pairs={{0,4},{2,6},{4,0},{6,2},{1,5},{3,7},{5,1},{7,3},{8,12},{10,14},{12... | collective-permute-start | bytes 393224 | tf_op jit(solution)/shard_map/ppermute | solution.py:81
  11.1 5.0 %collective-permute-start.9 = (bf16[128,512]{1,0:T(8,128)(2,1)S(1)}, bf16[128,512]{1,0:T(8,128)(2,1)S(1)}, u32[]{:S(2)}, u32[]{:S(2)}) collective-permute-start(bf16[128,512]{1,0:T(8,128)(2,1)S(1)} %collective-permute-done.2.refs_1_), channel_id=1, source_target_pairs={{0,8},{8,0},{16,24},{24,16},{1,9},{9,1},{17,25},{25,17},{2,10},{10... | collective-permute-start | bytes 393224 | tf_op jit(solution)/shard_map/ppermute | solution.py:213
  14.8 1.5 %collective-permute-start.5 = (f32[328,128]{1,0:T(8,128)S(1)}, f32[328,128]{1,0:T(8,128)S(1)}, u32[]{:S(2)}, u32[]{:S(2)}) collective-permute-start(f32[328,128]{1,0:T(8,128)S(1)} %get-tuple-element.21.refs_0_), channel_id=1, source_target_pairs={{0,1},{1,0},{2,3},{3,2},{4,5},{5,4},{6,7},{7,6},{8,9},{9,8},{10,11... | collective-permute-start | bytes 503816 | tf_op jit(solution)/shard_map/ppermute | solution.py:81
  14.9 1.6 %collective-permute-start.6 = (f32[328,128]{1,0:T(8,128)S(1)}, f32[328,128]{1,0:T(8,128)S(1)}, u32[]{:S(2)}, u32[]{:S(2)}) collective-permute-start(f32[328,128]{1,0:T(8,128)S(1)} %get-tuple-element.22.refs_1_), channel_id=1, source_target_pairs={{0,1},{1,0},{2,3},{3,2},{4,5},{5,4},{6,7},{7,6},{8,9},{9,8},{10,11... | collective-permute-start | bytes 503816 | tf_op jit(solution)/shard_map/ppermute | solution.py:81
  15.4 1.4 %collective-permute-start.7 = (f32[328,128]{1,0:T(8,128)S(1)}, f32[328,128]{1,0:T(8,128)S(1)}, u32[]{:S(2)}, u32[]{:S(2)}) collective-permute-start(f32[328,128]{1,0:T(8,128)S(1)} %get-tuple-element.23.refs_2_), channel_id=1, source_target_pairs={{0,1},{1,0},{2,3},{3,2},{4,5},{5,4},{6,7},{7,6},{8,9},{9,8},{10,11... | collective-permute-start | bytes 503816 | tf_op jit(solution)/shard_map/ppermute | solution.py:81
  15.5 1.6 %collective-permute-start.8 = (f32[328,128]{1,0:T(8,128)S(1)}, f32[328,128]{1,0:T(8,128)S(1)}, u32[]{:S(2)}, u32[]{:S(2)}) collective-permute-start(f32[328,128]{1,0:T(8,128)S(1)} %get-tuple-element.24.refs_3_), channel_id=1, source_target_pairs={{0,1},{1,0},{2,3},{3,2},{4,5},{5,4},{6,7},{7,6},{8,9},{9,8},{10,11... | collective-permute-start | bytes 503816 | tf_op jit(solution)/shard_map/ppermute | solution.py:81
  16.0 1.4 %collective-permute-start.10 = (bf16[128,512]{1,0:T(8,128)(2,1)S(1)}, bf16[128,512]{1,0:T(8,128)(2,1)S(1)}, u32[]{:S(2)}, u32[]{:S(2)}) collective-permute-start(bf16[128,512]{1,0:T(8,128)(2,1)S(1)} %last.1.refs_3_), channel_id=1, source_target_pairs={{0,1},{1,0},{2,3},{3,2},{4,5},{5,4},{6,7},{7,6},{8,9},{9,8},{10,11... | collective-permute-start | bytes 393224 | tf_op jit(solution)/shard_map/ppermute | solution.py:81
  17.7 4.9 %collective-permute-start.13 = (f32[1,256]{1,0:T(1,128)S(1)}, f32[1,256]{1,0:T(1,128)S(1)}, u32[]{:S(2)}, u32[]{:S(2)}) collective-permute-start(f32[1,256]{1,0:T(1,128)S(1)} %sums.1), channel_id=1, source_target_pairs={{0,25},{1,24},{8,17},{9,16},{16,9},{17,8},{24,1},{25,0},{2,27},{3,... | collective-permute-start | bytes 3080 | tf_op jit(solution)/shard_map/ppermute | solution.py:266
  19.3 3.9 %collective-permute-start.12 = (f32[1,256]{1,0:T(1,128)S(1)}, f32[1,256]{1,0:T(1,128)S(1)}, u32[]{:S(2)}, u32[]{:S(2)}) collective-permute-start(f32[1,256]{1,0:T(1,128)S(1)} %sums.1), channel_id=1, source_target_pairs={{0,17},{1,16},{8,25},{9,24},{16,1},{17,0},{24,9},{25,8},{2,19},{3,... | collective-permute-start | bytes 3080 | tf_op jit(solution)/shard_map/ppermute | solution.py:266
  20.3 3.0 %collective-permute-start.11 = (f32[1,256]{1,0:T(1,128)S(1)}, f32[1,256]{1,0:T(1,128)S(1)}, u32[]{:S(2)}, u32[]{:S(2)}) collective-permute-start(f32[1,256]{1,0:T(1,128)S(1)} %sums.1), channel_id=1, source_target_pairs={{0,9},{1,8},{8,1},{9,0},{16,25},{17,24},{24,17},{25,16},{2,11},{3,... | collective-permute-start | bytes 3080 | tf_op jit(solution)/shard_map/ppermute | solution.py:266

commit v9 on v8

--- a/solution.py
+++ b/solution.py
@@ -97,8 +97,11 @@
 
 def early_kernel(near, far, rights, after, mask, *refs):
     outs, left, held = refs[:-2], refs[-2], refs[-1]
-    held[0:2] = near[...]
-    held[2:4] = far[...]
+    layer = lax.axis_index("layer")
+    held[0] = near[0]
+    held[1 + layer] = near[1]
+    held[2 - layer] = far[0]
+    held[3] = far[1]
     row, col = lax.axis_index("row"), lax.axis_index("col")
     block = lax.rem(2 * row + 1, 5)
     left[...] = held[row ^ 3 ^ col]
@@ -145,14 +148,17 @@
     share = rows // count
     depth = left.shape[1]
     layer = lax.axis_index("layer")
-    lefts[:, 0:depth] = left[...]
+    crossed = jnp.logical_or(lax.axis_index("row") == 1, lax.axis_index("row") == 2)
+    here = pl.multiple_of(jnp.where(crossed, depth, 0), depth)
+    there = pl.multiple_of(jnp.where(crossed, 0, depth), depth)
+    lefts[:, pl.ds(here, depth)] = left[...]
     for n in range(count):
         columns = slice(n * broad, (n + 1) * broad)
         total[:, columns] = ours[n][0:rows, :] + theirs[n][0:rows, :]
         entries = slice(rows, rows + kept.shape[0])
         own = layer == n // wide
         kept[:, columns] = jnp.where(own, ours[n][entries, :], theirs[n][entries, :])
-        lefts[n * share : (n + 1) * share, depth:] = theirs[n][
+        lefts[n * share : (n + 1) * share, pl.ds(there, depth)] = theirs[n][
             theirs[n].shape[0] - share :, :
         ].astype(left.dtype)
 
@@ -208,10 +214,14 @@
     count = lax.axis_size("row")
     first = lax.ppermute(right, "row", [(0, 2), (3, 1), (1, 0), (2, 3)])
     second = lax.ppermute(right, "row", [(0, 1), (3, 2), (1, 3), (2, 0)])
-    pairs = [(2, 4), (3, 5), (4, 2), (5, 3), (0, 1), (1, 0), (6, 7), (7, 6)]
+    pairs = [(2, 5), (3, 4), (4, 3), (5, 2), (0, 1), (1, 0), (6, 7), (7, 6)]
     inner = lax.ppermute(right, ("row", "layer"), pairs)
     outer = lax.ppermute(first, "row", [(0, 1), (1, 0), (2, 3), (3, 2)])
-    beside = swapped(left, "col", 1)
+    along, across = (
+        [(2 * c + core, 2 * (c ^ (2 if core == turn else 1)) + core) for c in range(4) for core in (0, 1)]
+        for turn in (1, 0)
+    )
+    beside = lax.ppermute(left, ("col", "layer"), along)
     pair = call(
         pair_kernel, "pair", jax.ShapeDtypeStruct((2,) + left.shape, left.dtype), left, beside
     )
@@ -229,7 +239,7 @@
         "early",
         [part] * parts + [jax.ShapeDtypeStruct(left.shape, left.dtype)],
         pair,
-        swapped(pair, "col", 2),
+        lax.ppermute(pair, ("col", "layer"), across),
         rights,
         handed,
         prune_mask,

time: 24.2 us -> 24 us (level)
  starting transfers between devices: 13 us -> 12.3 us
  waiting for transfers between devices: 8.23 us -> 8.8 us
    ppermute x0 -> x2, waiting for transfers between devices: none -> 3.14 us  [the longest x1 2.77 us: on_device(): beside = lax.ppermute(left, ('col', 'layer'), along)]
    ppermute x7 -> x5, waiting for transfers between devices: 4.37 us -> 1.23 us  [swapped(): return lax.ppermute(value, axis, [(i, i ^ step) for i in range(count)])]
    ppermute x7 -> x5, starting transfers between devices: 4.22 us -> 1.15 us  [swapped(): return lax.ppermute(value, axis, [(i, i ^ step) for i in range(count)])]
    ppermute x0 -> x2, starting transfers between devices: none -> 3.08 us  [the longest x1 1.58 us: on_device(): lax.ppermute(pair, ('col', 'layer'), across)]
    ppermute x1, starting transfers between devices: 0.72 us -> 0.01 us  [on_device(): outer = lax.ppermute(first, 'row', [(0, 1), (1, 0), (2, 3), (3, 2)])]
    ppermute x1, waiting for transfers between devices: 2.29 us -> 3.01 us  [on_device(): second = lax.ppermute(right, 'row', [(0, 1), (3, 2), (1, 3), (2, 0)])]
where the time goes in v9:
time: 24 us; the launch traced here: 23.8 us
  starting transfers between devices  12.3 us (51%)
  waiting for transfers between devices  8.8 us (37%)
  Pallas kernels  1.96 us (8%)
  other arithmetic  0.74 us (3%)
    ppermute x1, starting transfers between devices, on_device(): first = lax.ppermute(right, 'row', [(0, 2), (3, 1), (1, 0), (2, 3)])  4.09 us
    ppermute x3, starting transfers between devices, on_device(): total = total + lax.ppermute(sums, ('row', 'layer'), pairs)  3.93 us
    ppermute x1, waiting for transfers between devices, on_device(): second = lax.ppermute(right, 'row', [(0, 1), (3, 2), (1, 3), (2, 0)])  3.01 us
    ppermute x1, waiting for transfers between devices, on_device(): beside = lax.ppermute(left, ('col', 'layer'), along)  2.77 us
    ppermute x1, starting transfers between devices, on_device(): lax.ppermute(pair, ('col', 'layer'), across)  1.58 us
    ppermute x1, starting transfers between devices, on_device(): beside = lax.ppermute(left, ('col', 'layer'), along)  1.49 us
    ppermute x3, waiting for transfers between devices, on_device(): total = total + lax.ppermute(sums, ('row', 'layer'), pairs)  1.28 us
    ppermute x5, waiting for transfers between devices, swapped(): return lax.ppermute(value, axis, [(i, i ^ step) for i in range(count)])  1.23 us
  transfers between devices with their start and end apart: 14, of which 11 were waited for; matrix products, arithmetic and copies ran while one was open for 0% of the time, Pallas kernels for 3%

profile of v9, /device:TPU:0, one launch (start us, length us, event | category | flops | bytes accessed | tf_op | source)
XLA Modules:
  0.0 23.8 jit_solution(1363884102318189866)
XLA Ops:
  0.0 1.1 %tiles.1 = (bf16[128,512]{1,0:T(8,128)(2,1)S(1)}, bf16[256,128]{1,0:T(8,128)(2,1)S(1)}, s32[2,2]{1,0:T(2,128)S(1)}) custom-call(s32[1,4]{1,0:T(1,128)} %bitcast.8, bf16[128,512]{1,0:T(8,128)(2,1)} %bitcast.5, s32[1,2]{1,0:T(1,128)} %bitcast.9, bf16[256,128]{1,0:T(8,128)(2,1)} %bitcast.6, s32[2,2]{1,0:T(2,128)} %refs_4_.1), custom_call_target="tpu_custom_call" | custom-call | tf_op jit(solution)/shard_map/tiles/pallas_call | solution.py:54
  1.1 4.1 %collective-permute-start.2 = (bf16[128,512]{1,0:T(8,128)(2,1)S(1)}, bf16[128,512]{1,0:T(8,128)(2,1)S(1)}, u32[]{:S(2)}, u32[]{:S(2)}) collective-permute-start(bf16[128,512]{1,0:T(8,128)(2,1)S(1)} %get-tuple-element.19.refs_0_), channel_id=1, source_target_pairs={{0,16},{24,8},{8,0},{16,24},{1,17},{25,9},{9,1},{17,25},{2,18},{26... | collective-permute-start | bytes 393224 | tf_op jit(solution)/shard_map/ppermute | solution.py:215
  5.2 1.5 %collective-permute-start = (bf16[256,128]{1,0:T(8,128)(2,1)S(1)}, bf16[256,128]{1,0:T(8,128)(2,1)S(1)}, u32[]{:S(2)}, u32[]{:S(2)}) collective-permute-start(bf16[256,128]{1,0:T(8,128)(2,1)S(1)} %get-tuple-element.18.here), channel_id=1, source_target_pairs={{0,2},{1,5},{2,0},{3,7},{4,6},{5,1},{6,4},{7,3},{8,10},{9,13},{10,... | collective-permute-start | bytes 196616 | tf_op jit(solution)/shard_map/ppermute | solution.py:224
  6.7 2.8 %collective-permute-done.beside = bf16[256,128]{1,0:T(8,128)(2,1)S(1)} collective-permute-done((bf16[256,128]{1,0:T(8,128)(2,1)S(1)}, bf16[256,128]{1,0:T(8,128)(2,1)S(1)}, u32[]{:S(2)}, u32[]{:S(2)}) %collective-permute-start) | collective-permute-done | bytes 65568 | tf_op jit(solution)/shard_map/ppermute | solution.py:224
  9.5 1.6 %collective-permute-start.1 = (bf16[2,256,128]{2,1,0:T(8,128)(2,1)S(1)}, bf16[2,256,128]{2,1,0:T(8,128)(2,1)S(1)}, u32[]{:S(2)}, u32[]{:S(2)}) collective-permute-start(bf16[2,256,128]{2,1,0:T(8,128)(2,1)S(1)} %pair.1.near), channel_id=1, source_target_pairs={{0,4},{1,3},{2,6},{3,1},{4,0},{5,7},{6,2},{7,5},{8,12},{9,11},{10,... | collective-permute-start | bytes 393224 | tf_op jit(solution)/shard_map/ppermute | solution.py:242
  11.1 3.0 %collective-permute-done.3.refs_2_ = bf16[128,512]{1,0:T(8,128)(2,1)S(1)} collective-permute-done((bf16[128,512]{1,0:T(8,128)(2,1)S(1)}, bf16[128,512]{1,0:T(8,128)(2,1)S(1)}, u32[]{:S(2)}, u32[]{:S(2)}) %collective-permute-start.3) | collective-permute-done | bytes 131104 | tf_op jit(solution)/shard_map/ppermute | solution.py:216
  14.1 0.4 %collective-permute-done.1.far = bf16[2,256,128]{2,1,0:T(8,128)(2,1)S(1)} collective-permute-done((bf16[2,256,128]{2,1,0:T(8,128)(2,1)S(1)}, bf16[2,256,128]{2,1,0:T(8,128)(2,1)S(1)}, u32[]{:S(2)}, u32[]{:S(2)}) %collective-permute-start.1) | collective-permute-done | bytes 131104 | tf_op jit(solution)/shard_map/ppermute | solution.py:242
  14.5 0.3 %early.1 = (f32[328,128]{1,0:T(8,128)S(1)}, f32[328,128]{1,0:T(8,128)S(1)}, f32[328,128]{1,0:T(8,128)S(1)}, f32[328,128]{1,0:T(8,128)S(1)}, bf16[256,128]{1,0:T(8,128)(2,1)S(1)}) custom-call(bf16[2,256,128]{2,1,0:T(8,128)(2,1)S(1)} %pair.1.near, bf16[2,256,128]{2,1,0:T(8,128)(2,1)S(1)} %collective-permute-done.1.far, bf16[3,128,512]{2,1,0:T(8,128)(2,1)S(1)} %rights.1.after, ...), custom_call_target="tpu_custom_call" | custom-call | tf_op jit(solution)/shard_map/early/pallas_call | solution.py:68
  14.9 0.5 %collective-permute-start.6 = (f32[328,128]{1,0:T(8,128)S(1)}, f32[328,128]{1,0:T(8,128)S(1)}, u32[]{:S(2)}, u32[]{:S(2)}) collective-permute-start(f32[328,128]{1,0:T(8,128)S(1)} %get-tuple-element.22.refs_1_), channel_id=1, source_target_pairs={{0,1},{1,0},{2,3},{3,2},{4,5},{5,4},{6,7},{7,6},{8,9},{9,8},{10,11... | collective-permute-start | bytes 503816 | tf_op jit(solution)/shard_map/ppermute | solution.py:81
  15.5 0.4 %collective-permute-start.8 = (f32[328,128]{1,0:T(8,128)S(1)}, f32[328,128]{1,0:T(8,128)S(1)}, u32[]{:S(2)}, u32[]{:S(2)}) collective-permute-start(f32[328,128]{1,0:T(8,128)S(1)} %get-tuple-element.24.refs_3_), channel_id=1, source_target_pairs={{0,1},{1,0},{2,3},{3,2},{4,5},{5,4},{6,7},{7,6},{8,9},{9,8},{10,11... | collective-permute-start | bytes 503816 | tf_op jit(solution)/shard_map/ppermute | solution.py:81
  15.9 0.1 collective-permute-done.9.outer
  16.1 0.2 collective-permute-done.5.refs_5_
  16.3 0.2 %collective-permute-done.6.refs_6_ = f32[328,128]{1,0:T(8,128)S(1)} collective-permute-done((f32[328,128]{1,0:T(8,128)S(1)}, f32[328,128]{1,0:T(8,128)S(1)}, u32[]{:S(2)}, u32[]{:S(2)}) %collective-permute-start.6) | collective-permute-done | bytes 167968 | tf_op jit(solution)/shard_map/ppermute | solution.py:81
  16.5 0.3 %collective-permute-done.7.refs_7_ = f32[328,128]{1,0:T(8,128)S(1)} collective-permute-done((f32[328,128]{1,0:T(8,128)S(1)}, f32[328,128]{1,0:T(8,128)S(1)}, u32[]{:S(2)}, u32[]{:S(2)}) %collective-permute-start.7) | collective-permute-done | bytes 167968 | tf_op jit(solution)/shard_map/ppermute | solution.py:81
  16.8 0.2 %collective-permute-done.8.refs_8_ = f32[328,128]{1,0:T(8,128)S(1)} collective-permute-done((f32[328,128]{1,0:T(8,128)S(1)}, f32[328,128]{1,0:T(8,128)S(1)}, u32[]{:S(2)}, u32[]{:S(2)}) %collective-permute-start.8) | collective-permute-done | bytes 167968 | tf_op jit(solution)/shard_map/ppermute | solution.py:81
  17.1 0.3 %collective-permute-done.10.refs_4_ = bf16[128,512]{1,0:T(8,128)(2,1)S(1)} collective-permute-done((bf16[128,512]{1,0:T(8,128)(2,1)S(1)}, bf16[128,512]{1,0:T(8,128)(2,1)S(1)}, u32[]{:S(2)}, u32[]{:S(2)}) %collective-permute-start.10) | collective-permute-done | bytes 131104 | tf_op jit(solution)/shard_map/ppermute | solution.py:81
  17.5 0.2 sums.1
  17.7 1.5 %collective-permute-start.13 = (f32[1,256]{1,0:T(1,128)S(1)}, f32[1,256]{1,0:T(1,128)S(1)}, u32[]{:S(2)}, u32[]{:S(2)}) collective-permute-start(f32[1,256]{1,0:T(1,128)S(1)} %sums.1), channel_id=1, source_target_pairs={{0,25},{1,24},{8,17},{9,16},{16,9},{17,8},{24,1},{25,0},{2,27},{3,... | collective-permute-start | bytes 3080 | tf_op jit(solution)/shard_map/ppermute | solution.py:276
  19.2 0.8 %collective-permute-start.12 = (f32[1,256]{1,0:T(1,128)S(1)}, f32[1,256]{1,0:T(1,128)S(1)}, u32[]{:S(2)}, u32[]{:S(2)}) collective-permute-start(f32[1,256]{1,0:T(1,128)S(1)} %sums.1), channel_id=1, source_target_pairs={{0,17},{1,16},{8,25},{9,24},{16,1},{17,0},{24,9},{25,8},{2,19},{3,... | collective-permute-start | bytes 3080 | tf_op jit(solution)/shard_map/ppermute | solution.py:276
  20.0 1.6 %collective-permute-start.11 = (f32[1,256]{1,0:T(1,128)S(1)}, f32[1,256]{1,0:T(1,128)S(1)}, u32[]{:S(2)}, u32[]{:S(2)}) collective-permute-start(f32[1,256]{1,0:T(1,128)S(1)} %sums.1), channel_id=1, source_target_pairs={{0,9},{1,8},{8,1},{9,0},{16,25},{17,24},{24,17},{25,16},{2,11},{3,... | collective-permute-start | bytes 3080 | tf_op jit(solution)/shard_map/ppermute | solution.py:276
  21.6 0.2 inflate.1
  21.8 0.7 %collective-permute-done.13 = f32[1,256]{1,0:T(1,128)S(1)} collective-permute-done((f32[1,256]{1,0:T(1,128)S(1)}, f32[1,256]{1,0:T(1,128)S(1)}, u32[]{:S(2)}, u32[]{:S(2)}) %collective-permute-start.13) | collective-permute-done | bytes 1056 | tf_op jit(solution)/shard_map/ppermute | solution.py:276
  22.5 0.6 %collective-permute-done.12 = f32[1,256]{1,0:T(1,128)S(1)} collective-permute-done((f32[1,256]{1,0:T(1,128)S(1)}, f32[1,256]{1,0:T(1,128)S(1)}, u32[]{:S(2)}, u32[]{:S(2)}) %collective-permute-start.12) | collective-permute-done | bytes 1056 | tf_op jit(solution)/shard_map/ppermute | solution.py:276
  23.1 0.7 %broadcast_multiply_fusion = f32[256,256]{1,0:T(8,128)} fusion(f32[256,256]{1,0:T(8,128)S(1)} %get-tuple-element.29, f32[256]{0:T(256)S(1)} %bitcast.7), kind=kLoop, calls=%fused_computation | loop fusion | flops 65536 | bytes 525312 | tf_op jit(solution)/shard_map/mul | solution.py:277
  (15 shorter events, 0.4 us)
Async XLA Ops:
  1.1 10.0 %collective-permute-start.2 = (bf16[128,512]{1,0:T(8,128)(2,1)S(1)}, bf16[128,512]{1,0:T(8,128)(2,1)S(1)}, u32[]{:S(2)}, u32[]{:S(2)}) collective-permute-start(bf16[128,512]{1,0:T(8,128)(2,1)S(1)} %get-tuple-element.19.refs_0_), channel_id=1, source_target_pairs={{0,16},{24,8},{8,0},{16,24},{1,17},{25,9},{9,1},{17,25},{2,18},{26... | collective-permute-start | bytes 393224 | tf_op jit(solution)/shard_map/ppermute | solution.py:215
  5.2 4.3 %collective-permute-start = (bf16[256,128]{1,0:T(8,128)(2,1)S(1)}, bf16[256,128]{1,0:T(8,128)(2,1)S(1)}, u32[]{:S(2)}, u32[]{:S(2)}) collective-permute-start(bf16[256,128]{1,0:T(8,128)(2,1)S(1)} %get-tuple-element.18.here), channel_id=1, source_target_pairs={{0,2},{1,5},{2,0},{3,7},{4,6},{5,1},{6,4},{7,3},{8,10},{9,13},{10,... | collective-permute-start | bytes 196616 | tf_op jit(solution)/shard_map/ppermute | solution.py:224
  6.7 7.4 %collective-permute-start.3 = (bf16[128,512]{1,0:T(8,128)(2,1)S(1)}, bf16[128,512]{1,0:T(8,128)(2,1)S(1)}, u32[]{:S(2)}, u32[]{:S(2)}) collective-permute-start(bf16[128,512]{1,0:T(8,128)(2,1)S(1)} %get-tuple-element.19.refs_0_), channel_id=1, source_target_pairs={{0,8},{24,16},{8,24},{16,0},{1,9},{25,17},{9,25},{17,1},{2,10},{26... | collective-permute-start | bytes 393224 | tf_op jit(solution)/shard_map/ppermute | solution.py:216
  6.7 7.4 %collective-permute-start.4 = (bf16[128,512]{1,0:T(8,128)(2,1)S(1)}, bf16[128,512]{1,0:T(8,128)(2,1)S(1)}, u32[]{:S(2)}, u32[]{:S(2)}) collective-permute-start(bf16[128,512]{1,0:T(8,128)(2,1)S(1)} %get-tuple-element.19.refs_0_), channel_id=1, source_target_pairs={{8,17},{9,16},{16,9},{17,8},{0,1},{1,0},{24,25},{25,24},{10,19},{1... | collective-permute-start | bytes 393224 | tf_op jit(solution)/shard_map/ppermute | solution.py:218
  9.5 5.0 %collective-permute-start.1 = (bf16[2,256,128]{2,1,0:T(8,128)(2,1)S(1)}, bf16[2,256,128]{2,1,0:T(8,128)(2,1)S(1)}, u32[]{:S(2)}, u32[]{:S(2)}) collective-permute-start(bf16[2,256,128]{2,1,0:T(8,128)(2,1)S(1)} %pair.1.near), channel_id=1, source_target_pairs={{0,4},{1,3},{2,6},{3,1},{4,0},{5,7},{6,2},{7,5},{8,12},{9,11},{10,... | collective-permute-start | bytes 393224 | tf_op jit(solution)/shard_map/ppermute | solution.py:242
  11.1 5.0 %collective-permute-start.9 = (bf16[128,512]{1,0:T(8,128)(2,1)S(1)}, bf16[128,512]{1,0:T(8,128)(2,1)S(1)}, u32[]{:S(2)}, u32[]{:S(2)}) collective-permute-start(bf16[128,512]{1,0:T(8,128)(2,1)S(1)} %collective-permute-done.2.refs_1_), channel_id=1, source_target_pairs={{0,8},{8,0},{16,24},{24,16},{1,9},{9,1},{17,25},{25,17},{2,10},{10... | collective-permute-start | bytes 393224 | tf_op jit(solution)/shard_map/ppermute | solution.py:219
  14.8 1.5 %collective-permute-start.5 = (f32[328,128]{1,0:T(8,128)S(1)}, f32[328,128]{1,0:T(8,128)S(1)}, u32[]{:S(2)}, u32[]{:S(2)}) collective-permute-start(f32[328,128]{1,0:T(8,128)S(1)} %get-tuple-element.21.refs_0_), channel_id=1, source_target_pairs={{0,1},{1,0},{2,3},{3,2},{4,5},{5,4},{6,7},{7,6},{8,9},{9,8},{10,11... | collective-permute-start | bytes 503816 | tf_op jit(solution)/shard_map/ppermute | solution.py:81
  14.9 1.6 %collective-permute-start.6 = (f32[328,128]{1,0:T(8,128)S(1)}, f32[328,128]{1,0:T(8,128)S(1)}, u32[]{:S(2)}, u32[]{:S(2)}) collective-permute-start(f32[328,128]{1,0:T(8,128)S(1)} %get-tuple-element.22.refs_1_), channel_id=1, source_target_pairs={{0,1},{1,0},{2,3},{3,2},{4,5},{5,4},{6,7},{7,6},{8,9},{9,8},{10,11... | collective-permute-start | bytes 503816 | tf_op jit(solution)/shard_map/ppermute | solution.py:81
  15.4 1.4 %collective-permute-start.7 = (f32[328,128]{1,0:T(8,128)S(1)}, f32[328,128]{1,0:T(8,128)S(1)}, u32[]{:S(2)}, u32[]{:S(2)}) collective-permute-start(f32[328,128]{1,0:T(8,128)S(1)} %get-tuple-element.23.refs_2_), channel_id=1, source_target_pairs={{0,1},{1,0},{2,3},{3,2},{4,5},{5,4},{6,7},{7,6},{8,9},{9,8},{10,11... | collective-permute-start | bytes 503816 | tf_op jit(solution)/shard_map/ppermute | solution.py:81
  15.5 1.6 %collective-permute-start.8 = (f32[328,128]{1,0:T(8,128)S(1)}, f32[328,128]{1,0:T(8,128)S(1)}, u32[]{:S(2)}, u32[]{:S(2)}) collective-permute-start(f32[328,128]{1,0:T(8,128)S(1)} %get-tuple-element.24.refs_3_), channel_id=1, source_target_pairs={{0,1},{1,0},{2,3},{3,2},{4,5},{5,4},{6,7},{7,6},{8,9},{9,8},{10,11... | collective-permute-start | bytes 503816 | tf_op jit(solution)/shard_map/ppermute | solution.py:81
  16.0 1.4 %collective-permute-start.10 = (bf16[128,512]{1,0:T(8,128)(2,1)S(1)}, bf16[128,512]{1,0:T(8,128)(2,1)S(1)}, u32[]{:S(2)}, u32[]{:S(2)}) collective-permute-start(bf16[128,512]{1,0:T(8,128)(2,1)S(1)} %last.1.refs_3_), channel_id=1, source_target_pairs={{0,1},{1,0},{2,3},{3,2},{4,5},{5,4},{6,7},{7,6},{8,9},{9,8},{10,11... | collective-permute-start | bytes 393224 | tf_op jit(solution)/shard_map/ppermute | solution.py:81
  17.7 4.9 %collective-permute-start.13 = (f32[1,256]{1,0:T(1,128)S(1)}, f32[1,256]{1,0:T(1,128)S(1)}, u32[]{:S(2)}, u32[]{:S(2)}) collective-permute-start(f32[1,256]{1,0:T(1,128)S(1)} %sums.1), channel_id=1, source_target_pairs={{0,25},{1,24},{8,17},{9,16},{16,9},{17,8},{24,1},{25,0},{2,27},{3,... | collective-permute-start | bytes 3080 | tf_op jit(solution)/shard_map/ppermute | solution.py:276
  19.2 3.9 %collective-permute-start.12 = (f32[1,256]{1,0:T(1,128)S(1)}, f32[1,256]{1,0:T(1,128)S(1)}, u32[]{:S(2)}, u32[]{:S(2)}) collective-permute-start(f32[1,256]{1,0:T(1,128)S(1)} %sums.1), channel_id=1, source_target_pairs={{0,17},{1,16},{8,25},{9,24},{16,1},{17,0},{24,9},{25,8},{2,19},{3,... | collective-permute-start | bytes 3080 | tf_op jit(solution)/shard_map/ppermute | solution.py:276
  20.0 3.1 %collective-permute-start.11 = (f32[1,256]{1,0:T(1,128)S(1)}, f32[1,256]{1,0:T(1,128)S(1)}, u32[]{:S(2)}, u32[]{:S(2)}) collective-permute-start(f32[1,256]{1,0:T(1,128)S(1)} %sums.1), channel_id=1, source_target_pairs={{0,9},{1,8},{8,1},{9,0},{16,25},{17,24},{24,17},{25,16},{2,11},{3,... | collective-permute-start | bytes 3080 | tf_op jit(solution)/shard_map/ppermute | solution.py:276

commit v10 on v9

--- a/solution.py
+++ b/solution.py
@@ -142,35 +142,35 @@
 def join_kernel(sizes, *refs):
     rows, half, tall, wide = sizes
     count = 2 * wide
-    ours, left, theirs = refs[:count], refs[count], refs[count + 1 : -3]
-    total, kept, lefts = refs[-3:]
+    ours, left, theirs, last = refs[:count], refs[count], refs[count + 1 : -5], refs[-5]
+    total, kept, lefts, other = refs[-4:]
     broad = half // wide
     share = rows // count
     depth = left.shape[1]
     layer = lax.axis_index("layer")
     crossed = jnp.logical_or(lax.axis_index("row") == 1, lax.axis_index("row") == 2)
-    here = pl.multiple_of(jnp.where(crossed, depth, 0), depth)
-    there = pl.multiple_of(jnp.where(crossed, 0, depth), depth)
-    lefts[:, pl.ds(here, depth)] = left[...]
     for n in range(count):
         columns = slice(n * broad, (n + 1) * broad)
         total[:, columns] = ours[n][0:rows, :] + theirs[n][0:rows, :]
         entries = slice(rows, rows + kept.shape[0])
         own = layer == n // wide
         kept[:, columns] = jnp.where(own, ours[n][entries, :], theirs[n][entries, :])
-        lefts[n * share : (n + 1) * share, pl.ds(there, depth)] = theirs[n][
+        other[n * share : (n + 1) * share, :] = theirs[n][
             theirs[n].shape[0] - share :, :
         ].astype(left.dtype)
+    mine = jnp.where(crossed, other[...], left[...])
+    lefts[...] = jnp.where(crossed, left[...], other[...])
+    total[...] += jnp.dot(mine, last[...], preferred_element_type=jnp.float32)
 
 
 def inflate(side, sizes, joined, out, sums):
     rows, half, tall, wide = sizes
-    early, kept, lefts, here, there = joined
+    early, kept, lefts, there = joined
     high = rows // tall
     columns = slice(side * half, (side + 1) * half)
     product = early[:, columns] + jnp.dot(
         lefts[...],
-        jnp.concatenate([here[:, columns], there[:, columns]], axis=0),
+        there[:, columns],
         preferred_element_type=jnp.float32,
     )
     total = jnp.zeros((1, half), jnp.float32)
@@ -255,19 +255,21 @@
         [
             jax.ShapeDtypeStruct((rows, columns), f32),
             jax.ShapeDtypeStruct(((tall + 7) // 8 * 8, columns), f32),
-            jax.ShapeDtypeStruct((rows, 2 * left.shape[1]), left.dtype),
+            jax.ShapeDtypeStruct(left.shape, left.dtype),
         ],
         *ours,
         *(swapped(value, "layer", 1) for value in ours[:-1]),
+        last,
+        scratch=[pltpu.VMEM(left.shape, left.dtype)],
     ))
-    operands += [last, swapped(last, "layer", 1)]
+    operands.append(swapped(last, "layer", 1))
     line = jax.ShapeDtypeStruct((1, half), f32)
     sums = call(functools.partial(sums_kernel, sizes), "sums", line, *operands)
     inflated, sums_here = call(
         functools.partial(inflate_kernel, sizes), "inflate", [piece, line], *operands
     )
     total = sums_here
-    for step in (1, 2, 3):
+    for step in (3, 2, 1):
         pairs = [
             (2 * z + core, 2 * (z ^ step) + 1 - core)
             for z in range(count)

time: 24 us -> 24 us (level)
  no operation moved by 1% of the time
where the time goes in v10:
time: 24 us; the launch traced here: 23.8 us
  starting transfers between devices  12.3 us (51%)
  waiting for transfers between devices  8.68 us (36%)
  Pallas kernels  2.06 us (9%)
  other arithmetic  0.74 us (3%)
    ppermute x1, starting transfers between devices, on_device(): first = lax.ppermute(right, 'row', [(0, 2), (3, 1), (1, 0), (2, 3)])  4.09 us
    ppermute x3, starting transfers between devices, on_device(): total = total + lax.ppermute(sums, ('row', 'layer'), pairs)  3.93 us
    ppermute x1, waiting for transfers between devices, on_device(): second = lax.ppermute(right, 'row', [(0, 1), (3, 2), (1, 3), (2, 0)])  3.01 us
    ppermute x1, waiting for transfers between devices, on_device(): beside = lax.ppermute(left, ('col', 'layer'), along)  2.77 us
    ppermute x1, starting transfers between devices, on_device(): lax.ppermute(pair, ('col', 'layer'), across)  1.58 us
    ppermute x1, starting transfers between devices, on_device(): beside = lax.ppermute(left, ('col', 'layer'), along)  1.49 us
    ppermute x3, waiting for transfers between devices, on_device(): total = total + lax.ppermute(sums, ('row', 'layer'), pairs)  1.3 us
    ppermute x5, starting transfers between devices, swapped(): return lax.ppermute(value, axis, [(i, i ^ step) for i in range(count)])  1.15 us
  transfers between devices with their start and end apart: 14, of which 11 were waited for; matrix products, arithmetic and copies ran while one was open for 0% of the time, Pallas kernels for 3%

profile of v10, /device:TPU:0, one launch (start us, length us, event | category | flops | bytes accessed | tf_op | source)
XLA Modules:
  0.0 23.8 jit_solution(9800879858599306383)
XLA Ops:
  0.0 1.1 %tiles.1 = (bf16[128,512]{1,0:T(8,128)(2,1)S(1)}, bf16[256,128]{1,0:T(8,128)(2,1)S(1)}, s32[2,2]{1,0:T(2,128)S(1)}) custom-call(s32[1,4]{1,0:T(1,128)} %bitcast.8, bf16[128,512]{1,0:T(8,128)(2,1)} %bitcast.5, s32[1,2]{1,0:T(1,128)} %bitcast.9, bf16[256,128]{1,0:T(8,128)(2,1)} %bitcast.6, s32[2,2]{1,0:T(2,128)} %refs_4_.1), custom_call_target="tpu_custom_call" | custom-call | tf_op jit(solution)/shard_map/tiles/pallas_call | solution.py:54
  1.1 4.1 %collective-permute-start.2 = (bf16[128,512]{1,0:T(8,128)(2,1)S(1)}, bf16[128,512]{1,0:T(8,128)(2,1)S(1)}, u32[]{:S(2)}, u32[]{:S(2)}) collective-permute-start(bf16[128,512]{1,0:T(8,128)(2,1)S(1)} %get-tuple-element.19.refs_0_), channel_id=1, source_target_pairs={{0,16},{24,8},{8,0},{16,24},{1,17},{25,9},{9,1},{17,25},{2,18},{26... | collective-permute-start | bytes 393224 | tf_op jit(solution)/shard_map/ppermute | solution.py:215
  5.2 1.5 %collective-permute-start = (bf16[256,128]{1,0:T(8,128)(2,1)S(1)}, bf16[256,128]{1,0:T(8,128)(2,1)S(1)}, u32[]{:S(2)}, u32[]{:S(2)}) collective-permute-start(bf16[256,128]{1,0:T(8,128)(2,1)S(1)} %get-tuple-element.18.here), channel_id=1, source_target_pairs={{0,2},{1,5},{2,0},{3,7},{4,6},{5,1},{6,4},{7,3},{8,10},{9,13},{10,... | collective-permute-start | bytes 196616 | tf_op jit(solution)/shard_map/ppermute | solution.py:224
  6.7 2.8 %collective-permute-done.beside = bf16[256,128]{1,0:T(8,128)(2,1)S(1)} collective-permute-done((bf16[256,128]{1,0:T(8,128)(2,1)S(1)}, bf16[256,128]{1,0:T(8,128)(2,1)S(1)}, u32[]{:S(2)}, u32[]{:S(2)}) %collective-permute-start) | collective-permute-done | bytes 65568 | tf_op jit(solution)/shard_map/ppermute | solution.py:224
  9.5 1.6 %collective-permute-start.1 = (bf16[2,256,128]{2,1,0:T(8,128)(2,1)S(1)}, bf16[2,256,128]{2,1,0:T(8,128)(2,1)S(1)}, u32[]{:S(2)}, u32[]{:S(2)}) collective-permute-start(bf16[2,256,128]{2,1,0:T(8,128)(2,1)S(1)} %pair.1.near), channel_id=1, source_target_pairs={{0,4},{1,3},{2,6},{3,1},{4,0},{5,7},{6,2},{7,5},{8,12},{9,11},{10,... | collective-permute-start | bytes 393224 | tf_op jit(solution)/shard_map/ppermute | solution.py:242
  11.1 3.0 %collective-permute-done.3.refs_2_ = bf16[128,512]{1,0:T(8,128)(2,1)S(1)} collective-permute-done((bf16[128,512]{1,0:T(8,128)(2,1)S(1)}, bf16[128,512]{1,0:T(8,128)(2,1)S(1)}, u32[]{:S(2)}, u32[]{:S(2)}) %collective-permute-start.3) | collective-permute-done | bytes 131104 | tf_op jit(solution)/shard_map/ppermute | solution.py:216
  14.1 0.4 %collective-permute-done.1.far = bf16[2,256,128]{2,1,0:T(8,128)(2,1)S(1)} collective-permute-done((bf16[2,256,128]{2,1,0:T(8,128)(2,1)S(1)}, bf16[2,256,128]{2,1,0:T(8,128)(2,1)S(1)}, u32[]{:S(2)}, u32[]{:S(2)}) %collective-permute-start.1) | collective-permute-done | bytes 131104 | tf_op jit(solution)/shard_map/ppermute | solution.py:242
  14.5 0.3 %early.1 = (f32[328,128]{1,0:T(8,128)S(1)}, f32[328,128]{1,0:T(8,128)S(1)}, f32[328,128]{1,0:T(8,128)S(1)}, f32[328,128]{1,0:T(8,128)S(1)}, bf16[256,128]{1,0:T(8,128)(2,1)S(1)}) custom-call(bf16[2,256,128]{2,1,0:T(8,128)(2,1)S(1)} %pair.1.near, bf16[2,256,128]{2,1,0:T(8,128)(2,1)S(1)} %collective-permute-done.1.far, bf16[3,128,512]{2,1,0:T(8,128)(2,1)S(1)} %rights.1.after, ...), custom_call_target="tpu_custom_call" | custom-call | tf_op jit(solution)/shard_map/early/pallas_call | solution.py:68
  14.9 0.5 %collective-permute-start.6 = (f32[328,128]{1,0:T(8,128)S(1)}, f32[328,128]{1,0:T(8,128)S(1)}, u32[]{:S(2)}, u32[]{:S(2)}) collective-permute-start(f32[328,128]{1,0:T(8,128)S(1)} %get-tuple-element.22.refs_1_), channel_id=1, source_target_pairs={{0,1},{1,0},{2,3},{3,2},{4,5},{5,4},{6,7},{7,6},{8,9},{9,8},{10,11... | collective-permute-start | bytes 503816 | tf_op jit(solution)/shard_map/ppermute | solution.py:81
  15.5 0.4 %collective-permute-start.8 = (f32[328,128]{1,0:T(8,128)S(1)}, f32[328,128]{1,0:T(8,128)S(1)}, u32[]{:S(2)}, u32[]{:S(2)}) collective-permute-start(f32[328,128]{1,0:T(8,128)S(1)} %get-tuple-element.24.refs_3_), channel_id=1, source_target_pairs={{0,1},{1,0},{2,3},{3,2},{4,5},{5,4},{6,7},{7,6},{8,9},{9,8},{10,11... | collective-permute-start | bytes 503816 | tf_op jit(solution)/shard_map/ppermute | solution.py:81
  16.1 0.2 collective-permute-done.5.refs_5_
  16.3 0.2 %collective-permute-done.6.refs_6_ = f32[328,128]{1,0:T(8,128)S(1)} collective-permute-done((f32[328,128]{1,0:T(8,128)S(1)}, f32[328,128]{1,0:T(8,128)S(1)}, u32[]{:S(2)}, u32[]{:S(2)}) %collective-permute-start.6) | collective-permute-done | bytes 167968 | tf_op jit(solution)/shard_map/ppermute | solution.py:81
  16.5 0.3 %collective-permute-done.7.refs_7_ = f32[328,128]{1,0:T(8,128)S(1)} collective-permute-done((f32[328,128]{1,0:T(8,128)S(1)}, f32[328,128]{1,0:T(8,128)S(1)}, u32[]{:S(2)}, u32[]{:S(2)}) %collective-permute-start.7) | collective-permute-done | bytes 167968 | tf_op jit(solution)/shard_map/ppermute | solution.py:81
  16.8 0.2 %collective-permute-done.8.refs_8_ = f32[328,128]{1,0:T(8,128)S(1)} collective-permute-done((f32[328,128]{1,0:T(8,128)S(1)}, f32[328,128]{1,0:T(8,128)S(1)}, u32[]{:S(2)}, u32[]{:S(2)}) %collective-permute-start.8) | collective-permute-done | bytes 167968 | tf_op jit(solution)/shard_map/ppermute | solution.py:81
  17.0 0.2 join.1
  17.3 0.2 collective-permute-done.10.refs_3_
  17.5 0.2 sums.1
  17.7 1.5 %collective-permute-start.11 = (f32[1,256]{1,0:T(1,128)S(1)}, f32[1,256]{1,0:T(1,128)S(1)}, u32[]{:S(2)}, u32[]{:S(2)}) collective-permute-start(f32[1,256]{1,0:T(1,128)S(1)} %sums.1), channel_id=1, source_target_pairs={{0,25},{1,24},{8,17},{9,16},{16,9},{17,8},{24,1},{25,0},{2,27},{3,... | collective-permute-start | bytes 3080 | tf_op jit(solution)/shard_map/ppermute | solution.py:278
  19.2 0.9 %collective-permute-start.12 = (f32[1,256]{1,0:T(1,128)S(1)}, f32[1,256]{1,0:T(1,128)S(1)}, u32[]{:S(2)}, u32[]{:S(2)}) collective-permute-start(f32[1,256]{1,0:T(1,128)S(1)} %sums.1), channel_id=1, source_target_pairs={{0,17},{1,16},{8,25},{9,24},{16,1},{17,0},{24,9},{25,8},{2,19},{3,... | collective-permute-start | bytes 3080 | tf_op jit(solution)/shard_map/ppermute | solution.py:278
  20.1 1.5 %collective-permute-start.13 = (f32[1,256]{1,0:T(1,128)S(1)}, f32[1,256]{1,0:T(1,128)S(1)}, u32[]{:S(2)}, u32[]{:S(2)}) collective-permute-start(f32[1,256]{1,0:T(1,128)S(1)} %sums.1), channel_id=1, source_target_pairs={{0,9},{1,8},{8,1},{9,0},{16,25},{17,24},{24,17},{25,16},{2,11},{3,... | collective-permute-start | bytes 3080 | tf_op jit(solution)/shard_map/ppermute | solution.py:278
  21.6 0.2 inflate.1
  21.8 0.7 %collective-permute-done.11 = f32[1,256]{1,0:T(1,128)S(1)} collective-permute-done((f32[1,256]{1,0:T(1,128)S(1)}, f32[1,256]{1,0:T(1,128)S(1)}, u32[]{:S(2)}, u32[]{:S(2)}) %collective-permute-start.11) | collective-permute-done | bytes 1056 | tf_op jit(solution)/shard_map/ppermute | solution.py:278
  22.5 0.6 %collective-permute-done.12 = f32[1,256]{1,0:T(1,128)S(1)} collective-permute-done((f32[1,256]{1,0:T(1,128)S(1)}, f32[1,256]{1,0:T(1,128)S(1)}, u32[]{:S(2)}, u32[]{:S(2)}) %collective-permute-start.12) | collective-permute-done | bytes 1056 | tf_op jit(solution)/shard_map/ppermute | solution.py:278
  23.1 0.7 %broadcast_multiply_fusion = f32[256,256]{1,0:T(8,128)} fusion(f32[256,256]{1,0:T(8,128)S(1)} %get-tuple-element.29, f32[256]{0:T(256)S(1)} %bitcast.7), kind=kLoop, calls=%fused_computation | loop fusion | flops 65536 | bytes 525312 | tf_op jit(solution)/shard_map/mul | solution.py:279
  (15 shorter events, 0.4 us)
Async XLA Ops:
  1.1 10.0 %collective-permute-start.2 = (bf16[128,512]{1,0:T(8,128)(2,1)S(1)}, bf16[128,512]{1,0:T(8,128)(2,1)S(1)}, u32[]{:S(2)}, u32[]{:S(2)}) collective-permute-start(bf16[128,512]{1,0:T(8,128)(2,1)S(1)} %get-tuple-element.19.refs_0_), channel_id=1, source_target_pairs={{0,16},{24,8},{8,0},{16,24},{1,17},{25,9},{9,1},{17,25},{2,18},{26... | collective-permute-start | bytes 393224 | tf_op jit(solution)/shard_map/ppermute | solution.py:215
  5.2 4.3 %collective-permute-start = (bf16[256,128]{1,0:T(8,128)(2,1)S(1)}, bf16[256,128]{1,0:T(8,128)(2,1)S(1)}, u32[]{:S(2)}, u32[]{:S(2)}) collective-permute-start(bf16[256,128]{1,0:T(8,128)(2,1)S(1)} %get-tuple-element.18.here), channel_id=1, source_target_pairs={{0,2},{1,5},{2,0},{3,7},{4,6},{5,1},{6,4},{7,3},{8,10},{9,13},{10,... | collective-permute-start | bytes 196616 | tf_op jit(solution)/shard_map/ppermute | solution.py:224
  6.7 7.4 %collective-permute-start.3 = (bf16[128,512]{1,0:T(8,128)(2,1)S(1)}, bf16[128,512]{1,0:T(8,128)(2,1)S(1)}, u32[]{:S(2)}, u32[]{:S(2)}) collective-permute-start(bf16[128,512]{1,0:T(8,128)(2,1)S(1)} %get-tuple-element.19.refs_0_), channel_id=1, source_target_pairs={{0,8},{24,16},{8,24},{16,0},{1,9},{25,17},{9,25},{17,1},{2,10},{26... | collective-permute-start | bytes 393224 | tf_op jit(solution)/shard_map/ppermute | solution.py:216
  6.7 7.4 %collective-permute-start.4 = (bf16[128,512]{1,0:T(8,128)(2,1)S(1)}, bf16[128,512]{1,0:T(8,128)(2,1)S(1)}, u32[]{:S(2)}, u32[]{:S(2)}) collective-permute-start(bf16[128,512]{1,0:T(8,128)(2,1)S(1)} %get-tuple-element.19.refs_0_), channel_id=1, source_target_pairs={{8,17},{9,16},{16,9},{17,8},{0,1},{1,0},{24,25},{25,24},{10,19},{1... | collective-permute-start | bytes 393224 | tf_op jit(solution)/shard_map/ppermute | solution.py:218
  9.5 5.0 %collective-permute-start.1 = (bf16[2,256,128]{2,1,0:T(8,128)(2,1)S(1)}, bf16[2,256,128]{2,1,0:T(8,128)(2,1)S(1)}, u32[]{:S(2)}, u32[]{:S(2)}) collective-permute-start(bf16[2,256,128]{2,1,0:T(8,128)(2,1)S(1)} %pair.1.near), channel_id=1, source_target_pairs={{0,4},{1,3},{2,6},{3,1},{4,0},{5,7},{6,2},{7,5},{8,12},{9,11},{10,... | collective-permute-start | bytes 393224 | tf_op jit(solution)/shard_map/ppermute | solution.py:242
  11.1 5.0 %collective-permute-start.9 = (bf16[128,512]{1,0:T(8,128)(2,1)S(1)}, bf16[128,512]{1,0:T(8,128)(2,1)S(1)}, u32[]{:S(2)}, u32[]{:S(2)}) collective-permute-start(bf16[128,512]{1,0:T(8,128)(2,1)S(1)} %collective-permute-done.2.refs_1_), channel_id=1, source_target_pairs={{0,8},{8,0},{16,24},{24,16},{1,9},{9,1},{17,25},{25,17},{2,10},{10... | collective-permute-start | bytes 393224 | tf_op jit(solution)/shard_map/ppermute | solution.py:219
  14.8 1.5 %collective-permute-start.5 = (f32[328,128]{1,0:T(8,128)S(1)}, f32[328,128]{1,0:T(8,128)S(1)}, u32[]{:S(2)}, u32[]{:S(2)}) collective-permute-start(f32[328,128]{1,0:T(8,128)S(1)} %get-tuple-element.21.refs_0_), channel_id=1, source_target_pairs={{0,1},{1,0},{2,3},{3,2},{4,5},{5,4},{6,7},{7,6},{8,9},{9,8},{10,11... | collective-permute-start | bytes 503816 | tf_op jit(solution)/shard_map/ppermute | solution.py:81
  14.9 1.6 %collective-permute-start.6 = (f32[328,128]{1,0:T(8,128)S(1)}, f32[328,128]{1,0:T(8,128)S(1)}, u32[]{:S(2)}, u32[]{:S(2)}) collective-permute-start(f32[328,128]{1,0:T(8,128)S(1)} %get-tuple-element.22.refs_1_), channel_id=1, source_target_pairs={{0,1},{1,0},{2,3},{3,2},{4,5},{5,4},{6,7},{7,6},{8,9},{9,8},{10,11... | collective-permute-start | bytes 503816 | tf_op jit(solution)/shard_map/ppermute | solution.py:81
  15.4 1.4 %collective-permute-start.7 = (f32[328,128]{1,0:T(8,128)S(1)}, f32[328,128]{1,0:T(8,128)S(1)}, u32[]{:S(2)}, u32[]{:S(2)}) collective-permute-start(f32[328,128]{1,0:T(8,128)S(1)} %get-tuple-element.23.refs_2_), channel_id=1, source_target_pairs={{0,1},{1,0},{2,3},{3,2},{4,5},{5,4},{6,7},{7,6},{8,9},{9,8},{10,11... | collective-permute-start | bytes 503816 | tf_op jit(solution)/shard_map/ppermute | solution.py:81
  15.5 1.6 %collective-permute-start.8 = (f32[328,128]{1,0:T(8,128)S(1)}, f32[328,128]{1,0:T(8,128)S(1)}, u32[]{:S(2)}, u32[]{:S(2)}) collective-permute-start(f32[328,128]{1,0:T(8,128)S(1)} %get-tuple-element.24.refs_3_), channel_id=1, source_target_pairs={{0,1},{1,0},{2,3},{3,2},{4,5},{5,4},{6,7},{7,6},{8,9},{9,8},{10,11... | collective-permute-start | bytes 503816 | tf_op jit(solution)/shard_map/ppermute | solution.py:81
  16.0 1.4 %collective-permute-start.10 = (bf16[128,512]{1,0:T(8,128)(2,1)S(1)}, bf16[128,512]{1,0:T(8,128)(2,1)S(1)}, u32[]{:S(2)}, u32[]{:S(2)}) collective-permute-start(bf16[128,512]{1,0:T(8,128)(2,1)S(1)} %last.1.refs_9_), channel_id=1, source_target_pairs={{0,1},{1,0},{2,3},{3,2},{4,5},{5,4},{6,7},{7,6},{8,9},{9,8},{10,11... | collective-permute-start | bytes 393224 | tf_op jit(solution)/shard_map/ppermute | solution.py:81
  17.7 4.9 %collective-permute-start.11 = (f32[1,256]{1,0:T(1,128)S(1)}, f32[1,256]{1,0:T(1,128)S(1)}, u32[]{:S(2)}, u32[]{:S(2)}) collective-permute-start(f32[1,256]{1,0:T(1,128)S(1)} %sums.1), channel_id=1, source_target_pairs={{0,25},{1,24},{8,17},{9,16},{16,9},{17,8},{24,1},{25,0},{2,27},{3,... | collective-permute-start | bytes 3080 | tf_op jit(solution)/shard_map/ppermute | solution.py:278
  19.2 3.9 %collective-permute-start.12 = (f32[1,256]{1,0:T(1,128)S(1)}, f32[1,256]{1,0:T(1,128)S(1)}, u32[]{:S(2)}, u32[]{:S(2)}) collective-permute-start(f32[1,256]{1,0:T(1,128)S(1)} %sums.1), channel_id=1, source_target_pairs={{0,17},{1,16},{8,25},{9,24},{16,1},{17,0},{24,9},{25,8},{2,19},{3,... | collective-permute-start | bytes 3080 | tf_op jit(solution)/shard_map/ppermute | solution.py:278
  20.1 3.0 %collective-permute-start.13 = (f32[1,256]{1,0:T(1,128)S(1)}, f32[1,256]{1,0:T(1,128)S(1)}, u32[]{:S(2)}, u32[]{:S(2)}) collective-permute-start(f32[1,256]{1,0:T(1,128)S(1)} %sums.1), channel_id=1, source_target_pairs={{0,9},{1,8},{8,1},{9,0},{16,25},{17,24},{24,17},{25,16},{2,11},{3,... | collective-permute-start | bytes 3080 | tf_op jit(solution)/shard_map/ppermute | solution.py:278

commit v11 on v9

--- a/solution.py
+++ b/solution.py
@@ -32,7 +32,7 @@
     operands, (right, left, prune), held, arrived = refs[:5], refs[5:8], refs[8:12], refs[12]
     copies = []
     for n, target in enumerate(held + (prune,)):
-        parts = 4 if n in (1, 3) else 1
+        parts = {1: 2, 3: 2}.get(n, 1)
         tall = operands[n].shape[0] // parts
         for part in range(parts):
             at = pl.ds(part * tall, tall)
@@ -41,10 +41,10 @@
             )
             copy.start()
             copies.append(copy)
-    for copy in copies[:5]:
+    for copy in copies[:3]:
         copy.wait()
     keep_tiles(held[0], False, held[1], right)
-    for copy in copies[5:]:
+    for copy in copies[3:]:
         copy.wait()
     keep_tiles(held[2], True, held[3], left)
 
@@ -58,7 +58,7 @@
         ],
         in_specs=[pl.BlockSpec(memory_space=pltpu.HBM)] * 5,
         out_specs=[VMEM, VMEM, VMEM],
-        scratch_shapes=held + [pltpu.SemaphoreType.DMA((11,))],
+        scratch_shapes=held + [pltpu.SemaphoreType.DMA((7,))],
         compiler_params=room,
         name="tiles",
     )(*(pltpu.with_memory_space_constraint(value, pltpu.HBM) for value in operands))

time: 24 us -> 24 us (level)
  no operation moved by 1% of the time
where the time goes in v11:
time: 24 us; the launch traced here: 23.9 us
  starting transfers between devices  12.3 us (51%)
  waiting for transfers between devices  8.8 us (37%)
  Pallas kernels  1.98 us (8%)
  other arithmetic  0.74 us (3%)
    ppermute x1, starting transfers between devices, on_device(): first = lax.ppermute(right, 'row', [(0, 2), (3, 1), (1, 0), (2, 3)])  4.09 us
    ppermute x3, starting transfers between devices, on_device(): total = total + lax.ppermute(sums, ('row', 'layer'), pairs)  3.93 us
    ppermute x1, waiting for transfers between devices, on_device(): second = lax.ppermute(right, 'row', [(0, 1), (3, 2), (1, 3), (2, 0)])  3.01 us
    ppermute x1, waiting for transfers between devices, on_device(): beside = lax.ppermute(left, ('col', 'layer'), along)  2.77 us
    ppermute x1, starting transfers between devices, on_device(): lax.ppermute(pair, ('col', 'layer'), across)  1.58 us
    ppermute x1, starting transfers between devices, on_device(): beside = lax.ppermute(left, ('col', 'layer'), along)  1.49 us
    ppermute x3, waiting for transfers between devices, on_device(): total = total + lax.ppermute(sums, ('row', 'layer'), pairs)  1.29 us
    ppermute x5, waiting for transfers between devices, swapped(): return lax.ppermute(value, axis, [(i, i ^ step) for i in range(count)])  1.23 us
  transfers between devices with their start and end apart: 14, of which 11 were waited for; matrix products, arithmetic and copies ran while one was open for 0% of the time, Pallas kernels for 3%

profile of v11, /device:TPU:0, one launch (start us, length us, event | category | flops | bytes accessed | tf_op | source)
XLA Modules:
  0.0 23.9 jit_solution(7466128295041086780)
XLA Ops:
  0.0 1.1 %tiles.1 = (bf16[128,512]{1,0:T(8,128)(2,1)S(1)}, bf16[256,128]{1,0:T(8,128)(2,1)S(1)}, s32[2,2]{1,0:T(2,128)S(1)}) custom-call(s32[1,4]{1,0:T(1,128)} %bitcast.8, bf16[128,512]{1,0:T(8,128)(2,1)} %bitcast.5, s32[1,2]{1,0:T(1,128)} %bitcast.9, bf16[256,128]{1,0:T(8,128)(2,1)} %bitcast.6, s32[2,2]{1,0:T(2,128)} %refs_4_.1), custom_call_target="tpu_custom_call" | custom-call | tf_op jit(solution)/shard_map/tiles/pallas_call | solution.py:54
  1.1 4.1 %collective-permute-start.2 = (bf16[128,512]{1,0:T(8,128)(2,1)S(1)}, bf16[128,512]{1,0:T(8,128)(2,1)S(1)}, u32[]{:S(2)}, u32[]{:S(2)}) collective-permute-start(bf16[128,512]{1,0:T(8,128)(2,1)S(1)} %get-tuple-element.19.refs_0_), channel_id=1, source_target_pairs={{0,16},{24,8},{8,0},{16,24},{1,17},{25,9},{9,1},{17,25},{2,18},{26... | collective-permute-start | bytes 393224 | tf_op jit(solution)/shard_map/ppermute | solution.py:215
  5.2 1.5 %collective-permute-start = (bf16[256,128]{1,0:T(8,128)(2,1)S(1)}, bf16[256,128]{1,0:T(8,128)(2,1)S(1)}, u32[]{:S(2)}, u32[]{:S(2)}) collective-permute-start(bf16[256,128]{1,0:T(8,128)(2,1)S(1)} %get-tuple-element.18.here), channel_id=1, source_target_pairs={{0,2},{1,5},{2,0},{3,7},{4,6},{5,1},{6,4},{7,3},{8,10},{9,13},{10,... | collective-permute-start | bytes 196616 | tf_op jit(solution)/shard_map/ppermute | solution.py:224
  6.7 2.8 %collective-permute-done.beside = bf16[256,128]{1,0:T(8,128)(2,1)S(1)} collective-permute-done((bf16[256,128]{1,0:T(8,128)(2,1)S(1)}, bf16[256,128]{1,0:T(8,128)(2,1)S(1)}, u32[]{:S(2)}, u32[]{:S(2)}) %collective-permute-start) | collective-permute-done | bytes 65568 | tf_op jit(solution)/shard_map/ppermute | solution.py:224
  9.5 1.6 %collective-permute-start.1 = (bf16[2,256,128]{2,1,0:T(8,128)(2,1)S(1)}, bf16[2,256,128]{2,1,0:T(8,128)(2,1)S(1)}, u32[]{:S(2)}, u32[]{:S(2)}) collective-permute-start(bf16[2,256,128]{2,1,0:T(8,128)(2,1)S(1)} %pair.1.near), channel_id=1, source_target_pairs={{0,4},{1,3},{2,6},{3,1},{4,0},{5,7},{6,2},{7,5},{8,12},{9,11},{10,... | collective-permute-start | bytes 393224 | tf_op jit(solution)/shard_map/ppermute | solution.py:242
  11.1 3.0 %collective-permute-done.3.refs_2_ = bf16[128,512]{1,0:T(8,128)(2,1)S(1)} collective-permute-done((bf16[128,512]{1,0:T(8,128)(2,1)S(1)}, bf16[128,512]{1,0:T(8,128)(2,1)S(1)}, u32[]{:S(2)}, u32[]{:S(2)}) %collective-permute-start.3) | collective-permute-done | bytes 131104 | tf_op jit(solution)/shard_map/ppermute | solution.py:216
  14.2 0.4 %collective-permute-done.1.far = bf16[2,256,128]{2,1,0:T(8,128)(2,1)S(1)} collective-permute-done((bf16[2,256,128]{2,1,0:T(8,128)(2,1)S(1)}, bf16[2,256,128]{2,1,0:T(8,128)(2,1)S(1)}, u32[]{:S(2)}, u32[]{:S(2)}) %collective-permute-start.1) | collective-permute-done | bytes 131104 | tf_op jit(solution)/shard_map/ppermute | solution.py:242
  14.5 0.3 %early.1 = (f32[328,128]{1,0:T(8,128)S(1)}, f32[328,128]{1,0:T(8,128)S(1)}, f32[328,128]{1,0:T(8,128)S(1)}, f32[328,128]{1,0:T(8,128)S(1)}, bf16[256,128]{1,0:T(8,128)(2,1)S(1)}) custom-call(bf16[2,256,128]{2,1,0:T(8,128)(2,1)S(1)} %pair.1.near, bf16[2,256,128]{2,1,0:T(8,128)(2,1)S(1)} %collective-permute-done.1.far, bf16[3,128,512]{2,1,0:T(8,128)(2,1)S(1)} %rights.1.after, ...), custom_call_target="tpu_custom_call" | custom-call | tf_op jit(solution)/shard_map/early/pallas_call | solution.py:68
  14.9 0.5 %collective-permute-start.6 = (f32[328,128]{1,0:T(8,128)S(1)}, f32[328,128]{1,0:T(8,128)S(1)}, u32[]{:S(2)}, u32[]{:S(2)}) collective-permute-start(f32[328,128]{1,0:T(8,128)S(1)} %get-tuple-element.22.refs_1_), channel_id=1, source_target_pairs={{0,1},{1,0},{2,3},{3,2},{4,5},{5,4},{6,7},{7,6},{8,9},{9,8},{10,11... | collective-permute-start | bytes 503816 | tf_op jit(solution)/shard_map/ppermute | solution.py:81
  15.5 0.4 %collective-permute-start.8 = (f32[328,128]{1,0:T(8,128)S(1)}, f32[328,128]{1,0:T(8,128)S(1)}, u32[]{:S(2)}, u32[]{:S(2)}) collective-permute-start(f32[328,128]{1,0:T(8,128)S(1)} %get-tuple-element.24.refs_3_), channel_id=1, source_target_pairs={{0,1},{1,0},{2,3},{3,2},{4,5},{5,4},{6,7},{7,6},{8,9},{9,8},{10,11... | collective-permute-start | bytes 503816 | tf_op jit(solution)/shard_map/ppermute | solution.py:81
  15.9 0.1 collective-permute-done.9.outer
  16.2 0.2 collective-permute-done.5.refs_5_
  16.3 0.2 %collective-permute-done.6.refs_6_ = f32[328,128]{1,0:T(8,128)S(1)} collective-permute-done((f32[328,128]{1,0:T(8,128)S(1)}, f32[328,128]{1,0:T(8,128)S(1)}, u32[]{:S(2)}, u32[]{:S(2)}) %collective-permute-start.6) | collective-permute-done | bytes 167968 | tf_op jit(solution)/shard_map/ppermute | solution.py:81
  16.6 0.3 %collective-permute-done.7.refs_7_ = f32[328,128]{1,0:T(8,128)S(1)} collective-permute-done((f32[328,128]{1,0:T(8,128)S(1)}, f32[328,128]{1,0:T(8,128)S(1)}, u32[]{:S(2)}, u32[]{:S(2)}) %collective-permute-start.7) | collective-permute-done | bytes 167968 | tf_op jit(solution)/shard_map/ppermute | solution.py:81
  16.8 0.2 %collective-permute-done.8.refs_8_ = f32[328,128]{1,0:T(8,128)S(1)} collective-permute-done((f32[328,128]{1,0:T(8,128)S(1)}, f32[328,128]{1,0:T(8,128)S(1)}, u32[]{:S(2)}, u32[]{:S(2)}) %collective-permute-start.8) | collective-permute-done | bytes 167968 | tf_op jit(solution)/shard_map/ppermute | solution.py:81
  17.2 0.3 %collective-permute-done.10.refs_4_ = bf16[128,512]{1,0:T(8,128)(2,1)S(1)} collective-permute-done((bf16[128,512]{1,0:T(8,128)(2,1)S(1)}, bf16[128,512]{1,0:T(8,128)(2,1)S(1)}, u32[]{:S(2)}, u32[]{:S(2)}) %collective-permute-start.10) | collective-permute-done | bytes 131104 | tf_op jit(solution)/shard_map/ppermute | solution.py:81
  17.5 0.2 sums.1
  17.7 1.5 %collective-permute-start.13 = (f32[1,256]{1,0:T(1,128)S(1)}, f32[1,256]{1,0:T(1,128)S(1)}, u32[]{:S(2)}, u32[]{:S(2)}) collective-permute-start(f32[1,256]{1,0:T(1,128)S(1)} %sums.1), channel_id=1, source_target_pairs={{0,25},{1,24},{8,17},{9,16},{16,9},{17,8},{24,1},{25,0},{2,27},{3,... | collective-permute-start | bytes 3080 | tf_op jit(solution)/shard_map/ppermute | solution.py:276
  19.2 0.8 %collective-permute-start.12 = (f32[1,256]{1,0:T(1,128)S(1)}, f32[1,256]{1,0:T(1,128)S(1)}, u32[]{:S(2)}, u32[]{:S(2)}) collective-permute-start(f32[1,256]{1,0:T(1,128)S(1)} %sums.1), channel_id=1, source_target_pairs={{0,17},{1,16},{8,25},{9,24},{16,1},{17,0},{24,9},{25,8},{2,19},{3,... | collective-permute-start | bytes 3080 | tf_op jit(solution)/shard_map/ppermute | solution.py:276
  20.0 1.6 %collective-permute-start.11 = (f32[1,256]{1,0:T(1,128)S(1)}, f32[1,256]{1,0:T(1,128)S(1)}, u32[]{:S(2)}, u32[]{:S(2)}) collective-permute-start(f32[1,256]{1,0:T(1,128)S(1)} %sums.1), channel_id=1, source_target_pairs={{0,9},{1,8},{8,1},{9,0},{16,25},{17,24},{24,17},{25,16},{2,11},{3,... | collective-permute-start | bytes 3080 | tf_op jit(solution)/shard_map/ppermute | solution.py:276
  21.6 0.2 inflate.1
  21.8 0.7 %collective-permute-done.13 = f32[1,256]{1,0:T(1,128)S(1)} collective-permute-done((f32[1,256]{1,0:T(1,128)S(1)}, f32[1,256]{1,0:T(1,128)S(1)}, u32[]{:S(2)}, u32[]{:S(2)}) %collective-permute-start.13) | collective-permute-done | bytes 1056 | tf_op jit(solution)/shard_map/ppermute | solution.py:276
  22.6 0.6 %collective-permute-done.12 = f32[1,256]{1,0:T(1,128)S(1)} collective-permute-done((f32[1,256]{1,0:T(1,128)S(1)}, f32[1,256]{1,0:T(1,128)S(1)}, u32[]{:S(2)}, u32[]{:S(2)}) %collective-permute-start.12) | collective-permute-done | bytes 1056 | tf_op jit(solution)/shard_map/ppermute | solution.py:276
  23.1 0.7 %broadcast_multiply_fusion = f32[256,256]{1,0:T(8,128)} fusion(f32[256,256]{1,0:T(8,128)S(1)} %get-tuple-element.29, f32[256]{0:T(256)S(1)} %bitcast.7), kind=kLoop, calls=%fused_computation | loop fusion | flops 65536 | bytes 525312 | tf_op jit(solution)/shard_map/mul | solution.py:277
  (15 shorter events, 0.4 us)
Async XLA Ops:
  1.1 10.0 %collective-permute-start.2 = (bf16[128,512]{1,0:T(8,128)(2,1)S(1)}, bf16[128,512]{1,0:T(8,128)(2,1)S(1)}, u32[]{:S(2)}, u32[]{:S(2)}) collective-permute-start(bf16[128,512]{1,0:T(8,128)(2,1)S(1)} %get-tuple-element.19.refs_0_), channel_id=1, source_target_pairs={{0,16},{24,8},{8,0},{16,24},{1,17},{25,9},{9,1},{17,25},{2,18},{26... | collective-permute-start | bytes 393224 | tf_op jit(solution)/shard_map/ppermute | solution.py:215
  5.2 4.3 %collective-permute-start = (bf16[256,128]{1,0:T(8,128)(2,1)S(1)}, bf16[256,128]{1,0:T(8,128)(2,1)S(1)}, u32[]{:S(2)}, u32[]{:S(2)}) collective-permute-start(bf16[256,128]{1,0:T(8,128)(2,1)S(1)} %get-tuple-element.18.here), channel_id=1, source_target_pairs={{0,2},{1,5},{2,0},{3,7},{4,6},{5,1},{6,4},{7,3},{8,10},{9,13},{10,... | collective-permute-start | bytes 196616 | tf_op jit(solution)/shard_map/ppermute | solution.py:224
  6.7 7.4 %collective-permute-start.3 = (bf16[128,512]{1,0:T(8,128)(2,1)S(1)}, bf16[128,512]{1,0:T(8,128)(2,1)S(1)}, u32[]{:S(2)}, u32[]{:S(2)}) collective-permute-start(bf16[128,512]{1,0:T(8,128)(2,1)S(1)} %get-tuple-element.19.refs_0_), channel_id=1, source_target_pairs={{0,8},{24,16},{8,24},{16,0},{1,9},{25,17},{9,25},{17,1},{2,10},{26... | collective-permute-start | bytes 393224 | tf_op jit(solution)/shard_map/ppermute | solution.py:216
  6.7 7.4 %collective-permute-start.4 = (bf16[128,512]{1,0:T(8,128)(2,1)S(1)}, bf16[128,512]{1,0:T(8,128)(2,1)S(1)}, u32[]{:S(2)}, u32[]{:S(2)}) collective-permute-start(bf16[128,512]{1,0:T(8,128)(2,1)S(1)} %get-tuple-element.19.refs_0_), channel_id=1, source_target_pairs={{8,17},{9,16},{16,9},{17,8},{0,1},{1,0},{24,25},{25,24},{10,19},{1... | collective-permute-start | bytes 393224 | tf_op jit(solution)/shard_map/ppermute | solution.py:218
  9.5 5.0 %collective-permute-start.1 = (bf16[2,256,128]{2,1,0:T(8,128)(2,1)S(1)}, bf16[2,256,128]{2,1,0:T(8,128)(2,1)S(1)}, u32[]{:S(2)}, u32[]{:S(2)}) collective-permute-start(bf16[2,256,128]{2,1,0:T(8,128)(2,1)S(1)} %pair.1.near), channel_id=1, source_target_pairs={{0,4},{1,3},{2,6},{3,1},{4,0},{5,7},{6,2},{7,5},{8,12},{9,11},{10,... | collective-permute-start | bytes 393224 | tf_op jit(solution)/shard_map/ppermute | solution.py:242
  11.1 5.0 %collective-permute-start.9 = (bf16[128,512]{1,0:T(8,128)(2,1)S(1)}, bf16[128,512]{1,0:T(8,128)(2,1)S(1)}, u32[]{:S(2)}, u32[]{:S(2)}) collective-permute-start(bf16[128,512]{1,0:T(8,128)(2,1)S(1)} %collective-permute-done.2.refs_1_), channel_id=1, source_target_pairs={{0,8},{8,0},{16,24},{24,16},{1,9},{9,1},{17,25},{25,17},{2,10},{10... | collective-permute-start | bytes 393224 | tf_op jit(solution)/shard_map/ppermute | solution.py:219
  14.8 1.5 %collective-permute-start.5 = (f32[328,128]{1,0:T(8,128)S(1)}, f32[328,128]{1,0:T(8,128)S(1)}, u32[]{:S(2)}, u32[]{:S(2)}) collective-permute-start(f32[328,128]{1,0:T(8,128)S(1)} %get-tuple-element.21.refs_0_), channel_id=1, source_target_pairs={{0,1},{1,0},{2,3},{3,2},{4,5},{5,4},{6,7},{7,6},{8,9},{9,8},{10,11... | collective-permute-start | bytes 503816 | tf_op jit(solution)/shard_map/ppermute | solution.py:81
  14.9 1.6 %collective-permute-start.6 = (f32[328,128]{1,0:T(8,128)S(1)}, f32[328,128]{1,0:T(8,128)S(1)}, u32[]{:S(2)}, u32[]{:S(2)}) collective-permute-start(f32[328,128]{1,0:T(8,128)S(1)} %get-tuple-element.22.refs_1_), channel_id=1, source_target_pairs={{0,1},{1,0},{2,3},{3,2},{4,5},{5,4},{6,7},{7,6},{8,9},{9,8},{10,11... | collective-permute-start | bytes 503816 | tf_op jit(solution)/shard_map/ppermute | solution.py:81
  15.4 1.4 %collective-permute-start.7 = (f32[328,128]{1,0:T(8,128)S(1)}, f32[328,128]{1,0:T(8,128)S(1)}, u32[]{:S(2)}, u32[]{:S(2)}) collective-permute-start(f32[328,128]{1,0:T(8,128)S(1)} %get-tuple-element.23.refs_2_), channel_id=1, source_target_pairs={{0,1},{1,0},{2,3},{3,2},{4,5},{5,4},{6,7},{7,6},{8,9},{9,8},{10,11... | collective-permute-start | bytes 503816 | tf_op jit(solution)/shard_map/ppermute | solution.py:81
  15.5 1.6 %collective-permute-start.8 = (f32[328,128]{1,0:T(8,128)S(1)}, f32[328,128]{1,0:T(8,128)S(1)}, u32[]{:S(2)}, u32[]{:S(2)}) collective-permute-start(f32[328,128]{1,0:T(8,128)S(1)} %get-tuple-element.24.refs_3_), channel_id=1, source_target_pairs={{0,1},{1,0},{2,3},{3,2},{4,5},{5,4},{6,7},{7,6},{8,9},{9,8},{10,11... | collective-permute-start | bytes 503816 | tf_op jit(solution)/shard_map/ppermute | solution.py:81
  16.1 1.4 %collective-permute-start.10 = (bf16[128,512]{1,0:T(8,128)(2,1)S(1)}, bf16[128,512]{1,0:T(8,128)(2,1)S(1)}, u32[]{:S(2)}, u32[]{:S(2)}) collective-permute-start(bf16[128,512]{1,0:T(8,128)(2,1)S(1)} %last.1.refs_3_), channel_id=1, source_target_pairs={{0,1},{1,0},{2,3},{3,2},{4,5},{5,4},{6,7},{7,6},{8,9},{9,8},{10,11... | collective-permute-start | bytes 393224 | tf_op jit(solution)/shard_map/ppermute | solution.py:81
  17.7 4.9 %collective-permute-start.13 = (f32[1,256]{1,0:T(1,128)S(1)}, f32[1,256]{1,0:T(1,128)S(1)}, u32[]{:S(2)}, u32[]{:S(2)}) collective-permute-start(f32[1,256]{1,0:T(1,128)S(1)} %sums.1), channel_id=1, source_target_pairs={{0,25},{1,24},{8,17},{9,16},{16,9},{17,8},{24,1},{25,0},{2,27},{3,... | collective-permute-start | bytes 3080 | tf_op jit(solution)/shard_map/ppermute | solution.py:276
  19.2 3.9 %collective-permute-start.12 = (f32[1,256]{1,0:T(1,128)S(1)}, f32[1,256]{1,0:T(1,128)S(1)}, u32[]{:S(2)}, u32[]{:S(2)}) collective-permute-start(f32[1,256]{1,0:T(1,128)S(1)} %sums.1), channel_id=1, source_target_pairs={{0,17},{1,16},{8,25},{9,24},{16,1},{17,0},{24,9},{25,8},{2,19},{3,... | collective-permute-start | bytes 3080 | tf_op jit(solution)/shard_map/ppermute | solution.py:276
  20.0 3.1 %collective-permute-start.11 = (f32[1,256]{1,0:T(1,128)S(1)}, f32[1,256]{1,0:T(1,128)S(1)}, u32[]{:S(2)}, u32[]{:S(2)}) collective-permute-start(f32[1,256]{1,0:T(1,128)S(1)} %sums.1), channel_id=1, source_target_pairs={{0,9},{1,8},{8,1},{9,0},{16,25},{17,24},{24,17},{25,16},{2,11},{3,... | collective-permute-start | bytes 3080 | tf_op jit(solution)/shard_map/ppermute | solution.py:276

commit v12 on v9

--- a/solution.py
+++ b/solution.py
@@ -216,7 +216,9 @@
     second = lax.ppermute(right, "row", [(0, 1), (3, 2), (1, 3), (2, 0)])
     pairs = [(2, 5), (3, 4), (4, 3), (5, 2), (0, 1), (1, 0), (6, 7), (7, 6)]
     inner = lax.ppermute(right, ("row", "layer"), pairs)
-    outer = lax.ppermute(first, "row", [(0, 1), (1, 0), (2, 3), (3, 2)])
+    pairs = [(2 * s + l, 2 * t + l) for s, t in ((1, 0), (2, 3)) for l in (0, 1)]
+    pairs += [(2 * s + l, 2 * t + 1 - l) for s, t in ((0, 1), (3, 2)) for l in (0, 1)]
+    outer = lax.ppermute(first, ("row", "layer"), pairs)
     along, across = (
         [(2 * c + core, 2 * (c ^ (2 if core == turn else 1)) + core) for c in range(4) for core in (0, 1)]
         for turn in (1, 0)

time: 24 us -> 24 us (level)
  no operation moved by 1% of the time
where the time goes in v12:
time: 24 us; the launch traced here: 23.8 us
  starting transfers between devices  12.3 us (51%)
  waiting for transfers between devices  8.8 us (37%)
  Pallas kernels  1.96 us (8%)
  other arithmetic  0.74 us (3%)
    ppermute x1, starting transfers between devices, on_device(): first = lax.ppermute(right, 'row', [(0, 2), (3, 1), (1, 0), (2, 3)])  4.09 us
    ppermute x3, starting transfers between devices, on_device(): total = total + lax.ppermute(sums, ('row', 'layer'), pairs)  3.93 us
    ppermute x1, waiting for transfers between devices, on_device(): second = lax.ppermute(right, 'row', [(0, 1), (3, 2), (1, 3), (2, 0)])  3.01 us
    ppermute x1, waiting for transfers between devices, on_device(): beside = lax.ppermute(left, ('col', 'layer'), along)  2.77 us
    ppermute x1, starting transfers between devices, on_device(): lax.ppermute(pair, ('col', 'layer'), across)  1.58 us
    ppermute x1, starting transfers between devices, on_device(): beside = lax.ppermute(left, ('col', 'layer'), along)  1.49 us
    ppermute x3, waiting for transfers between devices, on_device(): total = total + lax.ppermute(sums, ('row', 'layer'), pairs)  1.28 us
    ppermute x5, waiting for transfers between devices, swapped(): return lax.ppermute(value, axis, [(i, i ^ step) for i in range(count)])  1.23 us
  transfers between devices with their start and end apart: 14, of which 11 were waited for; matrix products, arithmetic and copies ran while one was open for 0% of the time, Pallas kernels for 3%

profile of v12, /device:TPU:0, one launch (start us, length us, event | category | flops | bytes accessed | tf_op | source)
XLA Modules:
  0.0 23.8 jit_solution(13558811455514104599)
XLA Ops:
  0.0 1.1 %tiles.1 = (bf16[128,512]{1,0:T(8,128)(2,1)S(1)}, bf16[256,128]{1,0:T(8,128)(2,1)S(1)}, s32[2,2]{1,0:T(2,128)S(1)}) custom-call(s32[1,4]{1,0:T(1,128)} %bitcast.8, bf16[128,512]{1,0:T(8,128)(2,1)} %bitcast.5, s32[1,2]{1,0:T(1,128)} %bitcast.9, bf16[256,128]{1,0:T(8,128)(2,1)} %bitcast.6, s32[2,2]{1,0:T(2,128)} %refs_4_.1), custom_call_target="tpu_custom_call" | custom-call | tf_op jit(solution)/shard_map/tiles/pallas_call | solution.py:54
  1.1 4.1 %collective-permute-start.2 = (bf16[128,512]{1,0:T(8,128)(2,1)S(1)}, bf16[128,512]{1,0:T(8,128)(2,1)S(1)}, u32[]{:S(2)}, u32[]{:S(2)}) collective-permute-start(bf16[128,512]{1,0:T(8,128)(2,1)S(1)} %get-tuple-element.19.refs_0_), channel_id=1, source_target_pairs={{0,16},{24,8},{8,0},{16,24},{1,17},{25,9},{9,1},{17,25},{2,18},{26... | collective-permute-start | bytes 393224 | tf_op jit(solution)/shard_map/ppermute | solution.py:215
  5.2 1.5 %collective-permute-start = (bf16[256,128]{1,0:T(8,128)(2,1)S(1)}, bf16[256,128]{1,0:T(8,128)(2,1)S(1)}, u32[]{:S(2)}, u32[]{:S(2)}) collective-permute-start(bf16[256,128]{1,0:T(8,128)(2,1)S(1)} %get-tuple-element.18.here), channel_id=1, source_target_pairs={{0,2},{1,5},{2,0},{3,7},{4,6},{5,1},{6,4},{7,3},{8,10},{9,13},{10,... | collective-permute-start | bytes 196616 | tf_op jit(solution)/shard_map/ppermute | solution.py:226
  6.7 2.8 %collective-permute-done.beside = bf16[256,128]{1,0:T(8,128)(2,1)S(1)} collective-permute-done((bf16[256,128]{1,0:T(8,128)(2,1)S(1)}, bf16[256,128]{1,0:T(8,128)(2,1)S(1)}, u32[]{:S(2)}, u32[]{:S(2)}) %collective-permute-start) | collective-permute-done | bytes 65568 | tf_op jit(solution)/shard_map/ppermute | solution.py:226
  9.5 1.6 %collective-permute-start.1 = (bf16[2,256,128]{2,1,0:T(8,128)(2,1)S(1)}, bf16[2,256,128]{2,1,0:T(8,128)(2,1)S(1)}, u32[]{:S(2)}, u32[]{:S(2)}) collective-permute-start(bf16[2,256,128]{2,1,0:T(8,128)(2,1)S(1)} %pair.1.near), channel_id=1, source_target_pairs={{0,4},{1,3},{2,6},{3,1},{4,0},{5,7},{6,2},{7,5},{8,12},{9,11},{10,... | collective-permute-start | bytes 393224 | tf_op jit(solution)/shard_map/ppermute | solution.py:244
  11.1 3.0 %collective-permute-done.3.refs_2_ = bf16[128,512]{1,0:T(8,128)(2,1)S(1)} collective-permute-done((bf16[128,512]{1,0:T(8,128)(2,1)S(1)}, bf16[128,512]{1,0:T(8,128)(2,1)S(1)}, u32[]{:S(2)}, u32[]{:S(2)}) %collective-permute-start.3) | collective-permute-done | bytes 131104 | tf_op jit(solution)/shard_map/ppermute | solution.py:216
  14.1 0.4 %collective-permute-done.1.far = bf16[2,256,128]{2,1,0:T(8,128)(2,1)S(1)} collective-permute-done((bf16[2,256,128]{2,1,0:T(8,128)(2,1)S(1)}, bf16[2,256,128]{2,1,0:T(8,128)(2,1)S(1)}, u32[]{:S(2)}, u32[]{:S(2)}) %collective-permute-start.1) | collective-permute-done | bytes 131104 | tf_op jit(solution)/shard_map/ppermute | solution.py:244
  14.5 0.3 %early.1 = (f32[328,128]{1,0:T(8,128)S(1)}, f32[328,128]{1,0:T(8,128)S(1)}, f32[328,128]{1,0:T(8,128)S(1)}, f32[328,128]{1,0:T(8,128)S(1)}, bf16[256,128]{1,0:T(8,128)(2,1)S(1)}) custom-call(bf16[2,256,128]{2,1,0:T(8,128)(2,1)S(1)} %pair.1.near, bf16[2,256,128]{2,1,0:T(8,128)(2,1)S(1)} %collective-permute-done.1.far, bf16[3,128,512]{2,1,0:T(8,128)(2,1)S(1)} %rights.1.after, ...), custom_call_target="tpu_custom_call" | custom-call | tf_op jit(solution)/shard_map/early/pallas_call | solution.py:68
  14.9 0.5 %collective-permute-start.6 = (f32[328,128]{1,0:T(8,128)S(1)}, f32[328,128]{1,0:T(8,128)S(1)}, u32[]{:S(2)}, u32[]{:S(2)}) collective-permute-start(f32[328,128]{1,0:T(8,128)S(1)} %get-tuple-element.22.refs_1_), channel_id=1, source_target_pairs={{0,1},{1,0},{2,3},{3,2},{4,5},{5,4},{6,7},{7,6},{8,9},{9,8},{10,11... | collective-permute-start | bytes 503816 | tf_op jit(solution)/shard_map/ppermute | solution.py:81
  15.5 0.4 %collective-permute-start.8 = (f32[328,128]{1,0:T(8,128)S(1)}, f32[328,128]{1,0:T(8,128)S(1)}, u32[]{:S(2)}, u32[]{:S(2)}) collective-permute-start(f32[328,128]{1,0:T(8,128)S(1)} %get-tuple-element.24.refs_3_), channel_id=1, source_target_pairs={{0,1},{1,0},{2,3},{3,2},{4,5},{5,4},{6,7},{7,6},{8,9},{9,8},{10,11... | collective-permute-start | bytes 503816 | tf_op jit(solution)/shard_map/ppermute | solution.py:81
  15.9 0.1 collective-permute-done.9.outer
  16.1 0.2 collective-permute-done.5.refs_5_
  16.3 0.2 %collective-permute-done.6.refs_6_ = f32[328,128]{1,0:T(8,128)S(1)} collective-permute-done((f32[328,128]{1,0:T(8,128)S(1)}, f32[328,128]{1,0:T(8,128)S(1)}, u32[]{:S(2)}, u32[]{:S(2)}) %collective-permute-start.6) | collective-permute-done | bytes 167968 | tf_op jit(solution)/shard_map/ppermute | solution.py:81
  16.5 0.3 %collective-permute-done.7.refs_7_ = f32[328,128]{1,0:T(8,128)S(1)} collective-permute-done((f32[328,128]{1,0:T(8,128)S(1)}, f32[328,128]{1,0:T(8,128)S(1)}, u32[]{:S(2)}, u32[]{:S(2)}) %collective-permute-start.7) | collective-permute-done | bytes 167968 | tf_op jit(solution)/shard_map/ppermute | solution.py:81
  16.8 0.2 %collective-permute-done.8.refs_8_ = f32[328,128]{1,0:T(8,128)S(1)} collective-permute-done((f32[328,128]{1,0:T(8,128)S(1)}, f32[328,128]{1,0:T(8,128)S(1)}, u32[]{:S(2)}, u32[]{:S(2)}) %collective-permute-start.8) | collective-permute-done | bytes 167968 | tf_op jit(solution)/shard_map/ppermute | solution.py:81
  17.1 0.3 %collective-permute-done.10.refs_4_ = bf16[128,512]{1,0:T(8,128)(2,1)S(1)} collective-permute-done((bf16[128,512]{1,0:T(8,128)(2,1)S(1)}, bf16[128,512]{1,0:T(8,128)(2,1)S(1)}, u32[]{:S(2)}, u32[]{:S(2)}) %collective-permute-start.10) | collective-permute-done | bytes 131104 | tf_op jit(solution)/shard_map/ppermute | solution.py:81
  17.5 0.2 sums.1
  17.7 1.5 %collective-permute-start.13 = (f32[1,256]{1,0:T(1,128)S(1)}, f32[1,256]{1,0:T(1,128)S(1)}, u32[]{:S(2)}, u32[]{:S(2)}) collective-permute-start(f32[1,256]{1,0:T(1,128)S(1)} %sums.1), channel_id=1, source_target_pairs={{0,25},{1,24},{8,17},{9,16},{16,9},{17,8},{24,1},{25,0},{2,27},{3,... | collective-permute-start | bytes 3080 | tf_op jit(solution)/shard_map/ppermute | solution.py:278
  19.2 0.7 %collective-permute-start.12 = (f32[1,256]{1,0:T(1,128)S(1)}, f32[1,256]{1,0:T(1,128)S(1)}, u32[]{:S(2)}, u32[]{:S(2)}) collective-permute-start(f32[1,256]{1,0:T(1,128)S(1)} %sums.1), channel_id=1, source_target_pairs={{0,17},{1,16},{8,25},{9,24},{16,1},{17,0},{24,9},{25,8},{2,19},{3,... | collective-permute-start | bytes 3080 | tf_op jit(solution)/shard_map/ppermute | solution.py:278
  19.9 1.7 %collective-permute-start.11 = (f32[1,256]{1,0:T(1,128)S(1)}, f32[1,256]{1,0:T(1,128)S(1)}, u32[]{:S(2)}, u32[]{:S(2)}) collective-permute-start(f32[1,256]{1,0:T(1,128)S(1)} %sums.1), channel_id=1, source_target_pairs={{0,9},{1,8},{8,1},{9,0},{16,25},{17,24},{24,17},{25,16},{2,11},{3,... | collective-permute-start | bytes 3080 | tf_op jit(solution)/shard_map/ppermute | solution.py:278
  21.6 0.2 inflate.1
  21.8 0.7 %collective-permute-done.13 = f32[1,256]{1,0:T(1,128)S(1)} collective-permute-done((f32[1,256]{1,0:T(1,128)S(1)}, f32[1,256]{1,0:T(1,128)S(1)}, u32[]{:S(2)}, u32[]{:S(2)}) %collective-permute-start.13) | collective-permute-done | bytes 1056 | tf_op jit(solution)/shard_map/ppermute | solution.py:278
  22.5 0.6 %collective-permute-done.12 = f32[1,256]{1,0:T(1,128)S(1)} collective-permute-done((f32[1,256]{1,0:T(1,128)S(1)}, f32[1,256]{1,0:T(1,128)S(1)}, u32[]{:S(2)}, u32[]{:S(2)}) %collective-permute-start.12) | collective-permute-done | bytes 1056 | tf_op jit(solution)/shard_map/ppermute | solution.py:278
  23.1 0.7 %broadcast_multiply_fusion = f32[256,256]{1,0:T(8,128)} fusion(f32[256,256]{1,0:T(8,128)S(1)} %get-tuple-element.29, f32[256]{0:T(256)S(1)} %bitcast.7), kind=kLoop, calls=%fused_computation | loop fusion | flops 65536 | bytes 525312 | tf_op jit(solution)/shard_map/mul | solution.py:279
  (15 shorter events, 0.4 us)
Async XLA Ops:
  1.1 10.0 %collective-permute-start.2 = (bf16[128,512]{1,0:T(8,128)(2,1)S(1)}, bf16[128,512]{1,0:T(8,128)(2,1)S(1)}, u32[]{:S(2)}, u32[]{:S(2)}) collective-permute-start(bf16[128,512]{1,0:T(8,128)(2,1)S(1)} %get-tuple-element.19.refs_0_), channel_id=1, source_target_pairs={{0,16},{24,8},{8,0},{16,24},{1,17},{25,9},{9,1},{17,25},{2,18},{26... | collective-permute-start | bytes 393224 | tf_op jit(solution)/shard_map/ppermute | solution.py:215
  5.2 4.3 %collective-permute-start = (bf16[256,128]{1,0:T(8,128)(2,1)S(1)}, bf16[256,128]{1,0:T(8,128)(2,1)S(1)}, u32[]{:S(2)}, u32[]{:S(2)}) collective-permute-start(bf16[256,128]{1,0:T(8,128)(2,1)S(1)} %get-tuple-element.18.here), channel_id=1, source_target_pairs={{0,2},{1,5},{2,0},{3,7},{4,6},{5,1},{6,4},{7,3},{8,10},{9,13},{10,... | collective-permute-start | bytes 196616 | tf_op jit(solution)/shard_map/ppermute | solution.py:226
  6.7 7.4 %collective-permute-start.3 = (bf16[128,512]{1,0:T(8,128)(2,1)S(1)}, bf16[128,512]{1,0:T(8,128)(2,1)S(1)}, u32[]{:S(2)}, u32[]{:S(2)}) collective-permute-start(bf16[128,512]{1,0:T(8,128)(2,1)S(1)} %get-tuple-element.19.refs_0_), channel_id=1, source_target_pairs={{0,8},{24,16},{8,24},{16,0},{1,9},{25,17},{9,25},{17,1},{2,10},{26... | collective-permute-start | bytes 393224 | tf_op jit(solution)/shard_map/ppermute | solution.py:216
  6.7 7.4 %collective-permute-start.4 = (bf16[128,512]{1,0:T(8,128)(2,1)S(1)}, bf16[128,512]{1,0:T(8,128)(2,1)S(1)}, u32[]{:S(2)}, u32[]{:S(2)}) collective-permute-start(bf16[128,512]{1,0:T(8,128)(2,1)S(1)} %get-tuple-element.19.refs_0_), channel_id=1, source_target_pairs={{8,17},{9,16},{16,9},{17,8},{0,1},{1,0},{24,25},{25,24},{10,19},{1... | collective-permute-start | bytes 393224 | tf_op jit(solution)/shard_map/ppermute | solution.py:218
  9.5 5.0 %collective-permute-start.1 = (bf16[2,256,128]{2,1,0:T(8,128)(2,1)S(1)}, bf16[2,256,128]{2,1,0:T(8,128)(2,1)S(1)}, u32[]{:S(2)}, u32[]{:S(2)}) collective-permute-start(bf16[2,256,128]{2,1,0:T(8,128)(2,1)S(1)} %pair.1.near), channel_id=1, source_target_pairs={{0,4},{1,3},{2,6},{3,1},{4,0},{5,7},{6,2},{7,5},{8,12},{9,11},{10,... | collective-permute-start | bytes 393224 | tf_op jit(solution)/shard_map/ppermute | solution.py:244
  11.1 5.0 %collective-permute-start.9 = (bf16[128,512]{1,0:T(8,128)(2,1)S(1)}, bf16[128,512]{1,0:T(8,128)(2,1)S(1)}, u32[]{:S(2)}, u32[]{:S(2)}) collective-permute-start(bf16[128,512]{1,0:T(8,128)(2,1)S(1)} %collective-permute-done.2.refs_1_), channel_id=1, source_target_pairs={{8,0},{9,1},{16,24},{17,25},{0,9},{1,8},{24,17},{25,16},{10,2},{11... | collective-permute-start | bytes 393224 | tf_op jit(solution)/shard_map/ppermute | solution.py:221
  14.8 1.5 %collective-permute-start.5 = (f32[328,128]{1,0:T(8,128)S(1)}, f32[328,128]{1,0:T(8,128)S(1)}, u32[]{:S(2)}, u32[]{:S(2)}) collective-permute-start(f32[328,128]{1,0:T(8,128)S(1)} %get-tuple-element.21.refs_0_), channel_id=1, source_target_pairs={{0,1},{1,0},{2,3},{3,2},{4,5},{5,4},{6,7},{7,6},{8,9},{9,8},{10,11... | collective-permute-start | bytes 503816 | tf_op jit(solution)/shard_map/ppermute | solution.py:81
  14.9 1.6 %collective-permute-start.6 = (f32[328,128]{1,0:T(8,128)S(1)}, f32[328,128]{1,0:T(8,128)S(1)}, u32[]{:S(2)}, u32[]{:S(2)}) collective-permute-start(f32[328,128]{1,0:T(8,128)S(1)} %get-tuple-element.22.refs_1_), channel_id=1, source_target_pairs={{0,1},{1,0},{2,3},{3,2},{4,5},{5,4},{6,7},{7,6},{8,9},{9,8},{10,11... | collective-permute-start | bytes 503816 | tf_op jit(solution)/shard_map/ppermute | solution.py:81
  15.4 1.4 %collective-permute-start.7 = (f32[328,128]{1,0:T(8,128)S(1)}, f32[328,128]{1,0:T(8,128)S(1)}, u32[]{:S(2)}, u32[]{:S(2)}) collective-permute-start(f32[328,128]{1,0:T(8,128)S(1)} %get-tuple-element.23.refs_2_), channel_id=1, source_target_pairs={{0,1},{1,0},{2,3},{3,2},{4,5},{5,4},{6,7},{7,6},{8,9},{9,8},{10,11... | collective-permute-start | bytes 503816 | tf_op jit(solution)/shard_map/ppermute | solution.py:81
  15.5 1.6 %collective-permute-start.8 = (f32[328,128]{1,0:T(8,128)S(1)}, f32[328,128]{1,0:T(8,128)S(1)}, u32[]{:S(2)}, u32[]{:S(2)}) collective-permute-start(f32[328,128]{1,0:T(8,128)S(1)} %get-tuple-element.24.refs_3_), channel_id=1, source_target_pairs={{0,1},{1,0},{2,3},{3,2},{4,5},{5,4},{6,7},{7,6},{8,9},{9,8},{10,11... | collective-permute-start | bytes 503816 | tf_op jit(solution)/shard_map/ppermute | solution.py:81
  16.0 1.4 %collective-permute-start.10 = (bf16[128,512]{1,0:T(8,128)(2,1)S(1)}, bf16[128,512]{1,0:T(8,128)(2,1)S(1)}, u32[]{:S(2)}, u32[]{:S(2)}) collective-permute-start(bf16[128,512]{1,0:T(8,128)(2,1)S(1)} %last.1.refs_3_), channel_id=1, source_target_pairs={{0,1},{1,0},{2,3},{3,2},{4,5},{5,4},{6,7},{7,6},{8,9},{9,8},{10,11... | collective-permute-start | bytes 393224 | tf_op jit(solution)/shard_map/ppermute | solution.py:81
  17.7 4.9 %collective-permute-start.13 = (f32[1,256]{1,0:T(1,128)S(1)}, f32[1,256]{1,0:T(1,128)S(1)}, u32[]{:S(2)}, u32[]{:S(2)}) collective-permute-start(f32[1,256]{1,0:T(1,128)S(1)} %sums.1), channel_id=1, source_target_pairs={{0,25},{1,24},{8,17},{9,16},{16,9},{17,8},{24,1},{25,0},{2,27},{3,... | collective-permute-start | bytes 3080 | tf_op jit(solution)/shard_map/ppermute | solution.py:278
  19.2 3.9 %collective-permute-start.12 = (f32[1,256]{1,0:T(1,128)S(1)}, f32[1,256]{1,0:T(1,128)S(1)}, u32[]{:S(2)}, u32[]{:S(2)}) collective-permute-start(f32[1,256]{1,0:T(1,128)S(1)} %sums.1), channel_id=1, source_target_pairs={{0,17},{1,16},{8,25},{9,24},{16,1},{17,0},{24,9},{25,8},{2,19},{3,... | collective-permute-start | bytes 3080 | tf_op jit(solution)/shard_map/ppermute | solution.py:278
  19.9 3.2 %collective-permute-start.11 = (f32[1,256]{1,0:T(1,128)S(1)}, f32[1,256]{1,0:T(1,128)S(1)}, u32[]{:S(2)}, u32[]{:S(2)}) collective-permute-start(f32[1,256]{1,0:T(1,128)S(1)} %sums.1), channel_id=1, source_target_pairs={{0,9},{1,8},{8,1},{9,0},{16,25},{17,24},{24,17},{25,16},{2,11},{3,... | collective-permute-start | bytes 3080 | tf_op jit(solution)/shard_map/ppermute | solution.py:278

commit v13 on v9

--- a/solution.py
+++ b/solution.py
@@ -232,6 +232,8 @@
     part = jax.ShapeDtypeStruct((rows + (tall + 7) // 8 * 8 + share, columns // parts), f32)
     block = jax.ShapeDtypeStruct(right.shape, right.dtype)
     rights = jax.ShapeDtypeStruct((3,) + right.shape, right.dtype)
+    for _ in range(2):
+        second = call(hand_kernel, "second", block, second, second)
     rights = call(stack_kernel, "rights", rights, right, first, second)
     handed = call(hand_kernel, "inner", block, inner, rights)
     ours = call(

time: 24 us -> 24 us (level)
    pallas_call x8 -> x10, Pallas kernels: 0.86 us -> 0.89 us  [call(): pl.pallas_call(kernel, out_shape=shapes, in_specs=[VMEM] * len(operands),...]
where the time goes in v13:
time: 24 us; the launch traced here: 23.8 us
  starting transfers between devices  12.3 us (51%)
  waiting for transfers between devices  8.75 us (36%)
  Pallas kernels  1.99 us (8%)
  other arithmetic  0.74 us (3%)
    ppermute x1, starting transfers between devices, on_device(): first = lax.ppermute(right, 'row', [(0, 2), (3, 1), (1, 0), (2, 3)])  4.09 us
    ppermute x3, starting transfers between devices, on_device(): total = total + lax.ppermute(sums, ('row', 'layer'), pairs)  3.93 us
    ppermute x1, waiting for transfers between devices, on_device(): second = lax.ppermute(right, 'row', [(0, 1), (3, 2), (1, 3), (2, 0)])  3.01 us
    ppermute x1, waiting for transfers between devices, on_device(): beside = lax.ppermute(left, ('col', 'layer'), along)  2.77 us
    ppermute x1, starting transfers between devices, on_device(): lax.ppermute(pair, ('col', 'layer'), across)  1.58 us
    ppermute x1, starting transfers between devices, on_device(): beside = lax.ppermute(left, ('col', 'layer'), along)  1.49 us
    ppermute x3, waiting for transfers between devices, on_device(): total = total + lax.ppermute(sums, ('row', 'layer'), pairs)  1.28 us
    ppermute x5, waiting for transfers between devices, swapped(): return lax.ppermute(value, axis, [(i, i ^ step) for i in range(count)])  1.23 us
  transfers between devices with their start and end apart: 14, of which 11 were waited for; matrix products, arithmetic and copies ran while one was open for 0% of the time, Pallas kernels for 3%

profile of v13, /device:TPU:0, one launch (start us, length us, event | category | flops | bytes accessed | tf_op | source)
XLA Modules:
  0.0 23.8 jit_solution(11149044921652165956)
XLA Ops:
  0.0 1.1 %tiles.1 = (bf16[128,512]{1,0:T(8,128)(2,1)S(1)}, bf16[256,128]{1,0:T(8,128)(2,1)S(1)}, s32[2,2]{1,0:T(2,128)S(1)}) custom-call(s32[1,4]{1,0:T(1,128)} %bitcast.8, bf16[128,512]{1,0:T(8,128)(2,1)} %bitcast.5, s32[1,2]{1,0:T(1,128)} %bitcast.9, bf16[256,128]{1,0:T(8,128)(2,1)} %bitcast.6, s32[2,2]{1,0:T(2,128)} %refs_4_.1), custom_call_target="tpu_custom_call" | custom-call | tf_op jit(solution)/shard_map/tiles/pallas_call | solution.py:54
  1.1 4.1 %collective-permute-start.2 = (bf16[128,512]{1,0:T(8,128)(2,1)S(1)}, bf16[128,512]{1,0:T(8,128)(2,1)S(1)}, u32[]{:S(2)}, u32[]{:S(2)}) collective-permute-start(bf16[128,512]{1,0:T(8,128)(2,1)S(1)} %get-tuple-element.19.refs_0_), channel_id=1, source_target_pairs={{0,16},{24,8},{8,0},{16,24},{1,17},{25,9},{9,1},{17,25},{2,18},{26... | collective-permute-start | bytes 393224 | tf_op jit(solution)/shard_map/ppermute | solution.py:215
  5.2 1.5 %collective-permute-start = (bf16[256,128]{1,0:T(8,128)(2,1)S(1)}, bf16[256,128]{1,0:T(8,128)(2,1)S(1)}, u32[]{:S(2)}, u32[]{:S(2)}) collective-permute-start(bf16[256,128]{1,0:T(8,128)(2,1)S(1)} %get-tuple-element.18.here), channel_id=1, source_target_pairs={{0,2},{1,5},{2,0},{3,7},{4,6},{5,1},{6,4},{7,3},{8,10},{9,13},{10,... | collective-permute-start | bytes 196616 | tf_op jit(solution)/shard_map/ppermute | solution.py:224
  6.7 2.8 %collective-permute-done.beside = bf16[256,128]{1,0:T(8,128)(2,1)S(1)} collective-permute-done((bf16[256,128]{1,0:T(8,128)(2,1)S(1)}, bf16[256,128]{1,0:T(8,128)(2,1)S(1)}, u32[]{:S(2)}, u32[]{:S(2)}) %collective-permute-start) | collective-permute-done | bytes 65568 | tf_op jit(solution)/shard_map/ppermute | solution.py:224
  9.5 1.6 %collective-permute-start.1 = (bf16[2,256,128]{2,1,0:T(8,128)(2,1)S(1)}, bf16[2,256,128]{2,1,0:T(8,128)(2,1)S(1)}, u32[]{:S(2)}, u32[]{:S(2)}) collective-permute-start(bf16[2,256,128]{2,1,0:T(8,128)(2,1)S(1)} %pair.1.near), channel_id=1, source_target_pairs={{0,4},{1,3},{2,6},{3,1},{4,0},{5,7},{6,2},{7,5},{8,12},{9,11},{10,... | collective-permute-start | bytes 393224 | tf_op jit(solution)/shard_map/ppermute | solution.py:244
  11.1 3.0 %collective-permute-done.3.block.after = bf16[128,512]{1,0:T(8,128)(2,1)S(1)} collective-permute-done((bf16[128,512]{1,0:T(8,128)(2,1)S(1)}, bf16[128,512]{1,0:T(8,128)(2,1)S(1)}, u32[]{:S(2)}, u32[]{:S(2)}) %collective-permute-start.3) | collective-permute-done | bytes 131104 | tf_op jit(solution)/shard_map/ppermute | solution.py:216
  14.2 0.3 %collective-permute-done.1.far = bf16[2,256,128]{2,1,0:T(8,128)(2,1)S(1)} collective-permute-done((bf16[2,256,128]{2,1,0:T(8,128)(2,1)S(1)}, bf16[2,256,128]{2,1,0:T(8,128)(2,1)S(1)}, u32[]{:S(2)}, u32[]{:S(2)}) %collective-permute-start.1) | collective-permute-done | bytes 131104 | tf_op jit(solution)/shard_map/ppermute | solution.py:244
  14.5 0.3 %early.1 = (f32[328,128]{1,0:T(8,128)S(1)}, f32[328,128]{1,0:T(8,128)S(1)}, f32[328,128]{1,0:T(8,128)S(1)}, f32[328,128]{1,0:T(8,128)S(1)}, bf16[256,128]{1,0:T(8,128)(2,1)S(1)}) custom-call(bf16[2,256,128]{2,1,0:T(8,128)(2,1)S(1)} %pair.1.near, bf16[2,256,128]{2,1,0:T(8,128)(2,1)S(1)} %collective-permute-done.1.far, bf16[3,128,512]{2,1,0:T(8,128)(2,1)S(1)} %rights.1.after, ...), custom_call_target="tpu_custom_call" | custom-call | tf_op jit(solution)/shard_map/early/pallas_call | solution.py:68
  14.9 0.5 %collective-permute-start.6 = (f32[328,128]{1,0:T(8,128)S(1)}, f32[328,128]{1,0:T(8,128)S(1)}, u32[]{:S(2)}, u32[]{:S(2)}) collective-permute-start(f32[328,128]{1,0:T(8,128)S(1)} %get-tuple-element.22.refs_1_), channel_id=1, source_target_pairs={{0,1},{1,0},{2,3},{3,2},{4,5},{5,4},{6,7},{7,6},{8,9},{9,8},{10,11... | collective-permute-start | bytes 503816 | tf_op jit(solution)/shard_map/ppermute | solution.py:81
  15.5 0.4 %collective-permute-start.8 = (f32[328,128]{1,0:T(8,128)S(1)}, f32[328,128]{1,0:T(8,128)S(1)}, u32[]{:S(2)}, u32[]{:S(2)}) collective-permute-start(f32[328,128]{1,0:T(8,128)S(1)} %get-tuple-element.24.refs_3_), channel_id=1, source_target_pairs={{0,1},{1,0},{2,3},{3,2},{4,5},{5,4},{6,7},{7,6},{8,9},{9,8},{10,11... | collective-permute-start | bytes 503816 | tf_op jit(solution)/shard_map/ppermute | solution.py:81
  15.9 0.1 collective-permute-done.9.outer
  16.1 0.2 collective-permute-done.5.refs_5_
  16.3 0.2 %collective-permute-done.6.refs_6_ = f32[328,128]{1,0:T(8,128)S(1)} collective-permute-done((f32[328,128]{1,0:T(8,128)S(1)}, f32[328,128]{1,0:T(8,128)S(1)}, u32[]{:S(2)}, u32[]{:S(2)}) %collective-permute-start.6) | collective-permute-done | bytes 167968 | tf_op jit(solution)/shard_map/ppermute | solution.py:81
  16.5 0.3 %collective-permute-done.7.refs_7_ = f32[328,128]{1,0:T(8,128)S(1)} collective-permute-done((f32[328,128]{1,0:T(8,128)S(1)}, f32[328,128]{1,0:T(8,128)S(1)}, u32[]{:S(2)}, u32[]{:S(2)}) %collective-permute-start.7) | collective-permute-done | bytes 167968 | tf_op jit(solution)/shard_map/ppermute | solution.py:81
  16.8 0.2 %collective-permute-done.8.refs_8_ = f32[328,128]{1,0:T(8,128)S(1)} collective-permute-done((f32[328,128]{1,0:T(8,128)S(1)}, f32[328,128]{1,0:T(8,128)S(1)}, u32[]{:S(2)}, u32[]{:S(2)}) %collective-permute-start.8) | collective-permute-done | bytes 167968 | tf_op jit(solution)/shard_map/ppermute | solution.py:81
  17.1 0.3 %collective-permute-done.10.refs_4_ = bf16[128,512]{1,0:T(8,128)(2,1)S(1)} collective-permute-done((bf16[128,512]{1,0:T(8,128)(2,1)S(1)}, bf16[128,512]{1,0:T(8,128)(2,1)S(1)}, u32[]{:S(2)}, u32[]{:S(2)}) %collective-permute-start.10) | collective-permute-done | bytes 131104 | tf_op jit(solution)/shard_map/ppermute | solution.py:81
  17.5 0.2 sums.1
  17.7 1.5 %collective-permute-start.13 = (f32[1,256]{1,0:T(1,128)S(1)}, f32[1,256]{1,0:T(1,128)S(1)}, u32[]{:S(2)}, u32[]{:S(2)}) collective-permute-start(f32[1,256]{1,0:T(1,128)S(1)} %sums.1), channel_id=1, source_target_pairs={{0,25},{1,24},{8,17},{9,16},{16,9},{17,8},{24,1},{25,0},{2,27},{3,... | collective-permute-start | bytes 3080 | tf_op jit(solution)/shard_map/ppermute | solution.py:278
  19.2 0.8 %collective-permute-start.12 = (f32[1,256]{1,0:T(1,128)S(1)}, f32[1,256]{1,0:T(1,128)S(1)}, u32[]{:S(2)}, u32[]{:S(2)}) collective-permute-start(f32[1,256]{1,0:T(1,128)S(1)} %sums.1), channel_id=1, source_target_pairs={{0,17},{1,16},{8,25},{9,24},{16,1},{17,0},{24,9},{25,8},{2,19},{3,... | collective-permute-start | bytes 3080 | tf_op jit(solution)/shard_map/ppermute | solution.py:278
  20.0 1.6 %collective-permute-start.11 = (f32[1,256]{1,0:T(1,128)S(1)}, f32[1,256]{1,0:T(1,128)S(1)}, u32[]{:S(2)}, u32[]{:S(2)}) collective-permute-start(f32[1,256]{1,0:T(1,128)S(1)} %sums.1), channel_id=1, source_target_pairs={{0,9},{1,8},{8,1},{9,0},{16,25},{17,24},{24,17},{25,16},{2,11},{3,... | collective-permute-start | bytes 3080 | tf_op jit(solution)/shard_map/ppermute | solution.py:278
  21.6 0.2 inflate.1
  21.8 0.7 %collective-permute-done.13 = f32[1,256]{1,0:T(1,128)S(1)} collective-permute-done((f32[1,256]{1,0:T(1,128)S(1)}, f32[1,256]{1,0:T(1,128)S(1)}, u32[]{:S(2)}, u32[]{:S(2)}) %collective-permute-start.13) | collective-permute-done | bytes 1056 | tf_op jit(solution)/shard_map/ppermute | solution.py:278
  22.5 0.6 %collective-permute-done.12 = f32[1,256]{1,0:T(1,128)S(1)} collective-permute-done((f32[1,256]{1,0:T(1,128)S(1)}, f32[1,256]{1,0:T(1,128)S(1)}, u32[]{:S(2)}, u32[]{:S(2)}) %collective-permute-start.12) | collective-permute-done | bytes 1056 | tf_op jit(solution)/shard_map/ppermute | solution.py:278
  23.1 0.7 %broadcast_multiply_fusion = f32[256,256]{1,0:T(8,128)} fusion(f32[256,256]{1,0:T(8,128)S(1)} %get-tuple-element.29, f32[256]{0:T(256)S(1)} %bitcast.7), kind=kLoop, calls=%fused_computation | loop fusion | flops 65536 | bytes 525312 | tf_op jit(solution)/shard_map/mul | solution.py:279
  (17 shorter events, 0.4 us)
Async XLA Ops:
  1.1 10.0 %collective-permute-start.2 = (bf16[128,512]{1,0:T(8,128)(2,1)S(1)}, bf16[128,512]{1,0:T(8,128)(2,1)S(1)}, u32[]{:S(2)}, u32[]{:S(2)}) collective-permute-start(bf16[128,512]{1,0:T(8,128)(2,1)S(1)} %get-tuple-element.19.refs_0_), channel_id=1, source_target_pairs={{0,16},{24,8},{8,0},{16,24},{1,17},{25,9},{9,1},{17,25},{2,18},{26... | collective-permute-start | bytes 393224 | tf_op jit(solution)/shard_map/ppermute | solution.py:215
  5.2 4.3 %collective-permute-start = (bf16[256,128]{1,0:T(8,128)(2,1)S(1)}, bf16[256,128]{1,0:T(8,128)(2,1)S(1)}, u32[]{:S(2)}, u32[]{:S(2)}) collective-permute-start(bf16[256,128]{1,0:T(8,128)(2,1)S(1)} %get-tuple-element.18.here), channel_id=1, source_target_pairs={{0,2},{1,5},{2,0},{3,7},{4,6},{5,1},{6,4},{7,3},{8,10},{9,13},{10,... | collective-permute-start | bytes 196616 | tf_op jit(solution)/shard_map/ppermute | solution.py:224
  6.7 7.4 %collective-permute-start.3 = (bf16[128,512]{1,0:T(8,128)(2,1)S(1)}, bf16[128,512]{1,0:T(8,128)(2,1)S(1)}, u32[]{:S(2)}, u32[]{:S(2)}) collective-permute-start(bf16[128,512]{1,0:T(8,128)(2,1)S(1)} %get-tuple-element.19.refs_0_), channel_id=1, source_target_pairs={{0,8},{24,16},{8,24},{16,0},{1,9},{25,17},{9,25},{17,1},{2,10},{26... | collective-permute-start | bytes 393224 | tf_op jit(solution)/shard_map/ppermute | solution.py:216
  6.7 7.5 %collective-permute-start.4 = (bf16[128,512]{1,0:T(8,128)(2,1)S(1)}, bf16[128,512]{1,0:T(8,128)(2,1)S(1)}, u32[]{:S(2)}, u32[]{:S(2)}) collective-permute-start(bf16[128,512]{1,0:T(8,128)(2,1)S(1)} %get-tuple-element.19.refs_0_), channel_id=1, source_target_pairs={{8,17},{9,16},{16,9},{17,8},{0,1},{1,0},{24,25},{25,24},{10,19},{1... | collective-permute-start | bytes 393224 | tf_op jit(solution)/shard_map/ppermute | solution.py:218
  9.5 5.0 %collective-permute-start.1 = (bf16[2,256,128]{2,1,0:T(8,128)(2,1)S(1)}, bf16[2,256,128]{2,1,0:T(8,128)(2,1)S(1)}, u32[]{:S(2)}, u32[]{:S(2)}) collective-permute-start(bf16[2,256,128]{2,1,0:T(8,128)(2,1)S(1)} %pair.1.near), channel_id=1, source_target_pairs={{0,4},{1,3},{2,6},{3,1},{4,0},{5,7},{6,2},{7,5},{8,12},{9,11},{10,... | collective-permute-start | bytes 393224 | tf_op jit(solution)/shard_map/ppermute | solution.py:244
  11.1 5.0 %collective-permute-start.9 = (bf16[128,512]{1,0:T(8,128)(2,1)S(1)}, bf16[128,512]{1,0:T(8,128)(2,1)S(1)}, u32[]{:S(2)}, u32[]{:S(2)}) collective-permute-start(bf16[128,512]{1,0:T(8,128)(2,1)S(1)} %collective-permute-done.2.refs_1_), channel_id=1, source_target_pairs={{0,8},{8,0},{16,24},{24,16},{1,9},{9,1},{17,25},{25,17},{2,10},{10... | collective-permute-start | bytes 393224 | tf_op jit(solution)/shard_map/ppermute | solution.py:219
  14.8 1.5 %collective-permute-start.5 = (f32[328,128]{1,0:T(8,128)S(1)}, f32[328,128]{1,0:T(8,128)S(1)}, u32[]{:S(2)}, u32[]{:S(2)}) collective-permute-start(f32[328,128]{1,0:T(8,128)S(1)} %get-tuple-element.21.refs_0_), channel_id=1, source_target_pairs={{0,1},{1,0},{2,3},{3,2},{4,5},{5,4},{6,7},{7,6},{8,9},{9,8},{10,11... | collective-permute-start | bytes 503816 | tf_op jit(solution)/shard_map/ppermute | solution.py:81
  14.9 1.6 %collective-permute-start.6 = (f32[328,128]{1,0:T(8,128)S(1)}, f32[328,128]{1,0:T(8,128)S(1)}, u32[]{:S(2)}, u32[]{:S(2)}) collective-permute-start(f32[328,128]{1,0:T(8,128)S(1)} %get-tuple-element.22.refs_1_), channel_id=1, source_target_pairs={{0,1},{1,0},{2,3},{3,2},{4,5},{5,4},{6,7},{7,6},{8,9},{9,8},{10,11... | collective-permute-start | bytes 503816 | tf_op jit(solution)/shard_map/ppermute | solution.py:81
  15.4 1.4 %collective-permute-start.7 = (f32[328,128]{1,0:T(8,128)S(1)}, f32[328,128]{1,0:T(8,128)S(1)}, u32[]{:S(2)}, u32[]{:S(2)}) collective-permute-start(f32[328,128]{1,0:T(8,128)S(1)} %get-tuple-element.23.refs_2_), channel_id=1, source_target_pairs={{0,1},{1,0},{2,3},{3,2},{4,5},{5,4},{6,7},{7,6},{8,9},{9,8},{10,11... | collective-permute-start | bytes 503816 | tf_op jit(solution)/shard_map/ppermute | solution.py:81
  15.5 1.6 %collective-permute-start.8 = (f32[328,128]{1,0:T(8,128)S(1)}, f32[328,128]{1,0:T(8,128)S(1)}, u32[]{:S(2)}, u32[]{:S(2)}) collective-permute-start(f32[328,128]{1,0:T(8,128)S(1)} %get-tuple-element.24.refs_3_), channel_id=1, source_target_pairs={{0,1},{1,0},{2,3},{3,2},{4,5},{5,4},{6,7},{7,6},{8,9},{9,8},{10,11... | collective-permute-start | bytes 503816 | tf_op jit(solution)/shard_map/ppermute | solution.py:81
  16.0 1.4 %collective-permute-start.10 = (bf16[128,512]{1,0:T(8,128)(2,1)S(1)}, bf16[128,512]{1,0:T(8,128)(2,1)S(1)}, u32[]{:S(2)}, u32[]{:S(2)}) collective-permute-start(bf16[128,512]{1,0:T(8,128)(2,1)S(1)} %last.1.refs_3_), channel_id=1, source_target_pairs={{0,1},{1,0},{2,3},{3,2},{4,5},{5,4},{6,7},{7,6},{8,9},{9,8},{10,11... | collective-permute-start | bytes 393224 | tf_op jit(solution)/shard_map/ppermute | solution.py:81
  17.7 4.9 %collective-permute-start.13 = (f32[1,256]{1,0:T(1,128)S(1)}, f32[1,256]{1,0:T(1,128)S(1)}, u32[]{:S(2)}, u32[]{:S(2)}) collective-permute-start(f32[1,256]{1,0:T(1,128)S(1)} %sums.1), channel_id=1, source_target_pairs={{0,25},{1,24},{8,17},{9,16},{16,9},{17,8},{24,1},{25,0},{2,27},{3,... | collective-permute-start | bytes 3080 | tf_op jit(solution)/shard_map/ppermute | solution.py:278
  19.2 3.9 %collective-permute-start.12 = (f32[1,256]{1,0:T(1,128)S(1)}, f32[1,256]{1,0:T(1,128)S(1)}, u32[]{:S(2)}, u32[]{:S(2)}) collective-permute-start(f32[1,256]{1,0:T(1,128)S(1)} %sums.1), channel_id=1, source_target_pairs={{0,17},{1,16},{8,25},{9,24},{16,1},{17,0},{24,9},{25,8},{2,19},{3,... | collective-permute-start | bytes 3080 | tf_op jit(solution)/shard_map/ppermute | solution.py:278
  20.0 3.1 %collective-permute-start.11 = (f32[1,256]{1,0:T(1,128)S(1)}, f32[1,256]{1,0:T(1,128)S(1)}, u32[]{:S(2)}, u32[]{:S(2)}) collective-permute-start(f32[1,256]{1,0:T(1,128)S(1)} %sums.1), channel_id=1, source_target_pairs={{0,9},{1,8},{8,1},{9,0},{16,25},{17,24},{24,17},{25,16},{2,11},{3,... | collective-permute-start | bytes 3080 | tf_op jit(solution)/shard_map/ppermute | solution.py:278
